TPU v7x, 256 devices: a whole 4x4x8 slice. The times are simulated.
256 devices in a mesh: blk: 32 (over z, x_hi, core), heads: 8 (over y, x_lo).
Axes of the slice: x: 4 (x_hi: 2, x_lo: 2; x = x_hi * 2 + x_lo), y: 4, z: 8, core: 2. Of those that a mesh axis runs over, the one named last changes fastest.
Arguments:
- queries: bfloat16 [8192, 5120], P('blk', 'heads'), may hold values from -8 to 8
- key_rows: bfloat16 [8192, 5120], P('blk', 'heads'), may hold values from -8 to 8
- value_rows: bfloat16 [8192, 5120], P('blk', 'heads'), may hold values from -12 to 12
- frame_ids: int32 [8192], P('blk'), may hold values from 0 to 7, never falling along the last dimension, each value on 1 to 2048 neighbouring positions
- ctx_keys: bfloat16 [32, 256, 5120], P('blk', None, 'heads'), may hold values from -8 to 8
- ctx_values: bfloat16 [32, 256, 5120], P('blk', None, 'heads'), may hold values from -12 to 12
- owners: int32 [4], replicated, may hold values from 0 to 31, as said below
- ctx_lengths: int32 [4], replicated, may hold values from 1 to 256, 768 in all
- out_weight: bfloat16 [5120, 5120], P('heads'), may hold values from -0.078125 to 0.078125
Outputs:
- projected: bfloat16 [8192, 5120], P('blk', 'heads')
Inputs may be any that keep to these rules, and one draw needn't show every extreme that they name: `owners`: 4 distinct slot numbers. `frame_ids`: never falling along the tokens; every frame from 0 to 7 occurs.
All inputs are finite; a program needn't handle non-finite values.
Results may differ from a plain program's by a relative error of at most 0.019.
Values may be sent and summed in bfloat16 or wider, within the bound.
No kernel may reach another device: no remote copies, remote signals or barrier semaphores. Data moves between devices by JAX's collectives and lax.ppermute only.
A program may use at most 192 MiB of HBM per device.

v0:
```python
import functools
import math

import jax
import jax.numpy as jnp
from jax import lax
from jax.experimental import pallas as pl
from jax.experimental.pallas import tpu as pltpu
from jax.sharding import PartitionSpec as P

DH = 128
LOW = -1e30
MASKED = -3e30
FRAMES = 8
VMEM = 60 << 20


def scaled_exponent():
    return DH ** (-0.5) * math.log2(math.e)


def attention_kernel(chunk_count, first, last, with_ctx, head_count, rows, *refs):
    refs = list(refs)
    ctx_info = refs.pop(0) if with_ctx else None
    query_ref = refs.pop(0)
    query_marks = refs.pop(0)
    chunks = []
    for index in range(chunk_count):
        is_ctx = with_ctx and index == chunk_count - 1
        key_ref = refs.pop(0)
        value_ref = refs.pop(0)
        mark_ref = None if is_ctx else refs.pop(0)
        chunks.append((key_ref, value_ref, mark_ref))
    if not first:
        acc_in = refs.pop(0)
        stat_in = refs.pop(0)
    if last:
        keep_out = refs.pop(0)
        send_out = refs.pop(0)
    else:
        acc_out = refs.pop(0)
        stat_out = refs.pop(0)
        token_out = refs.pop(0)
    limits = refs.pop(0)
    bounds = refs.pop(0)
    if last:
        stats = refs.pop(0)
        levels = refs.pop(0)

    head = pl.program_id(0)
    lane = 128
    factor = scaled_exponent()

    @pl.when(head == 0)
    def _():
        for index, (_, _, mark_ref) in enumerate(chunks):
            if mark_ref is None:
                live = ctx_info[4 + jnp.bitwise_and(ctx_info[8], 3)]
                limits[index, 0:1, :] = jnp.full(
                    (1, 4 * rows), live.astype(jnp.float32), jnp.float32
                )
                bounds[index] = jnp.int32(1)
                continue
            frame = lax.broadcasted_iota(jnp.int32, (FRAMES, rows), 0).astype(jnp.float32)
            key_marks = mark_ref[0:1, 0:rows].astype(jnp.float32)
            below = jnp.sum((key_marks <= frame).astype(jnp.float32), axis=1, keepdims=True)
            frame = lax.broadcasted_iota(jnp.int32, (FRAMES, 4 * rows), 0).astype(jnp.float32)
            marks = query_marks[0:1, :].astype(jnp.float32)
            most = jnp.sum(jnp.where(marks == frame, below, 0.0), axis=0, keepdims=True)
            limits[index, 0:1, :] = most
            bounds[index] = jnp.max(most).astype(jnp.int32)

    def update():
        row = lax.broadcasted_iota(jnp.int32, (rows, lane), 0)
        places = [row.astype(jnp.float32)] * chunk_count
        if with_ctx:
            start = (lax.shift_right_logical(ctx_info[8], 2) + 5) * (rows // 8)
            places[-1] = jnp.bitwise_and(row + start, rows - 1).astype(jnp.float32)
        turned = [value_ref[...].T for _, value_ref, _ in chunks]
        for tile in range(4 * rows // lane):
            spot = slice(tile * lane, (tile + 1) * lane)
            query = query_ref[:, spot]
            if first:
                top = jnp.full((1, lane), LOW, jnp.float32)
                total = jnp.zeros((1, lane), jnp.float32)
                acc = jnp.zeros((DH, lane), jnp.float32)
            else:
                top, total, acc = stat_in[0:1, spot], stat_in[1:2, spot], acc_in[:, spot]
            for index, (key_ref, _, _) in enumerate(chunks):
                scores = jnp.dot(key_ref[...], query, preferred_element_type=jnp.float32)
                scores = jnp.where(places[index] < limits[index, 0:1, spot], scores, MASKED)
                top_new = jnp.maximum(top, jnp.max(scores, axis=0, keepdims=True))
                weights = jnp.exp2((scores - top_new) * factor)
                fade = jnp.exp2((top - top_new) * factor)
                total = total * fade + jnp.sum(weights, axis=0, keepdims=True)
                acc = acc * fade + jnp.dot(
                    turned[index],
                    weights.astype(jnp.bfloat16),
                    preferred_element_type=jnp.float32,
                )
                top = top_new
            if not last:
                stat_out[0:1, spot] = top
                stat_out[1:2, spot] = total
                acc_out[:, spot] = acc
                continue
            out_ref, begin = (keep_out, 0) if tile * lane < 2 * rows else (send_out, 2 * rows)
            out_spot = slice(tile * lane - begin, (tile + 1) * lane - begin)
            out_ref[pl.ds(pl.multiple_of(head * DH, DH), DH), out_spot] = (
                acc * (1.0 / total)
            ).astype(jnp.bfloat16)
            levels[0:1, spot] = top * factor + jnp.log2(total)
        if last:
            level = levels[0:1, :]
            for part in range(3):
                piece = level.astype(jnp.bfloat16).astype(jnp.float32)
                stats[pl.ds(part * head_count + head, 1), :] = piece
                level = level - piece

    if first or last:
        update()
    else:
        seen = functools.reduce(jnp.maximum, [bounds[index] for index in range(chunk_count)]) > 0

        @pl.when(seen)
        def _():
            update()

        @pl.when(jnp.logical_not(seen))
        def _():
            acc_out[...] = acc_in[...]
            stat_out[0:2, :] = stat_in[0:2, :]

    if not last:
        token_out[...] = jnp.zeros_like(token_out)
    else:

        @pl.when(head == head_count - 1)
        def _():
            feat = head_count * DH
            keep_out[feat : feat + 16, :] = stats[:, 0 : 2 * rows].astype(jnp.bfloat16)
            send_out[feat : feat + 16, :] = stats[:, 2 * rows : 4 * rows].astype(jnp.bfloat16)


def attention_call(queries, chunks, state, ctx_info, last):
    feat = queries.shape[0] - 16
    rows = queries.shape[1] // 4
    head_count = feat // DH
    first = state is None
    with_ctx = ctx_info is not None
    operands, specs = [], []
    if with_ctx:
        operands.append(ctx_info)
        specs.append(pl.BlockSpec(memory_space=pltpu.SMEM))
    operands += [queries, queries]
    specs.append(pl.BlockSpec((DH, 4 * rows), lambda h: (h, 0)))
    specs.append(pl.BlockSpec((16, 4 * rows), lambda h: (feat // 16, 0)))
    for index, chunk in enumerate(chunks):
        keys, values = chunk if isinstance(chunk, tuple) else (chunk, chunk)
        first_value = values.shape[1] // DH - head_count
        operands += [keys, values]
        specs.append(pl.BlockSpec((rows, DH), lambda h: (0, h)))
        specs.append(pl.BlockSpec((rows, DH), lambda h, base=first_value: (0, base + h)))
        if not (with_ctx and index == len(chunks) - 1):
            operands.append(keys)
            specs.append(pl.BlockSpec((16, rows), lambda h: (rows // 16, 0)))
    aliases = {}
    state_specs = [
        pl.BlockSpec((DH, 4 * rows), lambda h: (h, 0)),
        pl.BlockSpec((8, 4 * rows), lambda h: (h, 0)),
    ]
    if not first:
        if not last:
            aliases = {len(operands): 0, len(operands) + 1: 1}
        operands.extend(state)
        specs.extend(state_specs)
    if last:
        out_shape = [jax.ShapeDtypeStruct((feat + 16, 2 * rows), jnp.bfloat16)] * 2
        out_specs = [pl.BlockSpec((feat + 16, 2 * rows), lambda h: (0, 0))] * 2
    else:
        out_shape = [
            jax.ShapeDtypeStruct((feat, 4 * rows), jnp.float32),
            jax.ShapeDtypeStruct((8 * head_count, 4 * rows), jnp.float32),
            jax.ShapeDtypeStruct((8, 128), jnp.float32),
        ]
        out_specs = state_specs + [pl.BlockSpec((8, 128), lambda h: (0, 0))]
    scratch = [
        pltpu.VMEM((len(chunks), 8, 4 * rows), jnp.float32),
        pltpu.SMEM((len(chunks),), jnp.int32),
    ]
    if last:
        scratch += [
            pltpu.VMEM((16, 4 * rows), jnp.float32),
            pltpu.VMEM((8, 4 * rows), jnp.float32),
        ]
    return pl.pallas_call(
        functools.partial(
            attention_kernel, len(chunks), first, last, with_ctx, head_count, rows
        ),
        grid=(head_count,),
        in_specs=specs,
        out_specs=out_specs,
        out_shape=out_shape,
        scratch_shapes=scratch,
        input_output_aliases=aliases,
        cost_estimate=pl.CostEstimate(
            flops=len(chunks) * 6 * 10**9, bytes_accessed=8 << 20, transcendentals=0
        ),
        compiler_params=pltpu.CompilerParams(vmem_limit_bytes=VMEM),
        name="attend",
    )(*operands)


def merge_kernel(head_count, turned, a_ref, b_ref, out_ref, *rest):
    feat = head_count * DH
    rows = a_ref.shape[1]
    a_stats = a_ref[feat : feat + 16, :].astype(jnp.float32)
    b_stats = b_ref[feat : feat + 16, :].astype(jnp.float32)
    pieces = [[], [], []]
    for head in range(head_count):
        levels = [
            s[head : head + 1]
            + s[head_count + head : head_count + head + 1]
            + s[2 * head_count + head : 2 * head_count + head + 1]
            for s in (a_stats, b_stats)
        ]
        top = jnp.maximum(levels[0], levels[1])
        a_weight = jnp.exp2(levels[0] - top)
        b_weight = jnp.exp2(levels[1] - top)
        total = a_weight + b_weight
        inverse = 1.0 / total
        span = slice(head * DH, (head + 1) * DH)
        mixed = a_ref[span, :].astype(jnp.float32) * (a_weight * inverse) + b_ref[span, :].astype(
            jnp.float32
        ) * (b_weight * inverse)
        if turned:
            out_ref[:, span] = mixed.T.astype(jnp.bfloat16)
        else:
            half = rows // 2
            out_ref[span, :] = mixed[:, :half].astype(jnp.bfloat16)
            rest[0][span, :] = mixed[:, half:].astype(jnp.bfloat16)
            level = top + jnp.log2(total)
            for part in range(3):
                piece = level.astype(jnp.bfloat16).astype(jnp.float32)
                pieces[part].append(piece)
                level = level - piece
    if not turned:
        stats = jnp.concatenate(
            pieces[0] + pieces[1] + pieces[2] + [jnp.zeros((1, rows), jnp.float32)], axis=0
        ).astype(jnp.bfloat16)
        out_ref[feat : feat + 16, :] = stats[:, :half]
        rest[0][feat : feat + 16, :] = stats[:, half:]


def merge_call(a, b, turned):
    feat = a.shape[0] - 16
    rows = a.shape[1]
    if turned:
        out_shape = jax.ShapeDtypeStruct((rows, feat), jnp.bfloat16)
        out_specs = pl.BlockSpec(memory_space=pltpu.VMEM)
    else:
        out_shape = [jax.ShapeDtypeStruct((feat + 16, rows // 2), jnp.bfloat16)] * 2
        out_specs = [pl.BlockSpec(memory_space=pltpu.VMEM)] * 2
    return pl.pallas_call(
        functools.partial(merge_kernel, feat // DH, turned),
        in_specs=[pl.BlockSpec(memory_space=pltpu.VMEM)] * 2,
        out_specs=out_specs,
        out_shape=out_shape,
        compiler_params=pltpu.CompilerParams(vmem_limit_bytes=VMEM),
        cost_estimate=pl.CostEstimate(flops=0, bytes_accessed=6 << 20, transcendentals=0),
        name="merge",
    )(a, b)


def columns_kernel(info, in_ref, out_ref):
    out_ref[0] = in_ref[...]


def column_blocks(weight, info, width, ring):
    rows = weight.shape[0]

    def place(j, info):
        target = jnp.bitwise_and(lax.shift_right_logical(info[9], 1) + j, ring - 1)
        half = jnp.bitwise_xor(jnp.bitwise_and(info[8], 1), lax.shift_right_logical(j, 2))
        return (0, 2 * target + half)

    return pl.pallas_call(
        columns_kernel,
        grid_spec=pltpu.PrefetchScalarGridSpec(
            num_scalar_prefetch=1,
            grid=(ring + 1,),
            in_specs=[pl.BlockSpec((rows, width), place)],
            out_specs=pl.BlockSpec((1, rows, width), lambda j, info: (j, 0, 0)),
        ),
        out_shape=jax.ShapeDtypeStruct((ring + 1, rows, width), weight.dtype),
        compiler_params=pltpu.CompilerParams(vmem_limit_bytes=VMEM),
        cost_estimate=pl.CostEstimate(
            flops=0, bytes_accessed=4 * (ring + 1) * rows * width, transcendentals=0
        ),
        name="columns",
    )(info, weight)


def offer_kernel(info, in_ref, *out_refs):
    for mask, out_ref in enumerate(out_refs):
        owner = info[jnp.bitwise_xor(jnp.bitwise_and(info[8], 3), mask)]
        out_ref[...] = in_ref[lax.shift_right_logical(owner, 2)]


def offer_pieces(pieces, info):
    return pl.pallas_call(
        offer_kernel,
        in_specs=[
            pl.BlockSpec(memory_space=pltpu.SMEM),
            pl.BlockSpec(memory_space=pltpu.VMEM),
        ],
        out_specs=[pl.BlockSpec(memory_space=pltpu.VMEM)] * 4,
        out_shape=[jax.ShapeDtypeStruct(pieces.shape[1:], pieces.dtype)] * 4,
        compiler_params=pltpu.CompilerParams(vmem_limit_bytes=VMEM),
        name="offer",
    )(info, pieces)


def choose_kernel(info, *refs):
    kind = jnp.bitwise_and(info[8], 3)
    source = jnp.bitwise_xor(jnp.bitwise_and(info[kind], 3), kind)
    out_ref = refs[-1]
    for mask, in_ref in enumerate(refs[:-1]):

        @pl.when(source == mask)
        def _(in_ref=in_ref):
            out_ref[...] = in_ref[...]


def choose_piece(offers, info):
    return pl.pallas_call(
        choose_kernel,
        in_specs=[pl.BlockSpec(memory_space=pltpu.SMEM)]
        + [pl.BlockSpec(memory_space=pltpu.VMEM)] * len(offers),
        out_specs=pl.BlockSpec(memory_space=pltpu.VMEM),
        out_shape=jax.ShapeDtypeStruct(offers[0].shape, offers[0].dtype),
        compiler_params=pltpu.CompilerParams(vmem_limit_bytes=VMEM),
        name="choose",
    )(info, *offers)


def shards(
    queries, key_rows, value_rows, frame_ids, ctx_keys, ctx_values, owners, ctx_lengths, out_weight
):
    rows, feat = queries.shape
    blk_count = lax.axis_size("blk")
    head_devices = lax.axis_size("heads")
    plane, pair = 4, 2
    depth, ring_y = blk_count // plane, head_devices // pair
    me = lax.axis_index("blk")
    head_me = lax.axis_index("heads")
    info = jnp.concatenate([owners, ctx_lengths, me[None], head_me[None]]).astype(jnp.int32)
    columns = [[c + plane * z for z in range(depth)] for c in range(plane)]

    def shift(item, distance):
        steps = [(i, (i + plane * distance) % blk_count) for i in range(blk_count)]
        return lax.ppermute(item, "blk", steps)

    def swap(item, mask):
        return lax.ppermute(item, "blk", [(i, i ^ mask) for i in range(blk_count)])

    def shift_y(item, step):
        steps = [(i, (i + pair * step) % head_devices) for i in range(head_devices)]
        return lax.ppermute(item, "heads", steps)

    marks = jnp.pad(frame_ids.astype(jnp.bfloat16)[None], ((0, 15), (0, 2 * feat - rows)))
    own = jnp.concatenate([jnp.concatenate([key_rows, value_rows], axis=1), marks], axis=0)
    query_own = jnp.concatenate([queries.T, marks[:, :rows]], axis=0)
    part = ctx_keys.shape[1] // depth
    slot = jnp.concatenate([ctx_keys[0], ctx_values[0]], axis=1).reshape(depth, part, 2 * feat)

    ahead, behind = shift(own, 1), shift(own, -1)
    query_x, query_core, query_both = swap(query_own, 2), swap(query_own, 1), swap(query_own, 3)
    pieces = lax.all_to_all(slot, "blk", 0, 0, axis_index_groups=columns)
    slabs = column_blocks(out_weight, info, feat, ring_y)
    query_plane = jnp.concatenate([query_own, query_x, query_core, query_both], axis=1)
    offers = list(offer_pieces(pieces, info))

    *state, _ = attention_call(query_plane, [own, ahead, behind], None, None, False)
    ahead, behind = shift(ahead, 1), shift(behind, -1)
    offers = offers[:1] + [swap(offers[mask], mask) for mask in range(1, plane)]
    piece = choose_piece(offers, info)

    *state, _ = attention_call(query_plane, [ahead, behind], state, None, False)
    ahead, behind = shift(ahead, 1), shift(behind, -1)
    ctx = {0: piece}
    for distance in (1, -1, 2, -2):
        ctx[distance] = shift(piece, distance)
    slab_near = shift_y(slabs[1], 1)
    slab_back = shift_y(slabs[ring_y - 1], ring_y - 1)
    ahead, behind, slab_near, slab_back = lax.optimization_barrier(
        (ahead, behind, slab_near, slab_back)
    )

    far = ahead[:, :feat], behind[:rows, feat:]
    *state, _ = attention_call(query_plane, [ahead, behind], state, None, False)
    far = shift(far[0], 1), shift(far[1], -1)
    ctx[3] = shift(ctx[2], 1)
    ctx[4] = shift(ctx[2], 2)
    ctx[-3] = shift(ctx[-2], -1)
    slab_far = shift_y(slabs[2], 2)
    ctx = jnp.concatenate([ctx[distance] for distance in (3, 2, 1, 0, -1, -2, -3, 4)], axis=0)
    own_slabs = [slabs[0], slab_near, slab_far, slab_back]
    core_slabs = [slabs[ring_y], swap(slab_near, 1), None, swap(slab_back, 1)]
    ctx, slab_far, *_ = lax.optimization_barrier((ctx, slab_far, core_slabs[1], core_slabs[3]))
    core_slabs[2] = swap(slab_far, 1)
    keep, send = attention_call(query_plane, [far, ctx], state, info, True)
    keep, send, core_slabs[2] = lax.optimization_barrier((keep, send, core_slabs[2]))
    received = swap(send, 1)
    own, other = merge_call(keep, received, False)
    received = swap(other, 2)
    attended = merge_call(own, received, True)

    def dots(block, step):
        return [
            jnp.dot(block, item[step], preferred_element_type=jnp.float32)
            for item in (own_slabs, core_slabs)
        ]

    total = dots(attended, 0)
    block_near, block_back = shift_y(attended, 1), shift_y(attended, ring_y - 1)
    block_far = shift_y(attended, 2)
    added = [dots(block_near, 1), dots(block_back, ring_y - 1)]
    added.append(dots(block_far, 2))
    total = [sum(items) for items in zip(total, *added)]
    same = jnp.bitwise_and(jnp.bitwise_xor(me, head_me), 1) == 0
    mine = jnp.where(same, total[0], total[1])
    other = jnp.where(same, total[1], total[0])
    received = lax.ppermute(
        other.astype(jnp.bfloat16), "heads", [(i, i ^ 1) for i in range(head_devices)]
    )
    return (mine + received.astype(jnp.float32)).astype(jnp.bfloat16)


def solution(mesh):
    return jax.shard_map(
        shards,
        mesh=mesh,
        in_specs=(
            P("blk", "heads"),
            P("blk", "heads"),
            P("blk", "heads"),
            P("blk"),
            P("blk", None, "heads"),
            P("blk", None, "heads"),
            P(),
            P(),
            P("heads", None),
        ),
        out_specs=P("blk", "heads"),
        check_vma=False,
    )
```

profile of v0, /device:TPU:2, one launch (start us, length us, event | category | flops | bytes accessed | tf_op | source)
XLA Modules:
  0.0 179.1 jit_solution(13395633997646554757)
XLA Ops:
  0.0 2.1 %pad_maximum_fusion.2 = bf16[8,32,1280]{2,1,0:T(8,128)(2,1)} fusion(bf16[8,32,640]{2,1,0:T(8,128)(2,1)} %bitcast.35, bf16[8,32,640]{2,1,0:T(8,128)(2,1)} %bitcast.36), kind=kLoop, calls=%fused_computation.13 | loop fusion | flops 1310720 | bytes 1310720 | tf_op jit(solution)/shard_map/concatenate | solution.py:375
  2.1 8.5 %all-to-all-start = ((bf16[8,32,1280]{2,1,0:T(8,128)(2,1)}), bf16[8,32,1280]{2,1,0:T(8,128)(2,1)S(1)}, u32[]{:S(2)}, u32[]{:S(2)}) async-start(bf16[8,32,1280]{2,1,0:T(8,128)(2,1)} %pad_maximum_fusion.2), calls=%async_computation | async-start | bytes 1310720 | tf_op jit(solution)/shard_map/all_to_all | solution.py:379
  10.6 0.9 pad_maximum_fusion.1.refs_2_.refs_3_.refs_4_
  11.5 2.0 %collective-permute-start.3 = (bf16[272,1280]{1,0:T(8,128)(2,1)}, bf16[272,1280]{1,0:T(8,128)(2,1)}, u32[]{:S(2)}, u32[]{:S(2)}) collective-permute-start(bf16[272,1280]{1,0:T(8,128)(2,1)} %pad_maximum_fusion.1.refs_2_.refs_3_.refs_4_), channel_id=1, source_target_pairs={{0,32},{8,40},{16,48},{24,56},{32,64},{40,72},{48,80},{56,88},{64,... | collective-permute-start | bytes 2088968 | tf_op jit(solution)/shard_map/ppermute | solution.py:362
  13.5 1.2 collective-permute-start.6
  14.8 0.2 copy.14
  14.9 0.7 pad_maximum_fusion.3
  15.7 2.1 %collective-permute-start = (bf16[656,256]{1,0:T(8,128)(2,1)}, bf16[656,256]{1,0:T(8,128)(2,1)}, u32[]{:S(2)}, u32[]{:S(2)}) collective-permute-start(bf16[656,256]{1,0:T(8,128)(2,1)} %pad_maximum_fusion.3), channel_id=1, source_target_pairs={{0,16},{8,24},{16,0},{24,8},{32,48},{40,56},{48,32},{56,40},{64,80... | collective-permute-start | bytes 1007624 | tf_op jit(solution)/shard_map/ppermute | solution.py:365
  17.8 1.5 collective-permute-start.2
  19.3 0.6 pad_add_fusion.info.refs_0_
  20.0 6.5 %columns.1 = bf16[5,640,640]{2,1,0:T(8,128)(2,1)} custom-call(s32[10]{0:T(128)} %pad_add_fusion.info.refs_0_, bf16[640,5120]{1,0:T(8,128)(2,1)} %in_ref.1), custom_call_target="tpu_custom_call" | custom-call | bytes 8192000 | tf_op jit(solution)/shard_map/columns/pallas_call | solution.py:287
  26.5 1.8 %slice_bitcast_fusion.4 = (bf16[640,640]{1,0:T(8,128)(2,1)S(1)}, bf16[640,640]{1,0:T(8,128)(2,1)S(1)}, bf16[640,640]{1,0:T(8,128)(2,1)S(1)}) fusion(bf16[5,640,640]{2,1,0:T(8,128)(2,1)} %columns.1), kind=kLoop, calls=%fused_computation.9 | loop fusion | bytes 4915200 | tf_op jit(solution)/shard_map/squeeze | solution.py:406
  28.4 2.4 %all-to-all-done.in_ref = bf16[8,32,1280]{2,1,0:T(8,128)(2,1)S(1)} async-done(((bf16[8,32,1280]{2,1,0:T(8,128)(2,1)}), bf16[8,32,1280]{2,1,0:T(8,128)(2,1)S(1)}, u32[]{:S(2)}, u32[]{:S(2)}) %all-to-all-start) | async-done | bytes 655392 | tf_op jit(solution)/shard_map/all_to_all | solution.py:379
  30.8 0.8 copy-done.1
  31.6 1.8 %offer.1 = (bf16[32,1280]{1,0:T(8,128)(2,1)}, bf16[32,1280]{1,0:T(8,128)(2,1)}, bf16[32,1280]{1,0:T(8,128)(2,1)}, bf16[32,1280]{1,0:T(8,128)(2,1)}) custom-call(s32[10]{0:T(128)} %pad_add_fusion.info.refs_0_, bf16[8,32,1280]{2,1,0:T(8,128)(2,1)} %copy-done.1), custom_call_target="tpu_custom_call" | custom-call | tf_op jit(solution)/shard_map/offer/pallas_call | solution.py:311
  33.5 2.2 %collective-permute-start.14 = (bf16[32,1280]{1,0:T(8,128)(2,1)}, bf16[32,1280]{1,0:T(8,128)(2,1)S(1)}, u32[]{:S(2)}, u32[]{:S(2)}) collective-permute-start(bf16[32,1280]{1,0:T(8,128)(2,1)} %get-tuple-element.32), channel_id=1, source_target_pairs={{0,16},{8,24},{16,0},{24,8},{32,48},{40,56},{48,32},{56,40},{64,80... | collective-permute-start | bytes 245768 | tf_op jit(solution)/shard_map/ppermute | solution.py:365
  35.7 1.2 collective-permute-start.15
  36.9 2.5 %pad_maximum_fusion.refs_0_.refs_1_.refs_2_ = bf16[656,1024]{1,0:T(8,128)(2,1)} fusion(bf16[656,256]{1,0:T(8,128)(2,1)} %collective-permute-done.2, bf16[656,256]{1,0:T(8,128)(2,1)} %collective-permute-done.1, bf16[656,256]{1,0:T(8,128)(2,1)} %collective-permute-done, bf16[16,256]{1,0:T(8,128)(2,1)S(1)} %pad_slice_fusion, bf16[640,256]{1,0:T(8,128)(2,1)S(1)} %bitcast.34), kind=kLoop, calls=%fused_computation | loop fusion | flops 6717440 | bytes 2686976 | tf_op jit(solution)/shard_map/concatenate | solution.py:381
  39.4 3.8 %collective-permute-done.3.refs_5_.refs_6_.refs_7_ = bf16[272,1280]{1,0:T(8,128)(2,1)} collective-permute-done((bf16[272,1280]{1,0:T(8,128)(2,1)}, bf16[272,1280]{1,0:T(8,128)(2,1)}, u32[]{:S(2)}, u32[]{:S(2)}) %collective-permute-start.3) | collective-permute-done | bytes 696352 | tf_op jit(solution)/shard_map/ppermute | solution.py:362
  43.2 3.0 %collective-permute-start.10 = (bf16[640,640]{1,0:T(8,128)(2,1)S(1)}, bf16[640,640]{1,0:T(8,128)(2,1)S(1)}, u32[]{:S(2)}, u32[]{:S(2)}) collective-permute-start(bf16[640,640]{1,0:T(8,128)(2,1)S(1)} %get-tuple-element.52), channel_id=1, source_target_pairs={{0,6},{1,7},{2,0},{3,1},{4,2},{5,3},{6,4},{7,5},{8,14},{9,15},{10,... | collective-permute-start | bytes 2457608 | tf_op jit(solution)/shard_map/ppermute | solution.py:369
  46.3 3.2 %collective-permute-start.7 = (bf16[272,1280]{1,0:T(8,128)(2,1)}, bf16[272,1280]{1,0:T(8,128)(2,1)}, u32[]{:S(2)}, u32[]{:S(2)}) collective-permute-start(bf16[272,1280]{1,0:T(8,128)(2,1)} %collective-permute-done.6.refs_8_.refs_9_.refs_10_), channel_id=1, source_target_pairs={{0,224},{8,232},{16,240},{24,248},{32,0},{40,8},{48,16},{56,24},{6... | collective-permute-start | bytes 2088968 | tf_op jit(solution)/shard_map/ppermute | solution.py:362
  49.6 0.6 copy-done.15
  50.2 1.7 choose.1
  51.9 9.5 %attend.4 = (f32[640,1024]{1,0:T(8,128)}, f32[40,1024]{1,0:T(8,128)}, f32[8,128]{1,0:T(8,128)}) custom-call(bf16[656,1024]{1,0:T(8,128)(2,1)} %pad_maximum_fusion.refs_0_.refs_1_.refs_2_, bf16[656,1024]{1,0:T(8,128)(2,1)} %pad_maximum_fusion.refs_0_.refs_1_.refs_2_, bf16[272,1280]{1,0:T(8,128)(2,1)} %pad_maximum_fusion.1.refs_2_.refs_3_.refs_4_, ...), custom_call_target="tpu_custom_call" | custom-call | flops 17999998976 | bytes 8388608 | tf_op jit(solution)/shard_map/attend/pallas_call | solution.py:196
  61.4 5.1 %collective-permute-done.16 = bf16[32,1280]{1,0:T(8,128)(2,1)S(1)} collective-permute-done((bf16[32,1280]{1,0:T(8,128)(2,1)}, bf16[32,1280]{1,0:T(8,128)(2,1)S(1)}, u32[]{:S(2)}, u32[]{:S(2)}) %collective-permute-start.16) | collective-permute-done | bytes 81952 | tf_op jit(solution)/shard_map/ppermute | solution.py:362
  66.5 2.7 %collective-permute-start.18 = (bf16[32,1280]{1,0:T(8,128)(2,1)S(1)}, bf16[32,1280]{1,0:T(8,128)(2,1)S(1)}, u32[]{:S(2)}, u32[]{:S(2)}) collective-permute-start(bf16[32,1280]{1,0:T(8,128)(2,1)S(1)} %copy-done.8), channel_id=1, source_target_pairs={{0,32},{8,40},{16,48},{24,56},{32,64},{40,72},{48,80},{56,88},{64,... | collective-permute-start | bytes 245768 | tf_op jit(solution)/shard_map/ppermute | solution.py:362
  69.1 0.8 collective-permute-start.20
  70.0 1.2 collective-permute-start.17
  71.2 5.6 %attend.5 = (f32[640,1024]{1,0:T(8,128)}, f32[40,1024]{1,0:T(8,128)}, f32[8,128]{1,0:T(8,128)}) custom-call(bf16[656,1024]{1,0:T(8,128)(2,1)} %pad_maximum_fusion.refs_0_.refs_1_.refs_2_, bf16[656,1024]{1,0:T(8,128)(2,1)} %pad_maximum_fusion.refs_0_.refs_1_.refs_2_, ...), custom_call_target="tpu_custom_call", output_to_operand_aliasing={{0}: (8, {}), {1}: (9, {})} | custom-call | flops 12000000000 | bytes 8388608 | tf_op jit(solution)/shard_map/attend/pallas_call | solution.py:196
  76.8 4.7 %collective-permute-start.19 = (bf16[32,1280]{1,0:T(8,128)(2,1)S(1)}, bf16[32,1280]{1,0:T(8,128)(2,1)S(1)}, u32[]{:S(2)}, u32[]{:S(2)}) collective-permute-start(bf16[32,1280]{1,0:T(8,128)(2,1)S(1)} %copy-done.8), channel_id=1, source_target_pairs={{0,224},{8,232},{16,240},{24,248},{32,0},{40,8},{48,16},{56,24},{6... | collective-permute-start | bytes 245768 | tf_op jit(solution)/shard_map/ppermute | solution.py:362
  81.5 0.5 collective-permute-start.21
  82.1 1.6 collective-permute-start.5
  83.8 3.4 %collective-permute-start.8 = (bf16[272,1280]{1,0:T(8,128)(2,1)}, bf16[272,1280]{1,0:T(8,128)(2,1)S(1)}, u32[]{:S(2)}, u32[]{:S(2)}) collective-permute-start(bf16[272,1280]{1,0:T(8,128)(2,1)} %collective-permute-done.7.refs_5_.refs_6_.refs_7_), channel_id=1, source_target_pairs={{0,224},{8,232},{16,240},{24,248},{32,0},{40,8},{48,16},{56,24},{6... | collective-permute-start | bytes 2088968 | tf_op jit(solution)/shard_map/ppermute | solution.py:362
  87.2 0.6 collective-permute-start.22
  87.8 13.0 %collective-permute-done.22 = bf16[32,1280]{1,0:T(8,128)(2,1)S(1)} collective-permute-done((bf16[32,1280]{1,0:T(8,128)(2,1)S(1)}, bf16[32,1280]{1,0:T(8,128)(2,1)S(1)}, u32[]{:S(2)}, u32[]{:S(2)}) %collective-permute-start.22) | collective-permute-done | bytes 81952 | tf_op jit(solution)/shard_map/ppermute | solution.py:362
  100.8 0.3 collective-permute-start.23
  101.4 0.6 copy-done.16
  102.0 4.2 %collective-permute-start.11 = (bf16[272,640]{1,0:T(8,128)(2,1)S(1)}, bf16[272,640]{1,0:T(8,128)(2,1)}, u32[]{:S(2)}, u32[]{:S(2)}) collective-permute-start(bf16[272,640]{1,0:T(8,128)(2,1)S(1)} %slice.27), channel_id=1, source_target_pairs={{0,32},{8,40},{16,48},{24,56},{32,64},{40,72},{48,80},{56,88},{64,... | collective-permute-start | bytes 1044488 | tf_op jit(solution)/shard_map/ppermute | solution.py:362
  106.3 5.6 %attend.6 = (f32[640,1024]{1,0:T(8,128)}, f32[40,1024]{1,0:T(8,128)}, f32[8,128]{1,0:T(8,128)}) custom-call(bf16[656,1024]{1,0:T(8,128)(2,1)} %pad_maximum_fusion.refs_0_.refs_1_.refs_2_, bf16[656,1024]{1,0:T(8,128)(2,1)} %pad_maximum_fusion.refs_0_.refs_1_.refs_2_, bf16[272,1280]{1,0:T(8,128)(2,1)} %copy-done.11, ...), custom_call_target="tpu_custom_call", output_to_operand_aliasing={{0}: (8, {}), {1}: (9, {})} | custom-call | flops 12000000000 | bytes 8388608 | tf_op jit(solution)/shard_map/attend/pallas_call | solution.py:196
  111.9 4.8 %collective-permute-done.23 = bf16[640,640]{1,0:T(8,128)(2,1)} collective-permute-done((bf16[640,640]{1,0:T(8,128)(2,1)S(1)}, bf16[640,640]{1,0:T(8,128)(2,1)}, u32[]{:S(2)}, u32[]{:S(2)}) %collective-permute-start.23) | collective-permute-done | bytes 819232 | tf_op jit(solution)/shard_map/ppermute | solution.py:369
  116.8 8.4 %attend.7 = (bf16[656,512]{1,0:T(8,128)(2,1)}, bf16[656,512]{1,0:T(8,128)(2,1)}) custom-call(s32[10]{0:T(128)} %pad_add_fusion.info.refs_0_, bf16[656,1024]{1,0:T(8,128)(2,1)} %pad_maximum_fusion.refs_0_.refs_1_.refs_2_, bf16[656,1024]{1,0:T(8,128)(2,1)} %pad_maximum_fusion.refs_0_.refs_1_.refs_2_, bf16[272,640]{1,0:T(8,128)(2,1)} %collective-permute-done.11.refs_3_.refs_5_, ...), custom_call_target="tpu_custom_call" | custom-call | flops 12000000000 | bytes 8388608 | tf_op jit(solution)/shard_map/attend/pallas_call | solution.py:196
  125.1 0.6 collective-permute-start.27
  125.7 2.1 %collective-permute-done.27.b_ref = bf16[656,512]{1,0:T(8,128)(2,1)} collective-permute-done((bf16[656,512]{1,0:T(8,128)(2,1)}, bf16[656,512]{1,0:T(8,128)(2,1)}, u32[]{:S(2)}, u32[]{:S(2)}) %collective-permute-start.27) | collective-permute-done | bytes 671776 | tf_op jit(solution)/shard_map/ppermute | solution.py:365
  127.8 2.5 %merge.2 = (bf16[656,256]{1,0:T(8,128)(2,1)}, bf16[656,256]{1,0:T(8,128)(2,1)}) custom-call(bf16[656,512]{1,0:T(8,128)(2,1)} %get-tuple-element.46.a_ref, bf16[656,512]{1,0:T(8,128)(2,1)} %collective-permute-done.27.b_ref), custom_call_target="tpu_custom_call" | custom-call | bytes 6291456 | tf_op jit(solution)/shard_map/merge/pallas_call | solution.py:264
  130.2 2.1 %collective-permute-start.28 = (bf16[656,256]{1,0:T(8,128)(2,1)}, bf16[656,256]{1,0:T(8,128)(2,1)S(1)}, u32[]{:S(2)}, u32[]{:S(2)}) collective-permute-start(bf16[656,256]{1,0:T(8,128)(2,1)} %get-tuple-element.49), channel_id=1, source_target_pairs={{0,16},{8,24},{16,0},{24,8},{32,48},{40,56},{48,32},{56,40},{64,80... | collective-permute-start | bytes 1007624 | tf_op jit(solution)/shard_map/ppermute | solution.py:365
  132.4 9.7 %collective-permute-done.28.b_ref = bf16[656,256]{1,0:T(8,128)(2,1)S(1)} collective-permute-done((bf16[656,256]{1,0:T(8,128)(2,1)}, bf16[656,256]{1,0:T(8,128)(2,1)S(1)}, u32[]{:S(2)}, u32[]{:S(2)}) %collective-permute-start.28) | collective-permute-done | bytes 335904 | tf_op jit(solution)/shard_map/ppermute | solution.py:365
  142.1 0.7 copy-done.6
  142.9 2.0 %merge.3 = bf16[256,640]{1,0:T(8,128)(2,1)} custom-call(bf16[656,256]{1,0:T(8,128)(2,1)} %get-tuple-element.48.a_ref, bf16[656,256]{1,0:T(8,128)(2,1)} %copy-done.6), custom_call_target="tpu_custom_call" | custom-call | bytes 6291456 | tf_op jit(solution)/shard_map/merge/pallas_call | solution.py:264
  144.9 1.0 collective-permute-start.29
  145.9 2.2 %collective-permute-start.30 = (bf16[256,640]{1,0:T(8,128)(2,1)}, bf16[256,640]{1,0:T(8,128)(2,1)S(1)}, u32[]{:S(2)}, u32[]{:S(2)}) collective-permute-start(bf16[256,640]{1,0:T(8,128)(2,1)} %merge.3), channel_id=1, source_target_pairs={{0,6},{1,7},{2,0},{3,1},{4,2},{5,3},{6,4},{7,5},{8,14},{9,15},{10,... | collective-permute-start | bytes 983048 | tf_op jit(solution)/shard_map/ppermute | solution.py:369
  148.1 0.3 collective-permute-start.31
  148.5 14.1 %collective-permute-done.29 = bf16[256,640]{1,0:T(8,128)(2,1)S(1)} collective-permute-done((bf16[256,640]{1,0:T(8,128)(2,1)}, bf16[256,640]{1,0:T(8,128)(2,1)S(1)}, u32[]{:S(2)}, u32[]{:S(2)}) %collective-permute-start.29) | collective-permute-done | bytes 327712 | tf_op jit(solution)/shard_map/ppermute | solution.py:369
  162.5 1.6 fusion.4
  164.1 0.5 fusion.5
  164.6 1.6 fusion.6
  166.2 1.6 fusion.1
  167.9 0.5 fusion.7
  168.3 0.5 fusion.8
  168.8 0.2 copy-done.5
  169.0 0.5 fusion.9
  169.5 1.6 select_convert_fusion
  171.1 0.6 collective-permute-start.32
  171.7 6.5 %collective-permute-done.32 = bf16[256,640]{1,0:T(8,128)(2,1)S(1)} collective-permute-done((bf16[256,640]{1,0:T(8,128)(2,1)S(1)}, bf16[256,640]{1,0:T(8,128)(2,1)S(1)}, u32[]{:S(2)}, u32[]{:S(2)}) %collective-permute-start.32) | collective-permute-done | bytes 327712 | tf_op jit(solution)/shard_map/ppermute | solution.py:434
  178.2 0.8 add_convert_fusion
  (83 shorter events, 0.8 us)
Async XLA Ops:
  0.0 10.6 %copy-start.19 = (s32[256]{0:T(256)S(1)}, s32[256]{0:T(256)}, u32[]{:S(2)}) copy-start(s32[256]{0:T(256)} %param.12) | copy-start | bytes 3076
  0.0 10.6 %copy-start.10 = (bf16[256,640]{1,0:T(8,128)(2,1)S(1)}, bf16[256,640]{1,0:T(8,128)(2,1)}, u32[]{:S(2)}) copy-start(bf16[256,640]{1,0:T(8,128)(2,1)} %param.10) | copy-start | bytes 983044
  0.0 10.6 %copy-start.9 = (bf16[256,640]{1,0:T(8,128)(2,1)S(1)}, bf16[256,640]{1,0:T(8,128)(2,1)}, u32[]{:S(2)}) copy-start(bf16[256,640]{1,0:T(8,128)(2,1)} %param.11) | copy-start | bytes 983044
  0.0 14.8 %copy-start.7 = (bf16[256,640]{1,0:T(8,128)(2,1)S(1)}, bf16[256,640]{1,0:T(8,128)(2,1)}, u32[]{:S(2)}) copy-start(bf16[256,640]{1,0:T(8,128)(2,1)} %param.9) | copy-start | bytes 983044
  0.0 19.3 %copy-start.17 = (s32[4]{0:T(128)S(1)}, s32[4]{0:T(128)}, u32[]{:S(2)}) copy-start(s32[4]{0:T(128)} %param.16) | copy-start | bytes 52
  0.0 19.3 %copy-start.18 = (s32[4]{0:T(128)S(1)}, s32[4]{0:T(128)}, u32[]{:S(2)}) copy-start(s32[4]{0:T(128)} %param.15) | copy-start | bytes 52
  2.1 28.7 %all-to-all-start = ((bf16[8,32,1280]{2,1,0:T(8,128)(2,1)}), bf16[8,32,1280]{2,1,0:T(8,128)(2,1)S(1)}, u32[]{:S(2)}, u32[]{:S(2)}) async-start(bf16[8,32,1280]{2,1,0:T(8,128)(2,1)} %pad_maximum_fusion.2), calls=%async_computation | async-start | bytes 1310720 | tf_op jit(solution)/shard_map/all_to_all | solution.py:379
  11.5 31.7 %collective-permute-start.3 = (bf16[272,1280]{1,0:T(8,128)(2,1)}, bf16[272,1280]{1,0:T(8,128)(2,1)}, u32[]{:S(2)}, u32[]{:S(2)}) collective-permute-start(bf16[272,1280]{1,0:T(8,128)(2,1)} %pad_maximum_fusion.1.refs_2_.refs_3_.refs_4_), channel_id=1, source_target_pairs={{0,32},{8,40},{16,48},{24,56},{32,64},{40,72},{48,80},{56,88},{64,... | collective-permute-start | bytes 2088968 | tf_op jit(solution)/shard_map/ppermute | solution.py:362
  13.5 32.7 %collective-permute-start.6 = (bf16[272,1280]{1,0:T(8,128)(2,1)}, bf16[272,1280]{1,0:T(8,128)(2,1)}, u32[]{:S(2)}, u32[]{:S(2)}) collective-permute-start(bf16[272,1280]{1,0:T(8,128)(2,1)} %pad_maximum_fusion.1.refs_2_.refs_3_.refs_4_), channel_id=1, source_target_pairs={{0,224},{8,232},{16,240},{24,248},{32,0},{40,8},{48,16},{56,24},{6... | collective-permute-start | bytes 2088968 | tf_op jit(solution)/shard_map/ppermute | solution.py:362
  15.7 17.8 %collective-permute-start = (bf16[656,256]{1,0:T(8,128)(2,1)}, bf16[656,256]{1,0:T(8,128)(2,1)}, u32[]{:S(2)}, u32[]{:S(2)}) collective-permute-start(bf16[656,256]{1,0:T(8,128)(2,1)} %pad_maximum_fusion.3), channel_id=1, source_target_pairs={{0,16},{8,24},{16,0},{24,8},{32,48},{40,56},{48,32},{56,40},{64,80... | collective-permute-start | bytes 1007624 | tf_op jit(solution)/shard_map/ppermute | solution.py:365
  17.8 15.7 %collective-permute-start.1 = (bf16[656,256]{1,0:T(8,128)(2,1)}, bf16[656,256]{1,0:T(8,128)(2,1)}, u32[]{:S(2)}, u32[]{:S(2)}) collective-permute-start(bf16[656,256]{1,0:T(8,128)(2,1)} %pad_maximum_fusion.3), channel_id=1, source_target_pairs={{0,8},{8,0},{16,24},{24,16},{32,40},{40,32},{48,56},{56,48},{64,72... | collective-permute-start | bytes 1007624 | tf_op jit(solution)/shard_map/ppermute | solution.py:365
  17.8 17.9 %collective-permute-start.2 = (bf16[656,256]{1,0:T(8,128)(2,1)}, bf16[656,256]{1,0:T(8,128)(2,1)}, u32[]{:S(2)}, u32[]{:S(2)}) collective-permute-start(bf16[656,256]{1,0:T(8,128)(2,1)} %pad_maximum_fusion.3), channel_id=1, source_target_pairs={{0,24},{8,16},{16,8},{24,0},{32,56},{40,48},{48,40},{56,32},{64,88... | collective-permute-start | bytes 1007624 | tf_op jit(solution)/shard_map/ppermute | solution.py:365
  30.8 0.8 copy-start.1
  33.5 12.7 %collective-permute-start.13 = (bf16[32,1280]{1,0:T(8,128)(2,1)}, bf16[32,1280]{1,0:T(8,128)(2,1)S(1)}, u32[]{:S(2)}, u32[]{:S(2)}) collective-permute-start(bf16[32,1280]{1,0:T(8,128)(2,1)} %get-tuple-element.31), channel_id=1, source_target_pairs={{0,8},{8,0},{16,24},{24,16},{32,40},{40,32},{48,56},{56,48},{64,72... | collective-permute-start | bytes 245768 | tf_op jit(solution)/shard_map/ppermute | solution.py:365
  33.5 12.8 %collective-permute-start.14 = (bf16[32,1280]{1,0:T(8,128)(2,1)}, bf16[32,1280]{1,0:T(8,128)(2,1)S(1)}, u32[]{:S(2)}, u32[]{:S(2)}) collective-permute-start(bf16[32,1280]{1,0:T(8,128)(2,1)} %get-tuple-element.32), channel_id=1, source_target_pairs={{0,16},{8,24},{16,0},{24,8},{32,48},{40,56},{48,32},{56,40},{64,80... | collective-permute-start | bytes 245768 | tf_op jit(solution)/shard_map/ppermute | solution.py:365
  35.7 13.8 %collective-permute-start.15 = (bf16[32,1280]{1,0:T(8,128)(2,1)}, bf16[32,1280]{1,0:T(8,128)(2,1)S(1)}, u32[]{:S(2)}, u32[]{:S(2)}) collective-permute-start(bf16[32,1280]{1,0:T(8,128)(2,1)} %get-tuple-element.33), channel_id=1, source_target_pairs={{0,24},{8,16},{16,8},{24,0},{32,56},{40,48},{48,40},{56,32},{64,88... | collective-permute-start | bytes 245768 | tf_op jit(solution)/shard_map/ppermute | solution.py:365
  43.2 57.9 %collective-permute-start.10 = (bf16[640,640]{1,0:T(8,128)(2,1)S(1)}, bf16[640,640]{1,0:T(8,128)(2,1)S(1)}, u32[]{:S(2)}, u32[]{:S(2)}) collective-permute-start(bf16[640,640]{1,0:T(8,128)(2,1)S(1)} %get-tuple-element.52), channel_id=1, source_target_pairs={{0,6},{1,7},{2,0},{3,1},{4,2},{5,3},{6,4},{7,5},{8,14},{9,15},{10,... | collective-permute-start | bytes 2457608 | tf_op jit(solution)/shard_map/ppermute | solution.py:369
  46.2 54.9 %collective-permute-start.9 = (bf16[640,640]{1,0:T(8,128)(2,1)S(1)}, bf16[640,640]{1,0:T(8,128)(2,1)}, u32[]{:S(2)}, u32[]{:S(2)}) collective-permute-start(bf16[640,640]{1,0:T(8,128)(2,1)S(1)} %get-tuple-element.53), channel_id=1, source_target_pairs={{0,2},{1,3},{2,4},{3,5},{4,6},{5,7},{6,0},{7,1},{8,10},{9,11},{10,... | collective-permute-start | bytes 2457608 | tf_op jit(solution)/shard_map/ppermute | solution.py:369
  46.2 3.3 %copy-start.13 = (bf16[32,1280]{1,0:T(8,128)(2,1)}, bf16[32,1280]{1,0:T(8,128)(2,1)S(1)}, u32[]{:S(2)}) copy-start(bf16[32,1280]{1,0:T(8,128)(2,1)S(1)} %collective-permute-done.13.refs_1_) | copy-start | bytes 245764
  46.2 22.9 %collective-permute-start.4 = (bf16[272,1280]{1,0:T(8,128)(2,1)}, bf16[272,1280]{1,0:T(8,128)(2,1)}, u32[]{:S(2)}, u32[]{:S(2)}) collective-permute-start(bf16[272,1280]{1,0:T(8,128)(2,1)} %collective-permute-done.3.refs_5_.refs_6_.refs_7_), channel_id=1, source_target_pairs={{0,32},{8,40},{16,48},{24,56},{32,64},{40,72},{48,80},{56,88},{64,... | collective-permute-start | bytes 2088968 | tf_op jit(solution)/shard_map/ppermute | solution.py:362
  46.3 3.2 %copy-start.14 = (bf16[32,1280]{1,0:T(8,128)(2,1)}, bf16[32,1280]{1,0:T(8,128)(2,1)S(1)}, u32[]{:S(2)}) copy-start(bf16[32,1280]{1,0:T(8,128)(2,1)S(1)} %collective-permute-done.14.refs_2_) | copy-start | bytes 245764
  46.3 23.6 %collective-permute-start.7 = (bf16[272,1280]{1,0:T(8,128)(2,1)}, bf16[272,1280]{1,0:T(8,128)(2,1)}, u32[]{:S(2)}, u32[]{:S(2)}) collective-permute-start(bf16[272,1280]{1,0:T(8,128)(2,1)} %collective-permute-done.6.refs_8_.refs_9_.refs_10_), channel_id=1, source_target_pairs={{0,224},{8,232},{16,240},{24,248},{32,0},{40,8},{48,16},{56,24},{6... | collective-permute-start | bytes 2088968 | tf_op jit(solution)/shard_map/ppermute | solution.py:362
  49.6 0.6 copy-start.15
  51.9 14.6 %copy-start.8 = (bf16[32,1280]{1,0:T(8,128)(2,1)S(1)}, bf16[32,1280]{1,0:T(8,128)(2,1)}, u32[]{:S(2)}) copy-start(bf16[32,1280]{1,0:T(8,128)(2,1)} %choose.1) | copy-start | bytes 245764
  51.9 14.6 %collective-permute-start.16 = (bf16[32,1280]{1,0:T(8,128)(2,1)}, bf16[32,1280]{1,0:T(8,128)(2,1)S(1)}, u32[]{:S(2)}, u32[]{:S(2)}) collective-permute-start(bf16[32,1280]{1,0:T(8,128)(2,1)} %choose.1), channel_id=1, source_target_pairs={{0,64},{8,72},{16,80},{24,88},{32,96},{40,104},{48,112},{56,120},{... | collective-permute-start | bytes 245768 | tf_op jit(solution)/shard_map/ppermute | solution.py:362
  66.5 15.6 %collective-permute-start.18 = (bf16[32,1280]{1,0:T(8,128)(2,1)S(1)}, bf16[32,1280]{1,0:T(8,128)(2,1)S(1)}, u32[]{:S(2)}, u32[]{:S(2)}) collective-permute-start(bf16[32,1280]{1,0:T(8,128)(2,1)S(1)} %copy-done.8), channel_id=1, source_target_pairs={{0,32},{8,40},{16,48},{24,56},{32,64},{40,72},{48,80},{56,88},{64,... | collective-permute-start | bytes 245768 | tf_op jit(solution)/shard_map/ppermute | solution.py:362
  69.1 7.6 %collective-permute-start.20 = (bf16[32,1280]{1,0:T(8,128)(2,1)S(1)}, bf16[32,1280]{1,0:T(8,128)(2,1)S(1)}, u32[]{:S(2)}, u32[]{:S(2)}) collective-permute-start(bf16[32,1280]{1,0:T(8,128)(2,1)S(1)} %copy-done.8), channel_id=1, source_target_pairs={{0,192},{8,200},{16,208},{24,216},{32,224},{40,232},{48,240},{56,2... | collective-permute-start | bytes 245768 | tf_op jit(solution)/shard_map/ppermute | solution.py:362
  70.0 11.5 %collective-permute-start.17 = (bf16[32,1280]{1,0:T(8,128)(2,1)S(1)}, bf16[32,1280]{1,0:T(8,128)(2,1)S(1)}, u32[]{:S(2)}, u32[]{:S(2)}) collective-permute-start(bf16[32,1280]{1,0:T(8,128)(2,1)S(1)} %collective-permute-done.16), channel_id=1, source_target_pairs={{0,32},{8,40},{16,48},{24,56},{32,64},{40,72},{48,80},{56,88},{64,... | collective-permute-start | bytes 245768 | tf_op jit(solution)/shard_map/ppermute | solution.py:362
  76.8 7.0 %collective-permute-start.19 = (bf16[32,1280]{1,0:T(8,128)(2,1)S(1)}, bf16[32,1280]{1,0:T(8,128)(2,1)S(1)}, u32[]{:S(2)}, u32[]{:S(2)}) collective-permute-start(bf16[32,1280]{1,0:T(8,128)(2,1)S(1)} %copy-done.8), channel_id=1, source_target_pairs={{0,224},{8,232},{16,240},{24,248},{32,0},{40,8},{48,16},{56,24},{6... | collective-permute-start | bytes 245768 | tf_op jit(solution)/shard_map/ppermute | solution.py:362
  81.5 5.7 %collective-permute-start.21 = (bf16[32,1280]{1,0:T(8,128)(2,1)S(1)}, bf16[32,1280]{1,0:T(8,128)(2,1)S(1)}, u32[]{:S(2)}, u32[]{:S(2)}) collective-permute-start(bf16[32,1280]{1,0:T(8,128)(2,1)S(1)} %collective-permute-done.20), channel_id=1, source_target_pairs={{0,224},{8,232},{16,240},{24,248},{32,0},{40,8},{48,16},{56,24},{6... | collective-permute-start | bytes 245768 | tf_op jit(solution)/shard_map/ppermute | solution.py:362
  82.1 19.2 %collective-permute-start.5 = (bf16[272,1280]{1,0:T(8,128)(2,1)}, bf16[272,1280]{1,0:T(8,128)(2,1)S(1)}, u32[]{:S(2)}, u32[]{:S(2)}) collective-permute-start(bf16[272,1280]{1,0:T(8,128)(2,1)} %collective-permute-done.4.refs_2_.refs_3_.refs_4_), channel_id=1, source_target_pairs={{0,32},{8,40},{16,48},{24,56},{32,64},{40,72},{48,80},{56,88},{64,... | collective-permute-start | bytes 2088968 | tf_op jit(solution)/shard_map/ppermute | solution.py:362
  83.8 17.5 %collective-permute-start.8 = (bf16[272,1280]{1,0:T(8,128)(2,1)}, bf16[272,1280]{1,0:T(8,128)(2,1)S(1)}, u32[]{:S(2)}, u32[]{:S(2)}) collective-permute-start(bf16[272,1280]{1,0:T(8,128)(2,1)} %collective-permute-done.7.refs_5_.refs_6_.refs_7_), channel_id=1, source_target_pairs={{0,224},{8,232},{16,240},{24,248},{32,0},{40,8},{48,16},{56,24},{6... | collective-permute-start | bytes 2088968 | tf_op jit(solution)/shard_map/ppermute | solution.py:362
  87.2 13.6 %collective-permute-start.22 = (bf16[32,1280]{1,0:T(8,128)(2,1)S(1)}, bf16[32,1280]{1,0:T(8,128)(2,1)S(1)}, u32[]{:S(2)}, u32[]{:S(2)}) collective-permute-start(bf16[32,1280]{1,0:T(8,128)(2,1)S(1)} %collective-permute-done.16), channel_id=1, source_target_pairs={{0,64},{8,72},{16,80},{24,88},{32,96},{40,104},{48,112},{56,120},{... | collective-permute-start | bytes 245768 | tf_op jit(solution)/shard_map/ppermute | solution.py:362
  100.8 15.9 %collective-permute-start.23 = (bf16[640,640]{1,0:T(8,128)(2,1)S(1)}, bf16[640,640]{1,0:T(8,128)(2,1)}, u32[]{:S(2)}, u32[]{:S(2)}) collective-permute-start(bf16[640,640]{1,0:T(8,128)(2,1)S(1)} %get-tuple-element.51), channel_id=1, source_target_pairs={{0,4},{1,5},{2,6},{3,7},{4,0},{5,1},{6,2},{7,3},{8,12},{9,13},{10,... | collective-permute-start | bytes 2457608 | tf_op jit(solution)/shard_map/ppermute | solution.py:369
  101.1 0.8 copy-start.16
  101.1 10.8 %copy-start.2 = (bf16[640,640]{1,0:T(8,128)(2,1)}, bf16[640,640]{1,0:T(8,128)(2,1)S(1)}, u32[]{:S(2)}) copy-start(bf16[640,640]{1,0:T(8,128)(2,1)S(1)} %collective-permute-done.10) | copy-start | bytes 2457604
  101.3 5.0 %copy-start.11 = (bf16[272,1280]{1,0:T(8,128)(2,1)}, bf16[272,1280]{1,0:T(8,128)(2,1)S(1)}, u32[]{:S(2)}) copy-start(bf16[272,1280]{1,0:T(8,128)(2,1)S(1)} %collective-permute-done.5.refs_2_.refs_3_.refs_4_) | copy-start | bytes 2088964
  101.3 5.0 %copy-start.12 = (bf16[272,1280]{1,0:T(8,128)(2,1)}, bf16[272,1280]{1,0:T(8,128)(2,1)S(1)}, u32[]{:S(2)}) copy-start(bf16[272,1280]{1,0:T(8,128)(2,1)S(1)} %collective-permute-done.8.refs_5_.refs_6_.refs_7_) | copy-start | bytes 2088964
  101.3 15.5 %collective-permute-start.24 = (bf16[640,640]{1,0:T(8,128)(2,1)}, bf16[640,640]{1,0:T(8,128)(2,1)S(1)}, u32[]{:S(2)}, u32[]{:S(2)}) collective-permute-start(bf16[640,640]{1,0:T(8,128)(2,1)} %collective-permute-done.9), channel_id=1, source_target_pairs={{0,8},{8,0},{16,24},{24,16},{32,40},{40,32},{48,56},{56,48},{64,72... | collective-permute-start | bytes 2457608 | tf_op jit(solution)/shard_map/ppermute | solution.py:365
  101.9 14.8 %collective-permute-start.25 = (bf16[640,640]{1,0:T(8,128)(2,1)S(1)}, bf16[640,640]{1,0:T(8,128)(2,1)S(1)}, u32[]{:S(2)}, u32[]{:S(2)}) collective-permute-start(bf16[640,640]{1,0:T(8,128)(2,1)S(1)} %collective-permute-done.10), channel_id=1, source_target_pairs={{0,8},{8,0},{16,24},{24,16},{32,40},{40,32},{48,56},{56,48},{64,72... | collective-permute-start | bytes 2457608 | tf_op jit(solution)/shard_map/ppermute | solution.py:365
  102.0 14.8 %collective-permute-start.11 = (bf16[272,640]{1,0:T(8,128)(2,1)S(1)}, bf16[272,640]{1,0:T(8,128)(2,1)}, u32[]{:S(2)}, u32[]{:S(2)}) collective-permute-start(bf16[272,640]{1,0:T(8,128)(2,1)S(1)} %slice.27), channel_id=1, source_target_pairs={{0,32},{8,40},{16,48},{24,56},{32,64},{40,72},{48,80},{56,88},{64,... | collective-permute-start | bytes 1044488 | tf_op jit(solution)/shard_map/ppermute | solution.py:362
  106.2 10.5 %collective-permute-start.12 = (bf16[256,640]{1,0:T(8,128)(2,1)S(1)}, bf16[256,640]{1,0:T(8,128)(2,1)}, u32[]{:S(2)}, u32[]{:S(2)}) collective-permute-start(bf16[256,640]{1,0:T(8,128)(2,1)S(1)} %slice.28), channel_id=1, source_target_pairs={{0,224},{8,232},{16,240},{24,248},{32,0},{40,8},{48,16},{56,24},{6... | collective-permute-start | bytes 983048 | tf_op jit(solution)/shard_map/ppermute | solution.py:362
  116.7 8.4 %collective-permute-start.26 = (bf16[640,640]{1,0:T(8,128)(2,1)}, bf16[640,640]{1,0:T(8,128)(2,1)S(1)}, u32[]{:S(2)}, u32[]{:S(2)}) collective-permute-start(bf16[640,640]{1,0:T(8,128)(2,1)} %collective-permute-done.23), channel_id=1, source_target_pairs={{0,8},{8,0},{16,24},{24,16},{32,40},{40,32},{48,56},{56,48},{64,72... | collective-permute-start | bytes 2457608 | tf_op jit(solution)/shard_map/ppermute | solution.py:365
  125.1 39.0 %copy-start.3 = (bf16[640,640]{1,0:T(8,128)(2,1)S(1)}, bf16[640,640]{1,0:T(8,128)(2,1)}, u32[]{:S(2)}) copy-start(bf16[640,640]{1,0:T(8,128)(2,1)} %copy-done.2) | copy-start | bytes 2457604
  125.1 17.0 %copy-start.4 = (bf16[640,640]{1,0:T(8,128)(2,1)}, bf16[640,640]{1,0:T(8,128)(2,1)S(1)}, u32[]{:S(2)}) copy-start(bf16[640,640]{1,0:T(8,128)(2,1)S(1)} %collective-permute-done.26) | copy-start | bytes 2457604
  125.1 2.7 %collective-permute-start.27 = (bf16[656,512]{1,0:T(8,128)(2,1)}, bf16[656,512]{1,0:T(8,128)(2,1)}, u32[]{:S(2)}, u32[]{:S(2)}) collective-permute-start(bf16[656,512]{1,0:T(8,128)(2,1)} %get-tuple-element.47), channel_id=1, source_target_pairs={{0,8},{8,0},{16,24},{24,16},{32,40},{40,32},{48,56},{56,48},{64,72... | collective-permute-start | bytes 2015240 | tf_op jit(solution)/shard_map/ppermute | solution.py:365
  130.2 11.9 %collective-permute-start.28 = (bf16[656,256]{1,0:T(8,128)(2,1)}, bf16[656,256]{1,0:T(8,128)(2,1)S(1)}, u32[]{:S(2)}, u32[]{:S(2)}) collective-permute-start(bf16[656,256]{1,0:T(8,128)(2,1)} %get-tuple-element.49), channel_id=1, source_target_pairs={{0,16},{8,24},{16,0},{24,8},{32,48},{40,56},{48,32},{56,40},{64,80... | collective-permute-start | bytes 1007624 | tf_op jit(solution)/shard_map/ppermute | solution.py:365
  142.1 0.7 copy-start.6
  144.9 17.6 %collective-permute-start.29 = (bf16[256,640]{1,0:T(8,128)(2,1)}, bf16[256,640]{1,0:T(8,128)(2,1)S(1)}, u32[]{:S(2)}, u32[]{:S(2)}) collective-permute-start(bf16[256,640]{1,0:T(8,128)(2,1)} %merge.3), channel_id=1, source_target_pairs={{0,2},{1,3},{2,4},{3,5},{4,6},{5,7},{6,0},{7,1},{8,10},{9,11},{10,... | collective-permute-start | bytes 983048 | tf_op jit(solution)/shard_map/ppermute | solution.py:369
  145.9 18.2 %collective-permute-start.30 = (bf16[256,640]{1,0:T(8,128)(2,1)}, bf16[256,640]{1,0:T(8,128)(2,1)S(1)}, u32[]{:S(2)}, u32[]{:S(2)}) collective-permute-start(bf16[256,640]{1,0:T(8,128)(2,1)} %merge.3), channel_id=1, source_target_pairs={{0,6},{1,7},{2,0},{3,1},{4,2},{5,3},{6,4},{7,5},{8,14},{9,15},{10,... | collective-permute-start | bytes 983048 | tf_op jit(solution)/shard_map/ppermute | solution.py:369
  148.1 18.1 %copy-start = (bf16[256,640]{1,0:T(8,128)(2,1)S(1)}, bf16[256,640]{1,0:T(8,128)(2,1)}, u32[]{:S(2)}) copy-start(bf16[256,640]{1,0:T(8,128)(2,1)} %merge.3) | copy-start | bytes 983044
  148.1 16.5 %collective-permute-start.31 = (bf16[256,640]{1,0:T(8,128)(2,1)}, bf16[256,640]{1,0:T(8,128)(2,1)S(1)}, u32[]{:S(2)}, u32[]{:S(2)}) collective-permute-start(bf16[256,640]{1,0:T(8,128)(2,1)} %merge.3), channel_id=1, source_target_pairs={{0,4},{1,5},{2,6},{3,7},{4,0},{5,1},{6,2},{7,3},{8,12},{9,13},{10,... | collective-permute-start | bytes 983048 | tf_op jit(solution)/shard_map/ppermute | solution.py:369
  167.8 1.1 copy-start.5
  171.1 7.2 %collective-permute-start.32 = (bf16[256,640]{1,0:T(8,128)(2,1)S(1)}, bf16[256,640]{1,0:T(8,128)(2,1)S(1)}, u32[]{:S(2)}, u32[]{:S(2)}) collective-permute-start(bf16[256,640]{1,0:T(8,128)(2,1)S(1)} %get-tuple-element.54), channel_id=1, source_target_pairs={{0,1},{1,0},{2,3},{3,2},{4,5},{5,4},{6,7},{7,6},{8,9},{9,8},{10,11... | collective-permute-start | bytes 983048 | tf_op jit(solution)/shard_map/ppermute | solution.py:434
where the time goes:
time: 182 us; the launch traced here: 179 us
  waiting for transfers between devices  61.8 us (34%)
  starting transfers between devices  52.1 us (29%)
  Pallas kernels  43.6 us (24%)
  matrix products  8.25 us (5%)
  other arithmetic  7.69 us (4%)
  local copies, waits for them, and re-layouts  5.22 us (3%)
    pallas_call x4, Pallas kernels, attention_call(): pl.pallas_call(functools.partial(attention_kernel, len(chunks), first, la...  29.1 us
    ppermute x15, starting transfers between devices, shift(): return lax.ppermute(item, 'blk', steps)  26.3 us
    ppermute x15, waiting for transfers between devices, shift(): return lax.ppermute(item, 'blk', steps)  22.1 us
    ppermute x6, waiting for transfers between devices, shift_y(): return lax.ppermute(item, 'heads', steps)  18.9 us
    ppermute x11, waiting for transfers between devices, swap(): return lax.ppermute(item, 'blk', [(i, i ^ mask) for i in range(blk_count)])  11.9 us
    ppermute x11, starting transfers between devices, swap(): return lax.ppermute(item, 'blk', [(i, i ^ mask) for i in range(blk_count)])  9.81 us
    all_to_all x1, starting transfers between devices, shards(): pieces = lax.all_to_all(slot, 'blk', 0, 0, axis_index_groups=columns)  8.47 us
    dot_general x8, matrix products, dots(): jnp.dot(block, item[step], preferred_element_type=jnp.float32)  8.25 us
  transfers between devices with their start and end apart: 34, of which 11 were waited for; matrix products, arithmetic and copies ran while one was open for 5% of the time, Pallas kernels for 22%

commit v1 on v0

--- a/solution.py
+++ b/solution.py
@@ -19,18 +19,17 @@
     return DH ** (-0.5) * math.log2(math.e)
 
 
-def attention_kernel(chunk_count, first, last, with_ctx, head_count, rows, *refs):
+def attention_kernel(layout, first, last, with_ctx, head_count, rows, *refs):
     refs = list(refs)
     ctx_info = refs.pop(0) if with_ctx else None
+    refs.pop(0)
     query_ref = refs.pop(0)
     query_marks = refs.pop(0)
     chunks = []
-    for index in range(chunk_count):
-        is_ctx = with_ctx and index == chunk_count - 1
-        key_ref = refs.pop(0)
-        value_ref = refs.pop(0)
-        mark_ref = None if is_ctx else refs.pop(0)
-        chunks.append((key_ref, value_ref, mark_ref))
+    for segments, marked in layout:
+        keys = [(refs.pop(0), refs.pop(0), begin, count) for begin, count in segments]
+        chunks.append((keys, refs.pop(0) if marked else None))
+    chunk_count = len(chunks)
     if not first:
         acc_in = refs.pop(0)
         stat_in = refs.pop(0)
@@ -53,7 +52,7 @@
 
     @pl.when(head == 0)
     def _():
-        for index, (_, _, mark_ref) in enumerate(chunks):
+        for index, (_, mark_ref) in enumerate(chunks):
             if mark_ref is None:
                 live = ctx_info[4 + jnp.bitwise_and(ctx_info[8], 3)]
                 limits[index, 0:1, :] = jnp.full(
@@ -76,7 +75,14 @@
         if with_ctx:
             start = (lax.shift_right_logical(ctx_info[8], 2) + 5) * (rows // 8)
             places[-1] = jnp.bitwise_and(row + start, rows - 1).astype(jnp.float32)
-        turned = [value_ref[...].T for _, value_ref, _ in chunks]
+        keys = [
+            jnp.concatenate([ref[begin : begin + count] for ref, _, begin, count in segments])
+            for segments, _ in chunks
+        ]
+        turned = [
+            jnp.concatenate([ref[begin : begin + count] for _, ref, begin, count in segments]).T
+            for segments, _ in chunks
+        ]
         for tile in range(4 * rows // lane):
             spot = slice(tile * lane, (tile + 1) * lane)
             query = query_ref[:, spot]
@@ -86,8 +92,8 @@
                 acc = jnp.zeros((DH, lane), jnp.float32)
             else:
                 top, total, acc = stat_in[0:1, spot], stat_in[1:2, spot], acc_in[:, spot]
-            for index, (key_ref, _, _) in enumerate(chunks):
-                scores = jnp.dot(key_ref[...], query, preferred_element_type=jnp.float32)
+            for index in range(chunk_count):
+                scores = jnp.dot(keys[index], query, preferred_element_type=jnp.float32)
                 scores = jnp.where(places[index] < limits[index, 0:1, spot], scores, MASKED)
                 top_new = jnp.maximum(top, jnp.max(scores, axis=0, keepdims=True))
                 weights = jnp.exp2((scores - top_new) * factor)
@@ -142,7 +148,7 @@
             send_out[feat : feat + 16, :] = stats[:, 2 * rows : 4 * rows].astype(jnp.bfloat16)
 
 
-def attention_call(queries, chunks, state, ctx_info, last):
+def attention_call(queries, chunks, state, ctx_info, last, token):
     feat = queries.shape[0] - 16
     rows = queries.shape[1] // 4
     head_count = feat // DH
@@ -152,18 +158,29 @@
     if with_ctx:
         operands.append(ctx_info)
         specs.append(pl.BlockSpec(memory_space=pltpu.SMEM))
-    operands += [queries, queries]
+    operands += [token, queries, queries]
+    specs.append(pl.BlockSpec(memory_space=pl.ANY))
     specs.append(pl.BlockSpec((DH, 4 * rows), lambda h: (h, 0)))
     specs.append(pl.BlockSpec((16, 4 * rows), lambda h: (feat // 16, 0)))
-    for index, chunk in enumerate(chunks):
-        keys, values = chunk if isinstance(chunk, tuple) else (chunk, chunk)
-        first_value = values.shape[1] // DH - head_count
-        operands += [keys, values]
-        specs.append(pl.BlockSpec((rows, DH), lambda h: (0, h)))
-        specs.append(pl.BlockSpec((rows, DH), lambda h, base=first_value: (0, base + h)))
-        if not (with_ctx and index == len(chunks) - 1):
-            operands.append(keys)
-            specs.append(pl.BlockSpec((16, rows), lambda h: (rows // 16, 0)))
+    layout = []
+    for segments, marks in chunks:
+        places = []
+        for array, begin, count in segments:
+            block, wanted = 0, count
+            if begin % count == 0:
+                block, begin = begin // count, 0
+            else:
+                count = array.shape[0]
+            operands += [array, array]
+            specs.append(pl.BlockSpec((count, DH), lambda h, at=block: (at, h)))
+            specs.append(pl.BlockSpec((count, DH), lambda h, at=block: (at, head_count + h)))
+            places.append((begin, wanted))
+        layout.append((tuple(places), marks is not None))
+        if marks is not None:
+            operands.append(marks)
+            specs.append(
+                pl.BlockSpec((16, rows), lambda h, at=marks.shape[0] // 16 - 1: (at, 0))
+            )
     aliases = {}
     state_specs = [
         pl.BlockSpec((DH, 4 * rows), lambda h: (h, 0)),
@@ -195,7 +212,7 @@
         ]
     return pl.pallas_call(
         functools.partial(
-            attention_kernel, len(chunks), first, last, with_ctx, head_count, rows
+            attention_kernel, layout, first, last, with_ctx, head_count, rows
         ),
         grid=(head_count,),
         in_specs=specs,
@@ -272,27 +289,27 @@
     )(a, b)
 
 
-def columns_kernel(info, in_ref, out_ref):
-    out_ref[0] = in_ref[...]
+def columns_kernel(ring, info, in_ref, *out_refs):
+    width = out_refs[0].shape[1]
+    core = jnp.bitwise_and(info[8], 1)
+    for step, out_ref in enumerate(out_refs):
+        target = jnp.bitwise_and(lax.shift_right_logical(info[9], 1) + step, ring - 1)
+        half = core if step < ring else 1 - core
+        begin = pl.multiple_of((2 * target + half) * width, DH)
+        out_ref[...] = in_ref[:, pl.ds(begin, width)]
 
 
 def column_blocks(weight, info, width, ring):
-    rows = weight.shape[0]
-
-    def place(j, info):
-        target = jnp.bitwise_and(lax.shift_right_logical(info[9], 1) + j, ring - 1)
-        half = jnp.bitwise_xor(jnp.bitwise_and(info[8], 1), lax.shift_right_logical(j, 2))
-        return (0, 2 * target + half)
-
+    rows, total = weight.shape
     return pl.pallas_call(
-        columns_kernel,
-        grid_spec=pltpu.PrefetchScalarGridSpec(
-            num_scalar_prefetch=1,
-            grid=(ring + 1,),
-            in_specs=[pl.BlockSpec((rows, width), place)],
-            out_specs=pl.BlockSpec((1, rows, width), lambda j, info: (j, 0, 0)),
-        ),
-        out_shape=jax.ShapeDtypeStruct((ring + 1, rows, width), weight.dtype),
+        functools.partial(columns_kernel, ring),
+        grid=(rows // DH,),
+        in_specs=[
+            pl.BlockSpec(memory_space=pltpu.SMEM),
+            pl.BlockSpec((DH, total), lambda i: (i, 0)),
+        ],
+        out_specs=[pl.BlockSpec((DH, width), lambda i: (i, 0))] * (ring + 1),
+        out_shape=[jax.ShapeDtypeStruct((rows, width), weight.dtype)] * (ring + 1),
         compiler_params=pltpu.CompilerParams(vmem_limit_bytes=VMEM),
         cost_estimate=pl.CostEstimate(
             flops=0, bytes_accessed=4 * (ring + 1) * rows * width, transcendentals=0
@@ -369,51 +386,79 @@
         return lax.ppermute(item, "heads", steps)
 
     marks = jnp.pad(frame_ids.astype(jnp.bfloat16)[None], ((0, 15), (0, 2 * feat - rows)))
-    own = jnp.concatenate([jnp.concatenate([key_rows, value_rows], axis=1), marks], axis=0)
+    mid = rows // 2
+    part = ctx_keys.shape[1] // depth
+    both = jnp.concatenate([key_rows, value_rows], axis=1)
+    own = jnp.concatenate([both[:mid], jnp.zeros((part, 2 * feat), both.dtype), both[mid:], marks])
     query_own = jnp.concatenate([queries.T, marks[:, :rows]], axis=0)
-    part = ctx_keys.shape[1] // depth
     slot = jnp.concatenate([ctx_keys[0], ctx_values[0]], axis=1).reshape(depth, part, 2 * feat)
 
     ahead, behind = shift(own, 1), shift(own, -1)
     query_x, query_core, query_both = swap(query_own, 2), swap(query_own, 1), swap(query_own, 3)
     pieces = lax.all_to_all(slot, "blk", 0, 0, axis_index_groups=columns)
     slabs = column_blocks(out_weight, info, feat, ring_y)
-    query_plane = jnp.concatenate([query_own, query_x, query_core, query_both], axis=1)
+    pieces, query_x, query_core, query_both, *slabs = lax.optimization_barrier(
+        (pieces, query_x, query_core, query_both, *slabs)
+    )
     offers = list(offer_pieces(pieces, info))
-
-    *state, _ = attention_call(query_plane, [own, ahead, behind], None, None, False)
-    ahead, behind = shift(ahead, 1), shift(behind, -1)
     offers = offers[:1] + [swap(offers[mask], mask) for mask in range(1, plane)]
     piece = choose_piece(offers, info)
 
-    *state, _ = attention_call(query_plane, [ahead, behind], state, None, False)
-    ahead, behind = shift(ahead, 1), shift(behind, -1)
-    ctx = {0: piece}
-    for distance in (1, -1, 2, -2):
-        ctx[distance] = shift(piece, distance)
-    slab_near = shift_y(slabs[1], 1)
-    slab_back = shift_y(slabs[ring_y - 1], ring_y - 1)
-    ahead, behind, slab_near, slab_back = lax.optimization_barrier(
-        (ahead, behind, slab_near, slab_back)
-    )
-
-    far = ahead[:, :feat], behind[:rows, feat:]
-    *state, _ = attention_call(query_plane, [ahead, behind], state, None, False)
-    far = shift(far[0], 1), shift(far[1], -1)
-    ctx[3] = shift(ctx[2], 1)
-    ctx[4] = shift(ctx[2], 2)
-    ctx[-3] = shift(ctx[-2], -1)
-    slab_far = shift_y(slabs[2], 2)
-    ctx = jnp.concatenate([ctx[distance] for distance in (3, 2, 1, 0, -1, -2, -3, 4)], axis=0)
-    own_slabs = [slabs[0], slab_near, slab_far, slab_back]
-    core_slabs = [slabs[ring_y], swap(slab_near, 1), None, swap(slab_back, 1)]
-    ctx, slab_far, *_ = lax.optimization_barrier((ctx, slab_far, core_slabs[1], core_slabs[3]))
-    core_slabs[2] = swap(slab_far, 1)
-    keep, send = attention_call(query_plane, [far, ctx], state, info, True)
-    keep, send, core_slabs[2] = lax.optimization_barrier((keep, send, core_slabs[2]))
+    def loaded(item):
+        return lax.dynamic_update_slice(item, piece, (mid, 0))
+
+    def halves(item):
+        return [(item, 0, mid), (item, mid + part, mid)], item
+
+    def carried(item):
+        return item, mid, part
+
+    slab_own, slab_core = slabs[0], slabs[ring_y]
+    *first, query_x, query_core, query_both, slab_near, slab_far, slab_back = (
+        lax.optimization_barrier(
+            (loaded(ahead), loaded(behind), query_x, query_core, query_both, *slabs[1:ring_y])
+        )
+    )
+    query_plane = jnp.concatenate([query_own, query_x, query_core, query_both], axis=1)
+    ahead, behind = shift(first[0], 1), shift(first[1], -1)
+    *state, token = attention_call(
+        query_plane, [halves(item) for item in (own, *first)], None, None, False, info
+    )
+    slab_near = shift_y(slab_near, 1)
+    slab_back = shift_y(slab_back, ring_y - 1)
+    slab_far = shift_y(slab_far, 2)
+
+    *second, token = lax.optimization_barrier((ahead, behind, token))
+    ahead, behind = shift(second[0], 1), shift(second[1], -1)
+    *state, token = attention_call(
+        query_plane, [halves(item) for item in second], state, None, False, token
+    )
+    ahead, behind, slab_near, slab_back, slab_far, token = lax.optimization_barrier(
+        (ahead, behind, slab_near, slab_back, slab_far, token)
+    )
+
+    far_ahead, far_behind = shift(ahead[: mid + part], 1), shift(behind[mid:], -1)
+    opposite = shift(ahead[mid : mid + part], 2)
+    *state, token = attention_call(
+        query_plane, [halves(ahead), halves(behind)], state, None, False, token
+    )
+    far = [(far_ahead, 0, mid), (far_behind, part, mid)], far_behind
+    ctx = [
+        (far_ahead, mid, part),
+        carried(ahead),
+        carried(second[0]),
+        (piece, 0, part),
+        carried(second[1]),
+        carried(behind),
+        (far_behind, 0, part),
+        (opposite, 0, part),
+    ]
+    keep, send = attention_call(query_plane, [far, (ctx, None)], state, info, True, token)
     received = swap(send, 1)
     own, other = merge_call(keep, received, False)
-    received = swap(other, 2)
+    own_slabs = [slab_own, slab_near, slab_far, slab_back]
+    core_slabs = [slab_core] + [swap(item, 1) for item in own_slabs[1:]]
+    received, *core_slabs = lax.optimization_barrier((swap(other, 2), *core_slabs))
     attended = merge_call(own, received, True)
 
     def dots(block, step):
@@ -423,11 +468,10 @@
         ]
 
     total = dots(attended, 0)
-    block_near, block_back = shift_y(attended, 1), shift_y(attended, ring_y - 1)
-    block_far = shift_y(attended, 2)
-    added = [dots(block_near, 1), dots(block_back, ring_y - 1)]
-    added.append(dots(block_far, 2))
-    total = [sum(items) for items in zip(total, *added)]
+    blocks = [(shift_y(attended, step), step) for step in (1, ring_y - 1, 2)]
+    for block, step in blocks:
+        block, *total = lax.optimization_barrier((block, *total))
+        total = [old + new for old, new in zip(total, dots(block, step))]
     same = jnp.bitwise_and(jnp.bitwise_xor(me, head_me), 1) == 0
     mine = jnp.where(same, total[0], total[1])
     other = jnp.where(same, total[1], total[0])

time: 182 us -> 170 us (0.934)
  starting transfers between devices: 52.1 us -> 43.9 us
  waiting for transfers between devices: 61.8 us -> 58.6 us
  other arithmetic: 7.69 us -> 5.32 us
    ppermute x15 -> x9, waiting for transfers between devices: 22.1 us -> 5.29 us  [shift(): return lax.ppermute(item, 'blk', steps)]
    ppermute x15 -> x9, starting transfers between devices: 26.3 us -> 14.5 us  [shift(): return lax.ppermute(item, 'blk', steps)]
    ppermute x11, waiting for transfers between devices: 11.9 us -> 23 us  [swap(): return lax.ppermute(item, 'blk', [(i, i ^ mask) for i in range(blk_count)])]
    ppermute x6, waiting for transfers between devices: 18.9 us -> 24.6 us  [shift_y(): return lax.ppermute(item, 'heads', steps)]
    all_to_all x1, waiting for transfers between devices: 2.43 us -> 0.01 us  [shards(): pieces = lax.all_to_all(slot, 'blk', 0, 0, axis_index_groups=columns)]
    ppermute x6, starting transfers between devices: 6.86 us -> 9.03 us  [shift_y(): return lax.ppermute(item, 'heads', steps)]
    squeeze x1 -> x0, local copies, waits for them, and re-layouts: 1.85 us -> none  [shards(): slab_far = shift_y(slabs[2], 2)]
  transfers between devices with their start and end apart: 34 -> 28, of which waited for: 11 -> 11; matrix products, arithmetic and copies ran while one was open for 5% -> 7% of each run, Pallas kernels for 22% -> 20%
where the time goes in v1:
time: 170 us; the launch traced here: 168 us
  waiting for transfers between devices  58.6 us (34%)
  Pallas kernels  44.8 us (26%)
  starting transfers between devices  43.9 us (26%)
  matrix products  9.25 us (5%)
  local copies, waits for them, and re-layouts  6.13 us (4%)
  other arithmetic  5.32 us (3%)
    pallas_call x4, Pallas kernels, attention_call(): pl.pallas_call(functools.partial(attention_kernel, layout, first, last, w...  30.3 us
    ppermute x6, waiting for transfers between devices, shift_y(): return lax.ppermute(item, 'heads', steps)  24.6 us
    ppermute x11, waiting for transfers between devices, swap(): return lax.ppermute(item, 'blk', [(i, i ^ mask) for i in range(blk_count)])  23 us
    ppermute x9, starting transfers between devices, shift(): return lax.ppermute(item, 'blk', steps)  14.5 us
    ppermute x11, starting transfers between devices, swap(): return lax.ppermute(item, 'blk', [(i, i ^ mask) for i in range(blk_count)])  10.4 us
    dot_general x8, matrix products, dots(): jnp.dot(block, item[step], preferred_element_type=jnp.float32)  9.25 us
    ppermute x6, starting transfers between devices, shift_y(): return lax.ppermute(item, 'heads', steps)  9.03 us
    all_to_all x1, starting transfers between devices, shards(): pieces = lax.all_to_all(slot, 'blk', 0, 0, axis_index_groups=columns)  8.47 us
  transfers between devices with their start and end apart: 28, of which 11 were waited for; matrix products, arithmetic and copies ran while one was open for 7% of the time, Pallas kernels for 20%

profile of v1, /device:TPU:2, one launch (start us, length us, event | category | flops | bytes accessed | tf_op | source)
XLA Modules:
  0.0 168.4 jit_solution(8304400647723700390)
XLA Ops:
  0.0 2.0 %pad_maximum_fusion.2 = bf16[8,32,1280]{2,1,0:T(8,128)(2,1)} fusion(bf16[8,32,640]{2,1,0:T(8,128)(2,1)} %bitcast.23, bf16[8,32,640]{2,1,0:T(8,128)(2,1)} %bitcast.24), kind=kLoop, calls=%fused_computation.2 | loop fusion | flops 1310720 | bytes 1310720 | tf_op jit(solution)/shard_map/concatenate | solution.py:394
  2.0 8.5 %all-to-all-start = ((bf16[8,32,1280]{2,1,0:T(8,128)(2,1)}), bf16[8,32,1280]{2,1,0:T(8,128)(2,1)S(1)}, u32[]{:S(2)}, u32[]{:S(2)}) async-start(bf16[8,32,1280]{2,1,0:T(8,128)(2,1)} %pad_maximum_fusion.2), calls=%async_computation | async-start | bytes 1310720 | tf_op jit(solution)/shard_map/all_to_all | solution.py:398
  10.8 0.2 pad_maximum_fusion.1.refs_3_.refs_4_.refs_5_.refs_6_.refs_7_
  11.0 3.3 %collective-permute-start.7 = (bf16[304,1280]{1,0:T(8,128)(2,1)S(1)}, bf16[304,1280]{1,0:T(8,128)(2,1)}, u32[]{:S(2)}, u32[]{:S(2)}) collective-permute-start(bf16[304,1280]{1,0:T(8,128)(2,1)S(1)} %pad_maximum_fusion.1.refs_3_.refs_4_.refs_5_.refs_6_.refs_7_), channel_id=1, source_target_pairs={{0,224},{8,232},{16,240},{24,248},{32,0},{40,8},{48,16},{56,24},{6... | collective-permute-start | bytes 2334728 | tf_op jit(solution)/shard_map/ppermute | solution.py:379
  14.5 0.8 collective-permute-start.3
  15.3 1.5 collective-permute-start.2
  16.8 1.4 collective-permute-start.1
  18.3 0.7 pad_add_fusion.info.refs_0_
  18.9 6.5 %columns.1 = (bf16[640,640]{1,0:T(8,128)(2,1)}, bf16[640,640]{1,0:T(8,128)(2,1)}, bf16[640,640]{1,0:T(8,128)(2,1)}, bf16[640,640]{1,0:T(8,128)(2,1)}, bf16[640,640]{1,0:T(8,128)(2,1)}) custom-call(s32[10]{0:T(128)} %pad_add_fusion.info.refs_0_, bf16[640,5120]{1,0:T(8,128)(2,1)} %in_ref.1), custom_call_target="tpu_custom_call" | custom-call | bytes 8192000 | tf_op jit(solution)/shard_map/columns/pallas_call | solution.py:304
  25.4 0.9 collective-permute-done.3
  26.3 5.6 %collective-permute-done.1 = bf16[656,256]{1,0:T(8,128)(2,1)S(1)} collective-permute-done((bf16[656,256]{1,0:T(8,128)(2,1)S(1)}, bf16[656,256]{1,0:T(8,128)(2,1)S(1)}, u32[]{:S(2)}, u32[]{:S(2)}) %collective-permute-start.1) | collective-permute-done | bytes 335904 | tf_op jit(solution)/shard_map/ppermute | solution.py:382
  31.9 0.8 copy-done.1
  32.7 1.8 %offer.1 = (bf16[32,1280]{1,0:T(8,128)(2,1)}, bf16[32,1280]{1,0:T(8,128)(2,1)}, bf16[32,1280]{1,0:T(8,128)(2,1)}, bf16[32,1280]{1,0:T(8,128)(2,1)}) custom-call(s32[10]{0:T(128)} %pad_add_fusion.info.refs_0_, bf16[8,32,1280]{2,1,0:T(8,128)(2,1)} %copy-done.1), custom_call_target="tpu_custom_call" | custom-call | tf_op jit(solution)/shard_map/offer/pallas_call | solution.py:328
  34.6 1.0 collective-permute-start.4
  35.6 1.7 %collective-permute-start.5 = (bf16[32,1280]{1,0:T(8,128)(2,1)}, bf16[32,1280]{1,0:T(8,128)(2,1)S(1)}, u32[]{:S(2)}, u32[]{:S(2)}) collective-permute-start(bf16[32,1280]{1,0:T(8,128)(2,1)} %get-tuple-element.75), channel_id=1, source_target_pairs={{0,16},{8,24},{16,0},{24,8},{32,48},{40,56},{48,32},{56,40},{64,80... | collective-permute-start | bytes 245768 | tf_op jit(solution)/shard_map/ppermute | solution.py:382
  37.3 1.1 collective-permute-start.6
  38.4 3.3 %collective-permute-done.5.refs_2_ = bf16[32,1280]{1,0:T(8,128)(2,1)S(1)} collective-permute-done((bf16[32,1280]{1,0:T(8,128)(2,1)}, bf16[32,1280]{1,0:T(8,128)(2,1)S(1)}, u32[]{:S(2)}, u32[]{:S(2)}) %collective-permute-start.5) | collective-permute-done | bytes 81952 | tf_op jit(solution)/shard_map/ppermute | solution.py:382
  41.7 1.9 %collective-permute-done.6.refs_3_ = bf16[32,1280]{1,0:T(8,128)(2,1)S(1)} collective-permute-done((bf16[32,1280]{1,0:T(8,128)(2,1)}, bf16[32,1280]{1,0:T(8,128)(2,1)S(1)}, u32[]{:S(2)}, u32[]{:S(2)}) %collective-permute-start.6) | collective-permute-done | bytes 81952 | tf_op jit(solution)/shard_map/ppermute | solution.py:382
  43.7 0.6 copy-done.12
  44.3 1.7 choose.1.refs_15_.refs_16_
  46.0 1.6 constant_dynamic-update-slice_fusion.2
  47.6 0.5 collective-permute-start.8
  48.1 2.7 %collective-permute-start.9 = (bf16[304,1280]{1,0:T(8,128)(2,1)}, bf16[304,1280]{1,0:T(8,128)(2,1)}, u32[]{:S(2)}, u32[]{:S(2)}) collective-permute-start(bf16[304,1280]{1,0:T(8,128)(2,1)} %get-tuple-element.84.refs_13_.refs_14_.refs_15_.refs_16_.refs_17_), channel_id=1, source_target_pairs={{0,224},{8,232},{16,240},{24,248},{32,0},{40,8},{48,16},{56,24},{6... | collective-permute-start | bytes 2334728 | tf_op jit(solution)/shard_map/ppermute | solution.py:379
  50.8 1.6 collective-permute-start.12
  52.4 1.7 collective-permute-start.13
  54.0 2.0 %collective-permute-start.14 = (bf16[640,640]{1,0:T(8,128)(2,1)}, bf16[640,640]{1,0:T(8,128)(2,1)S(1)}, u32[]{:S(2)}, u32[]{:S(2)}) collective-permute-start(bf16[640,640]{1,0:T(8,128)(2,1)} %get-tuple-element.93), channel_id=1, source_target_pairs={{0,4},{1,5},{2,6},{3,7},{4,0},{5,1},{6,2},{7,3},{8,12},{9,13},{10,... | collective-permute-start | bytes 2457608 | tf_op jit(solution)/shard_map/ppermute | solution.py:386
  56.0 1.3 pad_maximum_fusion.refs_1_.refs_2_.refs_3_
  57.3 9.8 %attend.4 = (f32[640,1024]{1,0:T(8,128)}, f32[40,1024]{1,0:T(8,128)}, f32[8,128]{1,0:T(8,128)}) custom-call(s32[10]{0:T(128)} %pad_add_fusion.info.refs_0_, bf16[656,1024]{1,0:T(8,128)(2,1)} %pad_maximum_fusion.refs_1_.refs_2_.refs_3_, bf16[656,1024]{1,0:T(8,128)(2,1)} %pad_maximum_fusion.refs_1_.refs_2_.refs_3_, bf16[304,1280]{1,0:T(8,128)(2,1)} %copy-done.4, ...), custom_call_target="tpu_custom_call" | custom-call | flops 17999998976 | bytes 8388608 | tf_op jit(solution)/shard_map/attend/pallas_call | solution.py:213
  67.1 1.5 collective-permute-done.8.refs_3_.refs_4_.refs_5_.refs_6_.refs_7_.refs_13_.refs_14_
  68.6 1.6 collective-permute-start.10
  70.1 1.7 collective-permute-start.11
  71.8 5.9 %attend.5 = (f32[640,1024]{1,0:T(8,128)}, f32[40,1024]{1,0:T(8,128)}, f32[8,128]{1,0:T(8,128)}) custom-call(f32[8,128]{1,0:T(8,128)} %get-tuple-element.94.refs_0_, bf16[656,1024]{1,0:T(8,128)(2,1)} %pad_maximum_fusion.refs_1_.refs_2_.refs_3_, ...), custom_call_target="tpu_custom_call", output_to_operand_aliasing={{0}: (13, {}), {1}: (14, {})} | custom-call | flops 12000000000 | bytes 8388608 | tf_op jit(solution)/shard_map/attend/pallas_call | solution.py:213
  77.8 13.0 %collective-permute-done.14 = bf16[640,640]{1,0:T(8,128)(2,1)S(1)} collective-permute-done((bf16[640,640]{1,0:T(8,128)(2,1)}, bf16[640,640]{1,0:T(8,128)(2,1)S(1)}, u32[]{:S(2)}, u32[]{:S(2)}) %collective-permute-start.14) | collective-permute-done | bytes 819232 | tf_op jit(solution)/shard_map/ppermute | solution.py:386
  90.9 1.4 collective-permute-start.17
  92.2 1.8 %collective-permute-start.15 = (bf16[160,1280]{1,0:T(8,128)(2,1)S(1)}, bf16[160,1280]{1,0:T(8,128)(2,1)}, u32[]{:S(2)}, u32[]{:S(2)}) collective-permute-start(bf16[160,1280]{1,0:T(8,128)(2,1)S(1)} %slice.21), channel_id=1, source_target_pairs={{0,32},{8,40},{16,48},{24,56},{32,64},{40,72},{48,80},{56,88},{64,... | collective-permute-start | bytes 1228808 | tf_op jit(solution)/shard_map/ppermute | solution.py:379
  94.0 1.0 slice.22
  95.1 1.5 collective-permute-start.16
  96.6 5.9 %attend.6 = (f32[640,1024]{1,0:T(8,128)}, f32[40,1024]{1,0:T(8,128)}, f32[8,128]{1,0:T(8,128)}) custom-call(f32[8,128]{1,0:T(8,128)} %get-tuple-element.98.refs_0_, bf16[656,1024]{1,0:T(8,128)(2,1)} %pad_maximum_fusion.refs_1_.refs_2_.refs_3_, ...), custom_call_target="tpu_custom_call", output_to_operand_aliasing={{0}: (13, {}), {1}: (14, {})} | custom-call | flops 12000000000 | bytes 8388608 | tf_op jit(solution)/shard_map/attend/pallas_call | solution.py:213
  102.6 3.8 %collective-permute-done.15.refs_4_.refs_5_.refs_9_.refs_10_ = bf16[160,1280]{1,0:T(8,128)(2,1)} collective-permute-done((bf16[160,1280]{1,0:T(8,128)(2,1)S(1)}, bf16[160,1280]{1,0:T(8,128)(2,1)}, u32[]{:S(2)}, u32[]{:S(2)}) %collective-permute-start.15) | collective-permute-done | bytes 409632 | tf_op jit(solution)/shard_map/ppermute | solution.py:379
  106.4 0.8 copy-done.15
  107.1 8.6 %attend.7 = (bf16[656,512]{1,0:T(8,128)(2,1)}, bf16[656,512]{1,0:T(8,128)(2,1)}) custom-call(s32[10]{0:T(128)} %pad_add_fusion.info.refs_0_, f32[8,128]{1,0:T(8,128)} %get-tuple-element.103.refs_1_, bf16[656,1024]{1,0:T(8,128)(2,1)} %pad_maximum_fusion.refs_1_.refs_2_.refs_3_, bf16[656,1024]{1,0:T(8,128)(2,1)} %pad_maximum_fusion.refs_1_.refs_2_.refs_3_, ...), custom_call_target="tpu_custom_call" | custom-call | flops 12000000000 | bytes 8388608 | tf_op jit(solution)/shard_map/attend/pallas_call | solution.py:213
  115.9 0.5 collective-permute-start.20
  116.5 0.4 collective-permute-start.22
  116.9 1.3 collective-permute-done.18.b_ref
  118.2 0.8 copy-done.5
  119.0 2.5 %merge.2 = (bf16[656,256]{1,0:T(8,128)(2,1)}, bf16[656,256]{1,0:T(8,128)(2,1)}) custom-call(bf16[656,512]{1,0:T(8,128)(2,1)} %get-tuple-element.106.a_ref, bf16[656,512]{1,0:T(8,128)(2,1)} %copy-done.5), custom_call_target="tpu_custom_call" | custom-call | bytes 6291456 | tf_op jit(solution)/shard_map/merge/pallas_call | solution.py:281
  121.5 1.7 %collective-permute-start.19 = (bf16[656,256]{1,0:T(8,128)(2,1)}, bf16[656,256]{1,0:T(8,128)(2,1)}, u32[]{:S(2)}, u32[]{:S(2)}) collective-permute-start(bf16[656,256]{1,0:T(8,128)(2,1)} %get-tuple-element.109), channel_id=1, source_target_pairs={{0,16},{8,24},{16,0},{24,8},{32,48},{40,56},{48,32},{56,40},{64,80... | collective-permute-start | bytes 1007624 | tf_op jit(solution)/shard_map/ppermute | solution.py:382
  123.2 10.0 %collective-permute-done.19.b_ref = bf16[656,256]{1,0:T(8,128)(2,1)} collective-permute-done((bf16[656,256]{1,0:T(8,128)(2,1)}, bf16[656,256]{1,0:T(8,128)(2,1)}, u32[]{:S(2)}, u32[]{:S(2)}) %collective-permute-start.19) | collective-permute-done | bytes 335904 | tf_op jit(solution)/shard_map/ppermute | solution.py:382
  133.2 2.0 %merge.3 = bf16[256,640]{1,0:T(8,128)(2,1)} custom-call(bf16[656,256]{1,0:T(8,128)(2,1)} %get-tuple-element.108.a_ref, bf16[656,256]{1,0:T(8,128)(2,1)} %collective-permute-done.19.b_ref), custom_call_target="tpu_custom_call" | custom-call | bytes 6291456 | tf_op jit(solution)/shard_map/merge/pallas_call | solution.py:281
  135.3 0.8 collective-permute-start.25
  136.1 2.5 %collective-permute-start.24 = (bf16[256,640]{1,0:T(8,128)(2,1)}, bf16[256,640]{1,0:T(8,128)(2,1)S(1)}, u32[]{:S(2)}, u32[]{:S(2)}) collective-permute-start(bf16[256,640]{1,0:T(8,128)(2,1)} %merge.3), channel_id=1, source_target_pairs={{0,6},{1,7},{2,0},{3,1},{4,2},{5,3},{6,4},{7,5},{8,14},{9,15},{10,... | collective-permute-start | bytes 983048 | tf_op jit(solution)/shard_map/ppermute | solution.py:386
  138.5 0.6 collective-permute-start.23
  139.1 1.5 fusion.2
  140.6 0.5 fusion.1
  141.1 11.6 %collective-permute-done.25 = bf16[256,640]{1,0:T(8,128)(2,1)S(1)} collective-permute-done((bf16[256,640]{1,0:T(8,128)(2,1)}, bf16[256,640]{1,0:T(8,128)(2,1)S(1)}, u32[]{:S(2)}, u32[]{:S(2)}) %collective-permute-start.25) | collective-permute-done | bytes 327712 | tf_op jit(solution)/shard_map/ppermute | solution.py:386
  152.7 1.6 fusion.3
  154.3 1.6 fusion.4
  156.0 0.5 fusion.5
  156.6 1.6 fusion.6
  158.3 0.5 fusion.7
  158.7 1.6 select_convert_fusion
  160.4 1.5 collective-permute-start.26
  161.9 5.6 %collective-permute-done.26 = bf16[256,640]{1,0:T(8,128)(2,1)S(1)} collective-permute-done((bf16[256,640]{1,0:T(8,128)(2,1)S(1)}, bf16[256,640]{1,0:T(8,128)(2,1)S(1)}, u32[]{:S(2)}, u32[]{:S(2)}) %collective-permute-start.26) | collective-permute-done | bytes 327712 | tf_op jit(solution)/shard_map/ppermute | solution.py:478
  167.5 0.9 add_convert_fusion
  (69 shorter events, 1.0 us)
Async XLA Ops:
  0.0 10.5 %copy-start.17 = (s32[256]{0:T(256)S(1)}, s32[256]{0:T(256)}, u32[]{:S(2)}) copy-start(s32[256]{0:T(256)} %param.12) | copy-start | bytes 3076
  0.0 10.5 %copy-start.6 = (bf16[256,640]{1,0:T(8,128)(2,1)S(1)}, bf16[256,640]{1,0:T(8,128)(2,1)}, u32[]{:S(2)}) copy-start(bf16[256,640]{1,0:T(8,128)(2,1)} %param.10) | copy-start | bytes 983044
  0.0 10.6 %copy-start.7 = (bf16[256,640]{1,0:T(8,128)(2,1)S(1)}, bf16[256,640]{1,0:T(8,128)(2,1)}, u32[]{:S(2)}) copy-start(bf16[256,640]{1,0:T(8,128)(2,1)} %param.11) | copy-start | bytes 983044
  2.0 29.8 %all-to-all-start = ((bf16[8,32,1280]{2,1,0:T(8,128)(2,1)}), bf16[8,32,1280]{2,1,0:T(8,128)(2,1)S(1)}, u32[]{:S(2)}, u32[]{:S(2)}) async-start(bf16[8,32,1280]{2,1,0:T(8,128)(2,1)} %pad_maximum_fusion.2), calls=%async_computation | async-start | bytes 1310720 | tf_op jit(solution)/shard_map/all_to_all | solution.py:398
  10.6 3.6 %copy-start.8 = (bf16[256,640]{1,0:T(8,128)(2,1)S(1)}, bf16[256,640]{1,0:T(8,128)(2,1)}, u32[]{:S(2)}) copy-start(bf16[256,640]{1,0:T(8,128)(2,1)} %param.9) | copy-start | bytes 983044
  10.7 7.5 %copy-start.13 = (s32[4]{0:T(128)S(1)}, s32[4]{0:T(128)}, u32[]{:S(2)}) copy-start(s32[4]{0:T(128)} %param.16) | copy-start | bytes 52
  10.7 7.5 %copy-start.14 = (s32[4]{0:T(128)S(1)}, s32[4]{0:T(128)}, u32[]{:S(2)}) copy-start(s32[4]{0:T(128)} %param.15) | copy-start | bytes 52
  11.0 14.4 %copy-start.4 = (bf16[304,1280]{1,0:T(8,128)(2,1)}, bf16[304,1280]{1,0:T(8,128)(2,1)S(1)}, u32[]{:S(2)}) copy-start(bf16[304,1280]{1,0:T(8,128)(2,1)S(1)} %pad_maximum_fusion.1.refs_3_.refs_4_.refs_5_.refs_6_.refs_7_) | copy-start | bytes 2334724
  11.0 35.0 %collective-permute-start.7 = (bf16[304,1280]{1,0:T(8,128)(2,1)S(1)}, bf16[304,1280]{1,0:T(8,128)(2,1)}, u32[]{:S(2)}, u32[]{:S(2)}) collective-permute-start(bf16[304,1280]{1,0:T(8,128)(2,1)S(1)} %pad_maximum_fusion.1.refs_3_.refs_4_.refs_5_.refs_6_.refs_7_), channel_id=1, source_target_pairs={{0,224},{8,232},{16,240},{24,248},{32,0},{40,8},{48,16},{56,24},{6... | collective-permute-start | bytes 2334728 | tf_op jit(solution)/shard_map/ppermute | solution.py:379
  14.3 31.7 %collective-permute-start = (bf16[304,1280]{1,0:T(8,128)(2,1)S(1)}, bf16[304,1280]{1,0:T(8,128)(2,1)}, u32[]{:S(2)}, u32[]{:S(2)}) collective-permute-start(bf16[304,1280]{1,0:T(8,128)(2,1)S(1)} %pad_maximum_fusion.1.refs_3_.refs_4_.refs_5_.refs_6_.refs_7_), channel_id=1, source_target_pairs={{0,32},{8,40},{16,48},{24,56},{32,64},{40,72},{48,80},{56,88},{64,... | collective-permute-start | bytes 2334728 | tf_op jit(solution)/shard_map/ppermute | solution.py:379
  14.5 11.7 %collective-permute-start.3 = (bf16[656,256]{1,0:T(8,128)(2,1)S(1)}, bf16[656,256]{1,0:T(8,128)(2,1)S(1)}, u32[]{:S(2)}, u32[]{:S(2)}) collective-permute-start(bf16[656,256]{1,0:T(8,128)(2,1)S(1)} %pad_maximum_fusion.3), channel_id=1, source_target_pairs={{0,24},{8,16},{16,8},{24,0},{32,56},{40,48},{48,40},{56,32},{64,88... | collective-permute-start | bytes 1007624 | tf_op jit(solution)/shard_map/ppermute | solution.py:382
  15.3 10.9 %collective-permute-start.2 = (bf16[656,256]{1,0:T(8,128)(2,1)S(1)}, bf16[656,256]{1,0:T(8,128)(2,1)S(1)}, u32[]{:S(2)}, u32[]{:S(2)}) collective-permute-start(bf16[656,256]{1,0:T(8,128)(2,1)S(1)} %pad_maximum_fusion.3), channel_id=1, source_target_pairs={{0,8},{8,0},{16,24},{24,16},{32,40},{40,32},{48,56},{56,48},{64,72... | collective-permute-start | bytes 1007624 | tf_op jit(solution)/shard_map/ppermute | solution.py:382
  16.8 15.0 %collective-permute-start.1 = (bf16[656,256]{1,0:T(8,128)(2,1)S(1)}, bf16[656,256]{1,0:T(8,128)(2,1)S(1)}, u32[]{:S(2)}, u32[]{:S(2)}) collective-permute-start(bf16[656,256]{1,0:T(8,128)(2,1)S(1)} %pad_maximum_fusion.3), channel_id=1, source_target_pairs={{0,16},{8,24},{16,0},{24,8},{32,48},{40,56},{48,32},{56,40},{64,80... | collective-permute-start | bytes 1007624 | tf_op jit(solution)/shard_map/ppermute | solution.py:382
  31.9 0.8 copy-start.1
  34.6 3.9 %collective-permute-start.4 = (bf16[32,1280]{1,0:T(8,128)(2,1)}, bf16[32,1280]{1,0:T(8,128)(2,1)S(1)}, u32[]{:S(2)}, u32[]{:S(2)}) collective-permute-start(bf16[32,1280]{1,0:T(8,128)(2,1)} %get-tuple-element.74), channel_id=1, source_target_pairs={{0,8},{8,0},{16,24},{24,16},{32,40},{40,32},{48,56},{56,48},{64,72... | collective-permute-start | bytes 245768 | tf_op jit(solution)/shard_map/ppermute | solution.py:382
  35.6 6.2 %collective-permute-start.5 = (bf16[32,1280]{1,0:T(8,128)(2,1)}, bf16[32,1280]{1,0:T(8,128)(2,1)S(1)}, u32[]{:S(2)}, u32[]{:S(2)}) collective-permute-start(bf16[32,1280]{1,0:T(8,128)(2,1)} %get-tuple-element.75), channel_id=1, source_target_pairs={{0,16},{8,24},{16,0},{24,8},{32,48},{40,56},{48,32},{56,40},{64,80... | collective-permute-start | bytes 245768 | tf_op jit(solution)/shard_map/ppermute | solution.py:382
  37.3 6.4 %collective-permute-start.6 = (bf16[32,1280]{1,0:T(8,128)(2,1)}, bf16[32,1280]{1,0:T(8,128)(2,1)S(1)}, u32[]{:S(2)}, u32[]{:S(2)}) collective-permute-start(bf16[32,1280]{1,0:T(8,128)(2,1)} %get-tuple-element.76), channel_id=1, source_target_pairs={{0,24},{8,16},{16,8},{24,0},{32,56},{40,48},{48,40},{56,32},{64,88... | collective-permute-start | bytes 245768 | tf_op jit(solution)/shard_map/ppermute | solution.py:382
  38.4 5.2 %copy-start.10 = (bf16[32,1280]{1,0:T(8,128)(2,1)}, bf16[32,1280]{1,0:T(8,128)(2,1)S(1)}, u32[]{:S(2)}) copy-start(bf16[32,1280]{1,0:T(8,128)(2,1)S(1)} %collective-permute-done.4.refs_1_) | copy-start | bytes 245764
  41.7 1.9 %copy-start.11 = (bf16[32,1280]{1,0:T(8,128)(2,1)}, bf16[32,1280]{1,0:T(8,128)(2,1)S(1)}, u32[]{:S(2)}) copy-start(bf16[32,1280]{1,0:T(8,128)(2,1)S(1)} %collective-permute-done.5.refs_2_) | copy-start | bytes 245764
  43.7 0.6 copy-start.12
  47.6 21.0 %collective-permute-start.8 = (bf16[304,1280]{1,0:T(8,128)(2,1)}, bf16[304,1280]{1,0:T(8,128)(2,1)}, u32[]{:S(2)}, u32[]{:S(2)}) collective-permute-start(bf16[304,1280]{1,0:T(8,128)(2,1)} %get-tuple-element.83.refs_8_.refs_9_.refs_10_.refs_11_.refs_12_), channel_id=1, source_target_pairs={{0,32},{8,40},{16,48},{24,56},{32,64},{40,72},{48,80},{56,88},{64,... | collective-permute-start | bytes 2334728 | tf_op jit(solution)/shard_map/ppermute | solution.py:379
  48.1 20.5 %collective-permute-start.9 = (bf16[304,1280]{1,0:T(8,128)(2,1)}, bf16[304,1280]{1,0:T(8,128)(2,1)}, u32[]{:S(2)}, u32[]{:S(2)}) collective-permute-start(bf16[304,1280]{1,0:T(8,128)(2,1)} %get-tuple-element.84.refs_13_.refs_14_.refs_15_.refs_16_.refs_17_), channel_id=1, source_target_pairs={{0,224},{8,232},{16,240},{24,248},{32,0},{40,8},{48,16},{56,24},{6... | collective-permute-start | bytes 2334728 | tf_op jit(solution)/shard_map/ppermute | solution.py:379
  50.8 26.9 %collective-permute-start.12 = (bf16[640,640]{1,0:T(8,128)(2,1)}, bf16[640,640]{1,0:T(8,128)(2,1)}, u32[]{:S(2)}, u32[]{:S(2)}) collective-permute-start(bf16[640,640]{1,0:T(8,128)(2,1)} %get-tuple-element.91), channel_id=1, source_target_pairs={{0,2},{1,3},{2,4},{3,5},{4,6},{5,7},{6,0},{7,1},{8,10},{9,11},{10,... | collective-permute-start | bytes 2457608 | tf_op jit(solution)/shard_map/ppermute | solution.py:386
  52.4 25.4 %collective-permute-start.13 = (bf16[640,640]{1,0:T(8,128)(2,1)}, bf16[640,640]{1,0:T(8,128)(2,1)S(1)}, u32[]{:S(2)}, u32[]{:S(2)}) collective-permute-start(bf16[640,640]{1,0:T(8,128)(2,1)} %get-tuple-element.92), channel_id=1, source_target_pairs={{0,6},{1,7},{2,0},{3,1},{4,2},{5,3},{6,4},{7,5},{8,14},{9,15},{10,... | collective-permute-start | bytes 2457608 | tf_op jit(solution)/shard_map/ppermute | solution.py:386
  54.0 36.8 %collective-permute-start.14 = (bf16[640,640]{1,0:T(8,128)(2,1)}, bf16[640,640]{1,0:T(8,128)(2,1)S(1)}, u32[]{:S(2)}, u32[]{:S(2)}) collective-permute-start(bf16[640,640]{1,0:T(8,128)(2,1)} %get-tuple-element.93), channel_id=1, source_target_pairs={{0,4},{1,5},{2,6},{3,7},{4,0},{5,1},{6,2},{7,3},{8,12},{9,13},{10,... | collective-permute-start | bytes 2457608 | tf_op jit(solution)/shard_map/ppermute | solution.py:386
  68.6 22.2 %collective-permute-start.10 = (bf16[304,1280]{1,0:T(8,128)(2,1)}, bf16[304,1280]{1,0:T(8,128)(2,1)S(1)}, u32[]{:S(2)}, u32[]{:S(2)}) collective-permute-start(bf16[304,1280]{1,0:T(8,128)(2,1)} %collective-permute-done.8.refs_3_.refs_4_.refs_5_.refs_6_.refs_7_.refs_13_.refs_14_), channel_id=1, source_target_pairs={{0,32},{8,40},{16,48},{24,56},{32,64},{40,72},{48,80},{56,88},{64,... | collective-permute-start | bytes 2334728 | tf_op jit(solution)/shard_map/ppermute | solution.py:379
  70.1 20.7 %collective-permute-start.11 = (bf16[304,1280]{1,0:T(8,128)(2,1)}, bf16[304,1280]{1,0:T(8,128)(2,1)}, u32[]{:S(2)}, u32[]{:S(2)}) collective-permute-start(bf16[304,1280]{1,0:T(8,128)(2,1)} %collective-permute-done.9.refs_8_.refs_9_.refs_10_.refs_11_.refs_12_.refs_17_.refs_18_), channel_id=1, source_target_pairs={{0,224},{8,232},{16,240},{24,248},{32,0},{40,8},{48,16},{56,24},{6... | collective-permute-start | bytes 2334728 | tf_op jit(solution)/shard_map/ppermute | solution.py:379
  90.8 5.8 %copy-start.9 = (bf16[304,1280]{1,0:T(8,128)(2,1)}, bf16[304,1280]{1,0:T(8,128)(2,1)S(1)}, u32[]{:S(2)}) copy-start(bf16[304,1280]{1,0:T(8,128)(2,1)S(1)} %collective-permute-done.10.refs_3_.refs_4_.refs_5_.refs_6_.refs_7_.refs_11_.refs_12_) | copy-start | bytes 2334724
  90.9 11.7 %collective-permute-start.17 = (bf16[32,1280]{1,0:T(8,128)(2,1)S(1)}, bf16[32,1280]{1,0:T(8,128)(2,1)S(1)}, u32[]{:S(2)}, u32[]{:S(2)}) collective-permute-start(bf16[32,1280]{1,0:T(8,128)(2,1)S(1)} %slice.23), channel_id=1, source_target_pairs={{0,64},{8,72},{16,80},{24,88},{32,96},{40,104},{48,112},{56,120},{... | collective-permute-start | bytes 245768 | tf_op jit(solution)/shard_map/ppermute | solution.py:379
  92.2 14.1 %collective-permute-start.15 = (bf16[160,1280]{1,0:T(8,128)(2,1)S(1)}, bf16[160,1280]{1,0:T(8,128)(2,1)}, u32[]{:S(2)}, u32[]{:S(2)}) collective-permute-start(bf16[160,1280]{1,0:T(8,128)(2,1)S(1)} %slice.21), channel_id=1, source_target_pairs={{0,32},{8,40},{16,48},{24,56},{32,64},{40,72},{48,80},{56,88},{64,... | collective-permute-start | bytes 1228808 | tf_op jit(solution)/shard_map/ppermute | solution.py:379
  95.1 11.3 %collective-permute-start.16 = (bf16[176,1280]{1,0:T(8,128)(2,1)S(1)}, bf16[176,1280]{1,0:T(8,128)(2,1)S(1)}, u32[]{:S(2)}, u32[]{:S(2)}) collective-permute-start(bf16[176,1280]{1,0:T(8,128)(2,1)S(1)} %slice.22), channel_id=1, source_target_pairs={{0,224},{8,232},{16,240},{24,248},{32,0},{40,8},{48,16},{56,24},{6... | collective-permute-start | bytes 1351688 | tf_op jit(solution)/shard_map/ppermute | solution.py:379
  102.6 3.8 %copy-start.16 = (bf16[32,1280]{1,0:T(8,128)(2,1)}, bf16[32,1280]{1,0:T(8,128)(2,1)S(1)}, u32[]{:S(2)}) copy-start(bf16[32,1280]{1,0:T(8,128)(2,1)S(1)} %collective-permute-done.17.refs_23_.refs_24_) | copy-start | bytes 245764
  106.3 0.8 copy-start.15
  115.8 23.3 %copy-start.3 = (bf16[640,640]{1,0:T(8,128)(2,1)S(1)}, bf16[640,640]{1,0:T(8,128)(2,1)}, u32[]{:S(2)}) copy-start(bf16[640,640]{1,0:T(8,128)(2,1)} %get-tuple-element.116) | copy-start | bytes 2457604
  115.8 2.4 %collective-permute-start.18 = (bf16[656,512]{1,0:T(8,128)(2,1)}, bf16[656,512]{1,0:T(8,128)(2,1)S(1)}, u32[]{:S(2)}, u32[]{:S(2)}) collective-permute-start(bf16[656,512]{1,0:T(8,128)(2,1)} %get-tuple-element.107), channel_id=1, source_target_pairs={{0,8},{8,0},{16,24},{24,16},{32,40},{40,32},{48,56},{56,48},{64,72... | collective-permute-start | bytes 2015240 | tf_op jit(solution)/shard_map/ppermute | solution.py:382
  115.9 7.3 %collective-permute-start.20 = (bf16[640,640]{1,0:T(8,128)(2,1)}, bf16[640,640]{1,0:T(8,128)(2,1)}, u32[]{:S(2)}, u32[]{:S(2)}) collective-permute-start(bf16[640,640]{1,0:T(8,128)(2,1)} %collective-permute-done.12), channel_id=1, source_target_pairs={{0,8},{8,0},{16,24},{24,16},{32,40},{40,32},{48,56},{56,48},{64,72... | collective-permute-start | bytes 2457608 | tf_op jit(solution)/shard_map/ppermute | solution.py:382
  116.4 6.8 %collective-permute-start.21 = (bf16[640,640]{1,0:T(8,128)(2,1)S(1)}, bf16[640,640]{1,0:T(8,128)(2,1)}, u32[]{:S(2)}, u32[]{:S(2)}) collective-permute-start(bf16[640,640]{1,0:T(8,128)(2,1)S(1)} %collective-permute-done.14), channel_id=1, source_target_pairs={{0,8},{8,0},{16,24},{24,16},{32,40},{40,32},{48,56},{56,48},{64,72... | collective-permute-start | bytes 2457608 | tf_op jit(solution)/shard_map/ppermute | solution.py:382
  116.5 6.7 %collective-permute-start.22 = (bf16[640,640]{1,0:T(8,128)(2,1)S(1)}, bf16[640,640]{1,0:T(8,128)(2,1)}, u32[]{:S(2)}, u32[]{:S(2)}) collective-permute-start(bf16[640,640]{1,0:T(8,128)(2,1)S(1)} %collective-permute-done.13), channel_id=1, source_target_pairs={{0,8},{8,0},{16,24},{24,16},{32,40},{40,32},{48,56},{56,48},{64,72... | collective-permute-start | bytes 2457608 | tf_op jit(solution)/shard_map/ppermute | solution.py:382
  118.2 0.8 copy-start.5
  121.5 19.1 %copy-start.2 = (bf16[640,640]{1,0:T(8,128)(2,1)S(1)}, bf16[640,640]{1,0:T(8,128)(2,1)}, u32[]{:S(2)}) copy-start(bf16[640,640]{1,0:T(8,128)(2,1)} %get-tuple-element.115) | copy-start | bytes 2457604
  121.5 11.7 %collective-permute-start.19 = (bf16[656,256]{1,0:T(8,128)(2,1)}, bf16[656,256]{1,0:T(8,128)(2,1)}, u32[]{:S(2)}, u32[]{:S(2)}) collective-permute-start(bf16[656,256]{1,0:T(8,128)(2,1)} %get-tuple-element.109), channel_id=1, source_target_pairs={{0,16},{8,24},{16,0},{24,8},{32,48},{40,56},{48,32},{56,40},{64,80... | collective-permute-start | bytes 1007624 | tf_op jit(solution)/shard_map/ppermute | solution.py:382
  135.3 5.3 %copy-start = (bf16[256,640]{1,0:T(8,128)(2,1)S(1)}, bf16[256,640]{1,0:T(8,128)(2,1)}, u32[]{:S(2)}) copy-start(bf16[256,640]{1,0:T(8,128)(2,1)} %merge.3) | copy-start | bytes 983044
  135.3 17.4 %collective-permute-start.25 = (bf16[256,640]{1,0:T(8,128)(2,1)}, bf16[256,640]{1,0:T(8,128)(2,1)S(1)}, u32[]{:S(2)}, u32[]{:S(2)}) collective-permute-start(bf16[256,640]{1,0:T(8,128)(2,1)} %merge.3), channel_id=1, source_target_pairs={{0,2},{1,3},{2,4},{3,5},{4,6},{5,7},{6,0},{7,1},{8,10},{9,11},{10,... | collective-permute-start | bytes 983048 | tf_op jit(solution)/shard_map/ppermute | solution.py:386
  136.1 20.0 %collective-permute-start.24 = (bf16[256,640]{1,0:T(8,128)(2,1)}, bf16[256,640]{1,0:T(8,128)(2,1)S(1)}, u32[]{:S(2)}, u32[]{:S(2)}) collective-permute-start(bf16[256,640]{1,0:T(8,128)(2,1)} %merge.3), channel_id=1, source_target_pairs={{0,6},{1,7},{2,0},{3,1},{4,2},{5,3},{6,4},{7,5},{8,14},{9,15},{10,... | collective-permute-start | bytes 983048 | tf_op jit(solution)/shard_map/ppermute | solution.py:386
  138.5 19.7 %collective-permute-start.23 = (bf16[256,640]{1,0:T(8,128)(2,1)}, bf16[256,640]{1,0:T(8,128)(2,1)S(1)}, u32[]{:S(2)}, u32[]{:S(2)}) collective-permute-start(bf16[256,640]{1,0:T(8,128)(2,1)} %merge.3), channel_id=1, source_target_pairs={{0,4},{1,5},{2,6},{3,7},{4,0},{5,1},{6,2},{7,3},{8,12},{9,13},{10,... | collective-permute-start | bytes 983048 | tf_op jit(solution)/shard_map/ppermute | solution.py:386
  160.4 7.2 %collective-permute-start.26 = (bf16[256,640]{1,0:T(8,128)(2,1)S(1)}, bf16[256,640]{1,0:T(8,128)(2,1)S(1)}, u32[]{:S(2)}, u32[]{:S(2)}) collective-permute-start(bf16[256,640]{1,0:T(8,128)(2,1)S(1)} %get-tuple-element.133), channel_id=1, source_target_pairs={{0,1},{1,0},{2,3},{3,2},{4,5},{5,4},{6,7},{7,6},{8,9},{9,8},{10,11... | collective-permute-start | bytes 983048 | tf_op jit(solution)/shard_map/ppermute | solution.py:478

commit v2 on v1

--- a/solution.py
+++ b/solution.py
@@ -47,6 +47,7 @@
         levels = refs.pop(0)
 
     head = pl.program_id(0)
+    span = query_ref.shape[1]
     lane = 128
     factor = scaled_exponent()
 
@@ -56,14 +57,14 @@
             if mark_ref is None:
                 live = ctx_info[4 + jnp.bitwise_and(ctx_info[8], 3)]
                 limits[index, 0:1, :] = jnp.full(
-                    (1, 4 * rows), live.astype(jnp.float32), jnp.float32
+                    (1, span), live.astype(jnp.float32), jnp.float32
                 )
                 bounds[index] = jnp.int32(1)
                 continue
             frame = lax.broadcasted_iota(jnp.int32, (FRAMES, rows), 0).astype(jnp.float32)
             key_marks = mark_ref[0:1, 0:rows].astype(jnp.float32)
             below = jnp.sum((key_marks <= frame).astype(jnp.float32), axis=1, keepdims=True)
-            frame = lax.broadcasted_iota(jnp.int32, (FRAMES, 4 * rows), 0).astype(jnp.float32)
+            frame = lax.broadcasted_iota(jnp.int32, (FRAMES, span), 0).astype(jnp.float32)
             marks = query_marks[0:1, :].astype(jnp.float32)
             most = jnp.sum(jnp.where(marks == frame, below, 0.0), axis=0, keepdims=True)
             limits[index, 0:1, :] = most
@@ -83,7 +84,7 @@
             jnp.concatenate([ref[begin : begin + count] for _, ref, begin, count in segments]).T
             for segments, _ in chunks
         ]
-        for tile in range(4 * rows // lane):
+        for tile in range(span // lane):
             spot = slice(tile * lane, (tile + 1) * lane)
             query = query_ref[:, spot]
             if first:
@@ -110,7 +111,7 @@
                 stat_out[1:2, spot] = total
                 acc_out[:, spot] = acc
                 continue
-            out_ref, begin = (keep_out, 0) if tile * lane < 2 * rows else (send_out, 2 * rows)
+            out_ref, begin = (keep_out, 0) if tile * lane < rows else (send_out, rows)
             out_spot = slice(tile * lane - begin, (tile + 1) * lane - begin)
             out_ref[pl.ds(pl.multiple_of(head * DH, DH), DH), out_spot] = (
                 acc * (1.0 / total)
@@ -144,15 +145,16 @@
         @pl.when(head == head_count - 1)
         def _():
             feat = head_count * DH
-            keep_out[feat : feat + 16, :] = stats[:, 0 : 2 * rows].astype(jnp.bfloat16)
-            send_out[feat : feat + 16, :] = stats[:, 2 * rows : 4 * rows].astype(jnp.bfloat16)
-
-
-def attention_call(queries, chunks, state, ctx_info, last, token):
+            keep_out[feat : feat + 16, :] = stats[:, :rows].astype(jnp.bfloat16)
+            send_out[feat : feat + 16, :] = stats[:, rows:].astype(jnp.bfloat16)
+
+
+def attention_call(queries, chunks, state, ctx_info, last, token, side=0):
     feat = queries.shape[0] - 16
     rows = queries.shape[1] // 4
     head_count = feat // DH
     first = state is None
+    span = (2 if last else 4) * rows
     with_ctx = ctx_info is not None
     operands, specs = [], []
     if with_ctx:
@@ -160,8 +162,8 @@
         specs.append(pl.BlockSpec(memory_space=pltpu.SMEM))
     operands += [token, queries, queries]
     specs.append(pl.BlockSpec(memory_space=pl.ANY))
-    specs.append(pl.BlockSpec((DH, 4 * rows), lambda h: (h, 0)))
-    specs.append(pl.BlockSpec((16, 4 * rows), lambda h: (feat // 16, 0)))
+    specs.append(pl.BlockSpec((DH, span), lambda h: (h, side)))
+    specs.append(pl.BlockSpec((16, span), lambda h: (feat // 16, side)))
     layout = []
     for segments, marks in chunks:
         places = []
@@ -183,8 +185,8 @@
             )
     aliases = {}
     state_specs = [
-        pl.BlockSpec((DH, 4 * rows), lambda h: (h, 0)),
-        pl.BlockSpec((8, 4 * rows), lambda h: (h, 0)),
+        pl.BlockSpec((DH, span), lambda h: (h, side)),
+        pl.BlockSpec((8, span), lambda h: (h, side)),
     ]
     if not first:
         if not last:
@@ -192,23 +194,23 @@
         operands.extend(state)
         specs.extend(state_specs)
     if last:
-        out_shape = [jax.ShapeDtypeStruct((feat + 16, 2 * rows), jnp.bfloat16)] * 2
-        out_specs = [pl.BlockSpec((feat + 16, 2 * rows), lambda h: (0, 0))] * 2
+        out_shape = [jax.ShapeDtypeStruct((feat + 16, rows), jnp.bfloat16)] * 2
+        out_specs = [pl.BlockSpec((feat + 16, rows), lambda h: (0, 0))] * 2
     else:
         out_shape = [
-            jax.ShapeDtypeStruct((feat, 4 * rows), jnp.float32),
-            jax.ShapeDtypeStruct((8 * head_count, 4 * rows), jnp.float32),
+            jax.ShapeDtypeStruct((feat, span), jnp.float32),
+            jax.ShapeDtypeStruct((8 * head_count, span), jnp.float32),
             jax.ShapeDtypeStruct((8, 128), jnp.float32),
         ]
         out_specs = state_specs + [pl.BlockSpec((8, 128), lambda h: (0, 0))]
     scratch = [
-        pltpu.VMEM((len(chunks), 8, 4 * rows), jnp.float32),
+        pltpu.VMEM((len(chunks), 8, span), jnp.float32),
         pltpu.SMEM((len(chunks),), jnp.int32),
     ]
     if last:
         scratch += [
-            pltpu.VMEM((16, 4 * rows), jnp.float32),
-            pltpu.VMEM((8, 4 * rows), jnp.float32),
+            pltpu.VMEM((16, span), jnp.float32),
+            pltpu.VMEM((8, span), jnp.float32),
         ]
     return pl.pallas_call(
         functools.partial(
@@ -221,72 +223,63 @@
         scratch_shapes=scratch,
         input_output_aliases=aliases,
         cost_estimate=pl.CostEstimate(
-            flops=len(chunks) * 6 * 10**9, bytes_accessed=8 << 20, transcendentals=0
+            flops=len(chunks) * span * 6 * 10**6, bytes_accessed=8 << 20, transcendentals=0
         ),
         compiler_params=pltpu.CompilerParams(vmem_limit_bytes=VMEM),
         name="attend",
     )(*operands)
 
 
-def merge_kernel(head_count, turned, a_ref, b_ref, out_ref, *rest):
+def merge_kernel(head_count, turned, *refs):
+    *in_refs, out_ref = refs
     feat = head_count * DH
-    rows = a_ref.shape[1]
-    a_stats = a_ref[feat : feat + 16, :].astype(jnp.float32)
-    b_stats = b_ref[feat : feat + 16, :].astype(jnp.float32)
+    rows = in_refs[0].shape[1]
+    stats = [ref[feat : feat + 16, :].astype(jnp.float32) for ref in in_refs]
     pieces = [[], [], []]
     for head in range(head_count):
         levels = [
             s[head : head + 1]
             + s[head_count + head : head_count + head + 1]
             + s[2 * head_count + head : 2 * head_count + head + 1]
-            for s in (a_stats, b_stats)
-        ]
-        top = jnp.maximum(levels[0], levels[1])
-        a_weight = jnp.exp2(levels[0] - top)
-        b_weight = jnp.exp2(levels[1] - top)
-        total = a_weight + b_weight
+            for s in stats
+        ]
+        top = functools.reduce(jnp.maximum, levels)
+        shares = [jnp.exp2(level - top) for level in levels]
+        total = sum(shares)
         inverse = 1.0 / total
         span = slice(head * DH, (head + 1) * DH)
-        mixed = a_ref[span, :].astype(jnp.float32) * (a_weight * inverse) + b_ref[span, :].astype(
-            jnp.float32
-        ) * (b_weight * inverse)
+        mixed = sum(
+            ref[span, :].astype(jnp.float32) * (share * inverse)
+            for ref, share in zip(in_refs, shares)
+        )
         if turned:
             out_ref[:, span] = mixed.T.astype(jnp.bfloat16)
         else:
-            half = rows // 2
-            out_ref[span, :] = mixed[:, :half].astype(jnp.bfloat16)
-            rest[0][span, :] = mixed[:, half:].astype(jnp.bfloat16)
+            out_ref[span, :] = mixed.astype(jnp.bfloat16)
             level = top + jnp.log2(total)
             for part in range(3):
                 piece = level.astype(jnp.bfloat16).astype(jnp.float32)
                 pieces[part].append(piece)
                 level = level - piece
     if not turned:
-        stats = jnp.concatenate(
+        out_ref[feat : feat + 16, :] = jnp.concatenate(
             pieces[0] + pieces[1] + pieces[2] + [jnp.zeros((1, rows), jnp.float32)], axis=0
         ).astype(jnp.bfloat16)
-        out_ref[feat : feat + 16, :] = stats[:, :half]
-        rest[0][feat : feat + 16, :] = stats[:, half:]
-
-
-def merge_call(a, b, turned):
-    feat = a.shape[0] - 16
-    rows = a.shape[1]
-    if turned:
-        out_shape = jax.ShapeDtypeStruct((rows, feat), jnp.bfloat16)
-        out_specs = pl.BlockSpec(memory_space=pltpu.VMEM)
-    else:
-        out_shape = [jax.ShapeDtypeStruct((feat + 16, rows // 2), jnp.bfloat16)] * 2
-        out_specs = [pl.BlockSpec(memory_space=pltpu.VMEM)] * 2
+
+
+def merge_call(parts, turned):
+    feat = parts[0].shape[0] - 16
+    rows = parts[0].shape[1]
+    shape = (rows, feat) if turned else (feat + 16, rows)
     return pl.pallas_call(
         functools.partial(merge_kernel, feat // DH, turned),
-        in_specs=[pl.BlockSpec(memory_space=pltpu.VMEM)] * 2,
-        out_specs=out_specs,
-        out_shape=out_shape,
+        in_specs=[pl.BlockSpec(memory_space=pltpu.VMEM)] * len(parts),
+        out_specs=pl.BlockSpec(memory_space=pltpu.VMEM),
+        out_shape=jax.ShapeDtypeStruct(shape, jnp.bfloat16),
         compiler_params=pltpu.CompilerParams(vmem_limit_bytes=VMEM),
-        cost_estimate=pl.CostEstimate(flops=0, bytes_accessed=6 << 20, transcendentals=0),
+        cost_estimate=pl.CostEstimate(flops=0, bytes_accessed=1 << 10, transcendentals=0),
         name="merge",
-    )(a, b)
+    )(*parts)
 
 
 def columns_kernel(ring, info, in_ref, *out_refs):
@@ -394,11 +387,11 @@
     slot = jnp.concatenate([ctx_keys[0], ctx_values[0]], axis=1).reshape(depth, part, 2 * feat)
 
     ahead, behind = shift(own, 1), shift(own, -1)
-    query_x, query_core, query_both = swap(query_own, 2), swap(query_own, 1), swap(query_own, 3)
+    query_x, query_core = swap(query_own, 2), swap(query_own, 1)
     pieces = lax.all_to_all(slot, "blk", 0, 0, axis_index_groups=columns)
     slabs = column_blocks(out_weight, info, feat, ring_y)
-    pieces, query_x, query_core, query_both, *slabs = lax.optimization_barrier(
-        (pieces, query_x, query_core, query_both, *slabs)
+    pieces, query_x, query_core, *slabs = lax.optimization_barrier(
+        (pieces, query_x, query_core, *slabs)
     )
     offers = list(offer_pieces(pieces, info))
     offers = offers[:1] + [swap(offers[mask], mask) for mask in range(1, plane)]
@@ -414,12 +407,11 @@
         return item, mid, part
 
     slab_own, slab_core = slabs[0], slabs[ring_y]
-    *first, query_x, query_core, query_both, slab_near, slab_far, slab_back = (
-        lax.optimization_barrier(
-            (loaded(ahead), loaded(behind), query_x, query_core, query_both, *slabs[1:ring_y])
-        )
-    )
-    query_plane = jnp.concatenate([query_own, query_x, query_core, query_both], axis=1)
+    *first, query_x, query_core, slab_near, slab_far, slab_back = lax.optimization_barrier(
+        (loaded(ahead), loaded(behind), query_x, query_core, *slabs[1:ring_y])
+    )
+    query_both = swap(query_x, 1)
+    query_plane = jnp.concatenate([query_x, query_both, query_own, query_core], axis=1)
     ahead, behind = shift(first[0], 1), shift(first[1], -1)
     *state, token = attention_call(
         query_plane, [halves(item) for item in (own, *first)], None, None, False, info
@@ -453,13 +445,16 @@
         (far_behind, 0, part),
         (opposite, 0, part),
     ]
-    keep, send = attention_call(query_plane, [far, (ctx, None)], state, info, True, token)
-    received = swap(send, 1)
-    own, other = merge_call(keep, received, False)
+    finish = [far, (ctx, None)]
+    keep, send = attention_call(query_plane, finish, state, info, True, token, 0)
+    other = merge_call([keep, swap(send, 1)], False)
+    other, token = lax.optimization_barrier((other, token))
+    keep, send = attention_call(query_plane, finish, state, info, True, token, 1)
     own_slabs = [slab_own, slab_near, slab_far, slab_back]
     core_slabs = [slab_core] + [swap(item, 1) for item in own_slabs[1:]]
     received, *core_slabs = lax.optimization_barrier((swap(other, 2), *core_slabs))
-    attended = merge_call(own, received, True)
+    own = merge_call([keep, received], False)
+    attended = merge_call([own, swap(send, 1)], True)
 
     def dots(block, step):
         return [

time: 170 us -> 167 us (0.982)
  waiting for transfers between devices: 58.6 us -> 52.2 us
  Pallas kernels: 44.8 us -> 51 us
  starting transfers between devices: 43.9 us -> 41.3 us
    ppermute x11 -> x12, waiting for transfers between devices: 23 us -> 11.2 us  [swap(): return lax.ppermute(item, 'blk', [(i, i ^ mask) for i in range(blk_count)])]
    pallas_call x4 -> x5, Pallas kernels: 30.3 us -> 34.9 us  [attention_call(): pl.pallas_call(functools.partial(attention_kernel, layout, first, last, w...]
    all_to_all x1, waiting for transfers between devices: 0.01 us -> 4.19 us  [shards(): pieces = lax.all_to_all(slot, 'blk', 0, 0, axis_index_groups=columns)]
    pallas_call x2 -> x3, Pallas kernels: 4.5 us -> 6.12 us  [merge_call(): pl.pallas_call(functools.partial(merge_kernel, feat // DH, turned), in_sp...]
    ppermute x11 -> x12, starting transfers between devices: 10.4 us -> 8.99 us  [swap(): return lax.ppermute(item, 'blk', [(i, i ^ mask) for i in range(blk_count)])]
  transfers between devices with their start and end apart: 28 -> 29, of which waited for: 11 -> 12; matrix products, arithmetic and copies ran while one was open for 7% -> 7% of each run, Pallas kernels for 20% -> 26%
where the time goes in v2:
time: 167 us; the launch traced here: 165 us
  waiting for transfers between devices  52.2 us (31%)
  Pallas kernels  51 us (31%)
  starting transfers between devices  41.3 us (25%)
  matrix products  8.11 us (5%)
  other arithmetic  6.41 us (4%)
  local copies, waits for them, and re-layouts  5.96 us (4%)
    pallas_call x5, Pallas kernels, attention_call(): pl.pallas_call(functools.partial(attention_kernel, layout, first, last, w...  34.9 us
    ppermute x6, waiting for transfers between devices, shift_y(): return lax.ppermute(item, 'heads', steps)  24.8 us
    ppermute x9, starting transfers between devices, shift(): return lax.ppermute(item, 'blk', steps)  14 us
    ppermute x12, waiting for transfers between devices, swap(): return lax.ppermute(item, 'blk', [(i, i ^ mask) for i in range(blk_count)])  11.2 us
    ppermute x12, starting transfers between devices, swap(): return lax.ppermute(item, 'blk', [(i, i ^ mask) for i in range(blk_count)])  8.99 us
    ppermute x6, starting transfers between devices, shift_y(): return lax.ppermute(item, 'heads', steps)  8.89 us
    all_to_all x1, starting transfers between devices, shards(): pieces = lax.all_to_all(slot, 'blk', 0, 0, axis_index_groups=columns)  8.47 us
    dot_general x8, matrix products, dots(): jnp.dot(block, item[step], preferred_element_type=jnp.float32)  8.11 us
  transfers between devices with their start and end apart: 29, of which 12 were waited for; matrix products, arithmetic and copies ran while one was open for 7% of the time, Pallas kernels for 26%

profile of v2, /device:TPU:2, one launch (start us, length us, event | category | flops | bytes accessed | tf_op | source)
XLA Modules:
  0.0 165.4 jit_solution(4263163543643246945)
XLA Ops:
  0.0 2.1 %pad_maximum_fusion.2 = bf16[8,32,1280]{2,1,0:T(8,128)(2,1)} fusion(bf16[8,32,640]{2,1,0:T(8,128)(2,1)} %bitcast.23, bf16[8,32,640]{2,1,0:T(8,128)(2,1)} %bitcast.24), kind=kLoop, calls=%fused_computation.2 | loop fusion | flops 1310720 | bytes 1310720 | tf_op jit(solution)/shard_map/concatenate | solution.py:387
  2.1 8.5 %all-to-all-start = ((bf16[8,32,1280]{2,1,0:T(8,128)(2,1)}), bf16[8,32,1280]{2,1,0:T(8,128)(2,1)S(1)}, u32[]{:S(2)}, u32[]{:S(2)}) async-start(bf16[8,32,1280]{2,1,0:T(8,128)(2,1)} %pad_maximum_fusion.2), calls=%async_computation | async-start | bytes 1310720 | tf_op jit(solution)/shard_map/all_to_all | solution.py:391
  10.8 0.2 pad_maximum_fusion.1.refs_3_.refs_4_.refs_5_.refs_6_.refs_7_
  11.0 3.3 %collective-permute-start.6 = (bf16[304,1280]{1,0:T(8,128)(2,1)S(1)}, bf16[304,1280]{1,0:T(8,128)(2,1)}, u32[]{:S(2)}, u32[]{:S(2)}) collective-permute-start(bf16[304,1280]{1,0:T(8,128)(2,1)S(1)} %pad_maximum_fusion.1.refs_3_.refs_4_.refs_5_.refs_6_.refs_7_), channel_id=1, source_target_pairs={{0,224},{8,232},{16,240},{24,248},{32,0},{40,8},{48,16},{56,24},{6... | collective-permute-start | bytes 2334728 | tf_op jit(solution)/shard_map/ppermute | solution.py:372
  14.7 2.2 %collective-permute-start.1 = (bf16[656,256]{1,0:T(8,128)(2,1)S(1)}, bf16[656,256]{1,0:T(8,128)(2,1)}, u32[]{:S(2)}, u32[]{:S(2)}) collective-permute-start(bf16[656,256]{1,0:T(8,128)(2,1)S(1)} %pad_maximum_fusion.3), channel_id=1, source_target_pairs={{0,16},{8,24},{16,0},{24,8},{32,48},{40,56},{48,32},{56,40},{64,80... | collective-permute-start | bytes 1007624 | tf_op jit(solution)/shard_map/ppermute | solution.py:375
  16.9 0.6 pad_add_fusion.info.refs_0_
  17.5 6.4 %columns.1 = (bf16[640,640]{1,0:T(8,128)(2,1)}, bf16[640,640]{1,0:T(8,128)(2,1)}, bf16[640,640]{1,0:T(8,128)(2,1)}, bf16[640,640]{1,0:T(8,128)(2,1)}, bf16[640,640]{1,0:T(8,128)(2,1)}) custom-call(s32[10]{0:T(128)} %pad_add_fusion.info.refs_0_, bf16[640,5120]{1,0:T(8,128)(2,1)} %in_ref.1), custom_call_target="tpu_custom_call" | custom-call | bytes 8192000 | tf_op jit(solution)/shard_map/columns/pallas_call | solution.py:297
  24.0 2.6 %collective-permute-done.1 = bf16[656,256]{1,0:T(8,128)(2,1)} collective-permute-done((bf16[656,256]{1,0:T(8,128)(2,1)S(1)}, bf16[656,256]{1,0:T(8,128)(2,1)}, u32[]{:S(2)}, u32[]{:S(2)}) %collective-permute-start.1) | collective-permute-done | bytes 335904 | tf_op jit(solution)/shard_map/ppermute | solution.py:375
  26.6 4.2 %all-to-all-done.in_ref = bf16[8,32,1280]{2,1,0:T(8,128)(2,1)S(1)} async-done(((bf16[8,32,1280]{2,1,0:T(8,128)(2,1)}), bf16[8,32,1280]{2,1,0:T(8,128)(2,1)S(1)}, u32[]{:S(2)}, u32[]{:S(2)}) %all-to-all-start) | async-done | bytes 655392 | tf_op jit(solution)/shard_map/all_to_all | solution.py:391
  30.8 0.9 copy-done.1
  31.7 1.8 %offer.1 = (bf16[32,1280]{1,0:T(8,128)(2,1)}, bf16[32,1280]{1,0:T(8,128)(2,1)}, bf16[32,1280]{1,0:T(8,128)(2,1)}, bf16[32,1280]{1,0:T(8,128)(2,1)}) custom-call(s32[10]{0:T(128)} %pad_add_fusion.info.refs_0_, bf16[8,32,1280]{2,1,0:T(8,128)(2,1)} %copy-done.1), custom_call_target="tpu_custom_call" | custom-call | tf_op jit(solution)/shard_map/offer/pallas_call | solution.py:321
  33.5 2.1 %collective-permute-start.4 = (bf16[32,1280]{1,0:T(8,128)(2,1)}, bf16[32,1280]{1,0:T(8,128)(2,1)S(1)}, u32[]{:S(2)}, u32[]{:S(2)}) collective-permute-start(bf16[32,1280]{1,0:T(8,128)(2,1)} %get-tuple-element.75), channel_id=1, source_target_pairs={{0,16},{8,24},{16,0},{24,8},{32,48},{40,56},{48,32},{56,40},{64,80... | collective-permute-start | bytes 245768 | tf_op jit(solution)/shard_map/ppermute | solution.py:375
  35.7 1.2 collective-permute-start.5
  36.9 3.2 %collective-permute-done.4.refs_2_ = bf16[32,1280]{1,0:T(8,128)(2,1)S(1)} collective-permute-done((bf16[32,1280]{1,0:T(8,128)(2,1)}, bf16[32,1280]{1,0:T(8,128)(2,1)S(1)}, u32[]{:S(2)}, u32[]{:S(2)}) %collective-permute-start.4) | collective-permute-done | bytes 81952 | tf_op jit(solution)/shard_map/ppermute | solution.py:375
  40.1 1.7 %collective-permute-done.5.refs_3_ = bf16[32,1280]{1,0:T(8,128)(2,1)S(1)} collective-permute-done((bf16[32,1280]{1,0:T(8,128)(2,1)}, bf16[32,1280]{1,0:T(8,128)(2,1)S(1)}, u32[]{:S(2)}, u32[]{:S(2)}) %collective-permute-start.5) | collective-permute-done | bytes 81952 | tf_op jit(solution)/shard_map/ppermute | solution.py:375
  41.8 0.6 copy-done.12
  42.4 1.7 %choose.1.refs_15_.refs_16_ = bf16[32,1280]{1,0:T(8,128)(2,1)} custom-call(s32[10]{0:T(128)} %pad_add_fusion.info.refs_0_, bf16[32,1280]{1,0:T(8,128)(2,1)} %get-tuple-element.73.refs_0_, bf16[32,1280]{1,0:T(8,128)(2,1)} %copy-done.10, bf16[32,1280]{1,0:T(8,128)(2,1)} %copy-done.11, bf16[32,1280]{1,0:T(8,128)(2,1)} %copy-done.12), custom_call_target="tpu_custom_call" | custom-call | tf_op jit(solution)/shard_map/choose/pallas_call | solution.py:346
  44.1 0.9 collective-permute-done
  45.0 1.6 constant_dynamic-update-slice_fusion.2
  46.5 1.3 collective-permute-start.7
  47.9 1.9 %collective-permute-start.8 = (bf16[304,1280]{1,0:T(8,128)(2,1)}, bf16[304,1280]{1,0:T(8,128)(2,1)}, u32[]{:S(2)}, u32[]{:S(2)}) collective-permute-start(bf16[304,1280]{1,0:T(8,128)(2,1)} %get-tuple-element.83.refs_13_.refs_14_.refs_15_.refs_16_.refs_17_), channel_id=1, source_target_pairs={{0,224},{8,232},{16,240},{24,248},{32,0},{40,8},{48,16},{56,24},{6... | collective-permute-start | bytes 2334728 | tf_op jit(solution)/shard_map/ppermute | solution.py:372
  49.8 1.6 collective-permute-start.12
  51.3 1.7 %collective-permute-start.13 = (bf16[640,640]{1,0:T(8,128)(2,1)}, bf16[640,640]{1,0:T(8,128)(2,1)S(1)}, u32[]{:S(2)}, u32[]{:S(2)}) collective-permute-start(bf16[640,640]{1,0:T(8,128)(2,1)} %get-tuple-element.90), channel_id=1, source_target_pairs={{0,6},{1,7},{2,0},{3,1},{4,2},{5,3},{6,4},{7,5},{8,14},{9,15},{10,... | collective-permute-start | bytes 2457608 | tf_op jit(solution)/shard_map/ppermute | solution.py:379
  53.0 2.0 %collective-permute-start.14 = (bf16[640,640]{1,0:T(8,128)(2,1)}, bf16[640,640]{1,0:T(8,128)(2,1)S(1)}, u32[]{:S(2)}, u32[]{:S(2)}) collective-permute-start(bf16[640,640]{1,0:T(8,128)(2,1)} %get-tuple-element.91), channel_id=1, source_target_pairs={{0,4},{1,5},{2,6},{3,7},{4,0},{5,1},{6,2},{7,3},{8,12},{9,13},{10,... | collective-permute-start | bytes 2457608 | tf_op jit(solution)/shard_map/ppermute | solution.py:379
  55.0 2.3 %pad_maximum_fusion.refs_1_.refs_2_.refs_3_ = bf16[656,1024]{1,0:T(8,128)(2,1)} fusion(bf16[656,256]{1,0:T(8,128)(2,1)} %collective-permute-done.2, bf16[16,256]{1,0:T(8,128)(2,1)S(1)} %pad_slice_fusion, bf16[640,256]{1,0:T(8,128)(2,1)S(1)} %bitcast.22, bf16[656,256]{1,0:T(8,128)(2,1)S(1)} %collective-permute-done.9, bf16[656,256]{1,0:T(8,128)(2,1)} %collective-permute-done.1), kind=kLoop, calls=%fused_computation | loop fusion | flops 6717440 | bytes 2686976 | tf_op jit(solution)/shard_map/concatenate | solution.py:414
  57.3 9.8 %attend.5 = (f32[640,1024]{1,0:T(8,128)}, f32[40,1024]{1,0:T(8,128)}, f32[8,128]{1,0:T(8,128)}) custom-call(s32[10]{0:T(128)} %pad_add_fusion.info.refs_0_, bf16[656,1024]{1,0:T(8,128)(2,1)} %pad_maximum_fusion.refs_1_.refs_2_.refs_3_, bf16[656,1024]{1,0:T(8,128)(2,1)} %pad_maximum_fusion.refs_1_.refs_2_.refs_3_, bf16[304,1280]{1,0:T(8,128)(2,1)} %copy-done.4, ...), custom_call_target="tpu_custom_call" | custom-call | flops 18432000000 | bytes 8388608 | tf_op jit(solution)/shard_map/attend/pallas_call | solution.py:215
  67.1 0.7 collective-permute-done.7.refs_3_.refs_4_.refs_5_.refs_6_.refs_7_.refs_13_.refs_14_
  67.8 1.2 collective-permute-start.10
  69.0 2.1 %collective-permute-start.11 = (bf16[304,1280]{1,0:T(8,128)(2,1)}, bf16[304,1280]{1,0:T(8,128)(2,1)}, u32[]{:S(2)}, u32[]{:S(2)}) collective-permute-start(bf16[304,1280]{1,0:T(8,128)(2,1)} %collective-permute-done.8.refs_8_.refs_9_.refs_10_.refs_11_.refs_12_.refs_17_.refs_18_), channel_id=1, source_target_pairs={{0,224},{8,232},{16,240},{24,248},{32,0},{40,8},{48,16},{56,24},{6... | collective-permute-start | bytes 2334728 | tf_op jit(solution)/shard_map/ppermute | solution.py:372
  71.1 5.9 %attend.6 = (f32[640,1024]{1,0:T(8,128)}, f32[40,1024]{1,0:T(8,128)}, f32[8,128]{1,0:T(8,128)}) custom-call(f32[8,128]{1,0:T(8,128)} %get-tuple-element.92.refs_0_, bf16[656,1024]{1,0:T(8,128)(2,1)} %pad_maximum_fusion.refs_1_.refs_2_.refs_3_, ...), custom_call_target="tpu_custom_call", output_to_operand_aliasing={{0}: (13, {}), {1}: (14, {})} | custom-call | flops 12288000000 | bytes 8388608 | tf_op jit(solution)/shard_map/attend/pallas_call | solution.py:215
  77.0 13.0 %collective-permute-done.14 = bf16[640,640]{1,0:T(8,128)(2,1)S(1)} collective-permute-done((bf16[640,640]{1,0:T(8,128)(2,1)}, bf16[640,640]{1,0:T(8,128)(2,1)S(1)}, u32[]{:S(2)}, u32[]{:S(2)}) %collective-permute-start.14) | collective-permute-done | bytes 819232 | tf_op jit(solution)/shard_map/ppermute | solution.py:379
  90.1 0.7 slice.23
  90.8 0.9 collective-permute-start.17
  91.8 1.7 %collective-permute-start.15 = (bf16[160,1280]{1,0:T(8,128)(2,1)S(1)}, bf16[160,1280]{1,0:T(8,128)(2,1)}, u32[]{:S(2)}, u32[]{:S(2)}) collective-permute-start(bf16[160,1280]{1,0:T(8,128)(2,1)S(1)} %slice.21), channel_id=1, source_target_pairs={{0,32},{8,40},{16,48},{24,56},{32,64},{40,72},{48,80},{56,88},{64,... | collective-permute-start | bytes 1228808 | tf_op jit(solution)/shard_map/ppermute | solution.py:372
  93.5 1.0 slice.22
  94.6 1.6 collective-permute-start.16
  96.1 6.0 %attend.7 = (f32[640,1024]{1,0:T(8,128)}, f32[40,1024]{1,0:T(8,128)}, f32[8,128]{1,0:T(8,128)}) custom-call(f32[8,128]{1,0:T(8,128)} %get-tuple-element.96.refs_0_, bf16[656,1024]{1,0:T(8,128)(2,1)} %pad_maximum_fusion.refs_1_.refs_2_.refs_3_, ...), custom_call_target="tpu_custom_call", output_to_operand_aliasing={{0}: (13, {}), {1}: (14, {})} | custom-call | flops 12288000000 | bytes 8388608 | tf_op jit(solution)/shard_map/attend/pallas_call | solution.py:215
  102.1 4.1 %collective-permute-done.15.refs_4_.refs_5_.refs_9_.refs_10_ = bf16[160,1280]{1,0:T(8,128)(2,1)} collective-permute-done((bf16[160,1280]{1,0:T(8,128)(2,1)S(1)}, bf16[160,1280]{1,0:T(8,128)(2,1)}, u32[]{:S(2)}, u32[]{:S(2)}) %collective-permute-start.15) | collective-permute-done | bytes 409632 | tf_op jit(solution)/shard_map/ppermute | solution.py:372
  106.2 6.7 %attend.8 = (bf16[656,256]{1,0:T(8,128)(2,1)}, bf16[656,256]{1,0:T(8,128)(2,1)}) custom-call(s32[10]{0:T(128)} %pad_add_fusion.info.refs_0_, f32[8,128]{1,0:T(8,128)} %get-tuple-element.106.refs_1_, bf16[656,1024]{1,0:T(8,128)(2,1)} %pad_maximum_fusion.refs_1_.refs_2_.refs_3_, bf16[656,1024]{1,0:T(8,128)(2,1)} %pad_maximum_fusion.refs_1_.refs_2_.refs_3_, ...), custom_call_target="tpu_custom_call" | custom-call | flops 6144000000 | bytes 8388608 | tf_op jit(solution)/shard_map/attend/pallas_call | solution.py:215
  113.0 0.5 collective-permute-start.20
  113.6 0.4 collective-permute-start.22
  114.0 0.8 collective-permute-done.18.refs_1_
  114.8 0.7 copy-done.5
  115.5 2.0 %merge.3 = bf16[656,256]{1,0:T(8,128)(2,1)} custom-call(bf16[656,256]{1,0:T(8,128)(2,1)} %get-tuple-element.104.refs_0_, bf16[656,256]{1,0:T(8,128)(2,1)} %copy-done.5), custom_call_target="tpu_custom_call" | custom-call | bytes 1024 | tf_op jit(solution)/shard_map/merge/pallas_call | solution.py:274
  117.6 2.1 %collective-permute-start.19 = (bf16[656,256]{1,0:T(8,128)(2,1)}, bf16[656,256]{1,0:T(8,128)(2,1)}, u32[]{:S(2)}, u32[]{:S(2)}) collective-permute-start(bf16[656,256]{1,0:T(8,128)(2,1)} %merge.3), channel_id=1, source_target_pairs={{0,16},{8,24},{16,0},{24,8},{32,48},{40,56},{48,32},{56,40},{64,80... | collective-permute-start | bytes 1007624 | tf_op jit(solution)/shard_map/ppermute | solution.py:375
  119.7 6.6 %attend.9 = (bf16[656,256]{1,0:T(8,128)(2,1)}, bf16[656,256]{1,0:T(8,128)(2,1)}) custom-call(s32[10]{0:T(128)} %pad_add_fusion.info.refs_0_, f32[8,128]{1,0:T(8,128)} %get-tuple-element.106.refs_1_, bf16[656,1024]{1,0:T(8,128)(2,1)} %pad_maximum_fusion.refs_1_.refs_2_.refs_3_, bf16[656,1024]{1,0:T(8,128)(2,1)} %pad_maximum_fusion.refs_1_.refs_2_.refs_3_, ...), custom_call_target="tpu_custom_call" | custom-call | flops 6144000000 | bytes 8388608 | tf_op jit(solution)/shard_map/attend/pallas_call | solution.py:215
  126.5 2.8 %collective-permute-done.19.refs_1_ = bf16[656,256]{1,0:T(8,128)(2,1)} collective-permute-done((bf16[656,256]{1,0:T(8,128)(2,1)}, bf16[656,256]{1,0:T(8,128)(2,1)}, u32[]{:S(2)}, u32[]{:S(2)}) %collective-permute-start.19) | collective-permute-done | bytes 335904 | tf_op jit(solution)/shard_map/ppermute | solution.py:375
  129.3 2.0 %merge.4.refs_0_ = bf16[656,256]{1,0:T(8,128)(2,1)} custom-call(bf16[656,256]{1,0:T(8,128)(2,1)} %get-tuple-element.107.refs_0_, bf16[656,256]{1,0:T(8,128)(2,1)} %collective-permute-done.19.refs_1_), custom_call_target="tpu_custom_call" | custom-call | bytes 1024 | tf_op jit(solution)/shard_map/merge/pallas_call | solution.py:274
  131.3 2.1 %merge.5 = bf16[256,640]{1,0:T(8,128)(2,1)} custom-call(bf16[656,256]{1,0:T(8,128)(2,1)} %merge.4.refs_0_, bf16[656,256]{1,0:T(8,128)(2,1)} %collective-permute-done.23.refs_1_), custom_call_target="tpu_custom_call" | custom-call | bytes 1024 | tf_op jit(solution)/shard_map/merge/pallas_call | solution.py:274
  133.4 0.8 collective-permute-start.26
  134.2 2.4 %collective-permute-start.25 = (bf16[256,640]{1,0:T(8,128)(2,1)}, bf16[256,640]{1,0:T(8,128)(2,1)S(1)}, u32[]{:S(2)}, u32[]{:S(2)}) collective-permute-start(bf16[256,640]{1,0:T(8,128)(2,1)} %merge.5), channel_id=1, source_target_pairs={{0,6},{1,7},{2,0},{3,1},{4,2},{5,3},{6,4},{7,5},{8,14},{9,15},{10,... | collective-permute-start | bytes 983048 | tf_op jit(solution)/shard_map/ppermute | solution.py:379
  136.7 0.4 collective-permute-start.24
  137.1 1.5 fusion.2
  138.6 0.5 fusion.1
  139.1 11.7 %collective-permute-done.26 = bf16[256,640]{1,0:T(8,128)(2,1)S(1)} collective-permute-done((bf16[256,640]{1,0:T(8,128)(2,1)}, bf16[256,640]{1,0:T(8,128)(2,1)S(1)}, u32[]{:S(2)}, u32[]{:S(2)}) %collective-permute-start.26) | collective-permute-done | bytes 327712 | tf_op jit(solution)/shard_map/ppermute | solution.py:379
  150.8 0.5 fusion.3
  151.3 1.6 fusion.4
  153.0 0.5 fusion.5
  153.6 1.6 fusion.6
  155.3 0.5 fusion.7
  155.7 1.6 select_convert_fusion
  157.4 0.9 collective-permute-start.27
  158.3 6.2 %collective-permute-done.27 = bf16[256,640]{1,0:T(8,128)(2,1)S(1)} collective-permute-done((bf16[256,640]{1,0:T(8,128)(2,1)S(1)}, bf16[256,640]{1,0:T(8,128)(2,1)S(1)}, u32[]{:S(2)}, u32[]{:S(2)}) %collective-permute-start.27) | collective-permute-done | bytes 327712 | tf_op jit(solution)/shard_map/ppermute | solution.py:473
  164.5 0.9 add_convert_fusion
  (69 shorter events, 1.2 us)
Async XLA Ops:
  0.0 10.6 %copy-start.15 = (s32[256]{0:T(256)S(1)}, s32[256]{0:T(256)}, u32[]{:S(2)}) copy-start(s32[256]{0:T(256)} %param.12) | copy-start | bytes 3076
  0.0 10.6 %copy-start.6 = (bf16[256,640]{1,0:T(8,128)(2,1)S(1)}, bf16[256,640]{1,0:T(8,128)(2,1)}, u32[]{:S(2)}) copy-start(bf16[256,640]{1,0:T(8,128)(2,1)} %param.10) | copy-start | bytes 983044
  0.0 10.6 %copy-start.7 = (bf16[256,640]{1,0:T(8,128)(2,1)S(1)}, bf16[256,640]{1,0:T(8,128)(2,1)}, u32[]{:S(2)}) copy-start(bf16[256,640]{1,0:T(8,128)(2,1)} %param.11) | copy-start | bytes 983044
  2.1 28.7 %all-to-all-start = ((bf16[8,32,1280]{2,1,0:T(8,128)(2,1)}), bf16[8,32,1280]{2,1,0:T(8,128)(2,1)S(1)}, u32[]{:S(2)}, u32[]{:S(2)}) async-start(bf16[8,32,1280]{2,1,0:T(8,128)(2,1)} %pad_maximum_fusion.2), calls=%async_computation | async-start | bytes 1310720 | tf_op jit(solution)/shard_map/all_to_all | solution.py:391
  10.7 3.6 %copy-start.8 = (bf16[256,640]{1,0:T(8,128)(2,1)S(1)}, bf16[256,640]{1,0:T(8,128)(2,1)}, u32[]{:S(2)}) copy-start(bf16[256,640]{1,0:T(8,128)(2,1)} %param.9) | copy-start | bytes 983044
  10.8 6.1 %copy-start.13 = (s32[4]{0:T(128)S(1)}, s32[4]{0:T(128)}, u32[]{:S(2)}) copy-start(s32[4]{0:T(128)} %param.16) | copy-start | bytes 52
  10.8 6.1 %copy-start.14 = (s32[4]{0:T(128)S(1)}, s32[4]{0:T(128)}, u32[]{:S(2)}) copy-start(s32[4]{0:T(128)} %param.15) | copy-start | bytes 52
  11.0 12.9 %copy-start.4 = (bf16[304,1280]{1,0:T(8,128)(2,1)}, bf16[304,1280]{1,0:T(8,128)(2,1)S(1)}, u32[]{:S(2)}) copy-start(bf16[304,1280]{1,0:T(8,128)(2,1)S(1)} %pad_maximum_fusion.1.refs_3_.refs_4_.refs_5_.refs_6_.refs_7_) | copy-start | bytes 2334724
  11.0 33.1 %collective-permute-start.6 = (bf16[304,1280]{1,0:T(8,128)(2,1)S(1)}, bf16[304,1280]{1,0:T(8,128)(2,1)}, u32[]{:S(2)}, u32[]{:S(2)}) collective-permute-start(bf16[304,1280]{1,0:T(8,128)(2,1)S(1)} %pad_maximum_fusion.1.refs_3_.refs_4_.refs_5_.refs_6_.refs_7_), channel_id=1, source_target_pairs={{0,224},{8,232},{16,240},{24,248},{32,0},{40,8},{48,16},{56,24},{6... | collective-permute-start | bytes 2334728 | tf_op jit(solution)/shard_map/ppermute | solution.py:372
  14.3 30.6 %collective-permute-start = (bf16[304,1280]{1,0:T(8,128)(2,1)S(1)}, bf16[304,1280]{1,0:T(8,128)(2,1)}, u32[]{:S(2)}, u32[]{:S(2)}) collective-permute-start(bf16[304,1280]{1,0:T(8,128)(2,1)S(1)} %pad_maximum_fusion.1.refs_3_.refs_4_.refs_5_.refs_6_.refs_7_), channel_id=1, source_target_pairs={{0,32},{8,40},{16,48},{24,56},{32,64},{40,72},{48,80},{56,88},{64,... | collective-permute-start | bytes 2334728 | tf_op jit(solution)/shard_map/ppermute | solution.py:372
  14.6 9.4 %collective-permute-start.2 = (bf16[656,256]{1,0:T(8,128)(2,1)S(1)}, bf16[656,256]{1,0:T(8,128)(2,1)}, u32[]{:S(2)}, u32[]{:S(2)}) collective-permute-start(bf16[656,256]{1,0:T(8,128)(2,1)S(1)} %pad_maximum_fusion.3), channel_id=1, source_target_pairs={{0,8},{8,0},{16,24},{24,16},{32,40},{40,32},{48,56},{56,48},{64,72... | collective-permute-start | bytes 1007624 | tf_op jit(solution)/shard_map/ppermute | solution.py:375
  14.7 11.9 %collective-permute-start.1 = (bf16[656,256]{1,0:T(8,128)(2,1)S(1)}, bf16[656,256]{1,0:T(8,128)(2,1)}, u32[]{:S(2)}, u32[]{:S(2)}) collective-permute-start(bf16[656,256]{1,0:T(8,128)(2,1)S(1)} %pad_maximum_fusion.3), channel_id=1, source_target_pairs={{0,16},{8,24},{16,0},{24,8},{32,48},{40,56},{48,32},{56,40},{64,80... | collective-permute-start | bytes 1007624 | tf_op jit(solution)/shard_map/ppermute | solution.py:375
  30.8 0.9 copy-start.1
  33.5 3.4 %collective-permute-start.3 = (bf16[32,1280]{1,0:T(8,128)(2,1)}, bf16[32,1280]{1,0:T(8,128)(2,1)S(1)}, u32[]{:S(2)}, u32[]{:S(2)}) collective-permute-start(bf16[32,1280]{1,0:T(8,128)(2,1)} %get-tuple-element.74), channel_id=1, source_target_pairs={{0,8},{8,0},{16,24},{24,16},{32,40},{40,32},{48,56},{56,48},{64,72... | collective-permute-start | bytes 245768 | tf_op jit(solution)/shard_map/ppermute | solution.py:375
  33.5 6.6 %collective-permute-start.4 = (bf16[32,1280]{1,0:T(8,128)(2,1)}, bf16[32,1280]{1,0:T(8,128)(2,1)S(1)}, u32[]{:S(2)}, u32[]{:S(2)}) collective-permute-start(bf16[32,1280]{1,0:T(8,128)(2,1)} %get-tuple-element.75), channel_id=1, source_target_pairs={{0,16},{8,24},{16,0},{24,8},{32,48},{40,56},{48,32},{56,40},{64,80... | collective-permute-start | bytes 245768 | tf_op jit(solution)/shard_map/ppermute | solution.py:375
  35.7 6.1 %collective-permute-start.5 = (bf16[32,1280]{1,0:T(8,128)(2,1)}, bf16[32,1280]{1,0:T(8,128)(2,1)S(1)}, u32[]{:S(2)}, u32[]{:S(2)}) collective-permute-start(bf16[32,1280]{1,0:T(8,128)(2,1)} %get-tuple-element.76), channel_id=1, source_target_pairs={{0,24},{8,16},{16,8},{24,0},{32,56},{40,48},{48,40},{56,32},{64,88... | collective-permute-start | bytes 245768 | tf_op jit(solution)/shard_map/ppermute | solution.py:375
  36.9 4.9 %copy-start.10 = (bf16[32,1280]{1,0:T(8,128)(2,1)}, bf16[32,1280]{1,0:T(8,128)(2,1)S(1)}, u32[]{:S(2)}) copy-start(bf16[32,1280]{1,0:T(8,128)(2,1)S(1)} %collective-permute-done.3.refs_1_) | copy-start | bytes 245764
  40.1 1.7 %copy-start.11 = (bf16[32,1280]{1,0:T(8,128)(2,1)}, bf16[32,1280]{1,0:T(8,128)(2,1)S(1)}, u32[]{:S(2)}) copy-start(bf16[32,1280]{1,0:T(8,128)(2,1)S(1)} %collective-permute-done.4.refs_2_) | copy-start | bytes 245764
  41.8 0.6 copy-start.12
  46.5 6.5 %collective-permute-start.9 = (bf16[656,256]{1,0:T(8,128)(2,1)}, bf16[656,256]{1,0:T(8,128)(2,1)S(1)}, u32[]{:S(2)}, u32[]{:S(2)}) collective-permute-start(bf16[656,256]{1,0:T(8,128)(2,1)} %collective-permute-done.1), channel_id=1, source_target_pairs={{0,8},{8,0},{16,24},{24,16},{32,40},{40,32},{48,56},{56,48},{64,72... | collective-permute-start | bytes 1007624 | tf_op jit(solution)/shard_map/ppermute | solution.py:375
  46.5 21.3 %collective-permute-start.7 = (bf16[304,1280]{1,0:T(8,128)(2,1)}, bf16[304,1280]{1,0:T(8,128)(2,1)}, u32[]{:S(2)}, u32[]{:S(2)}) collective-permute-start(bf16[304,1280]{1,0:T(8,128)(2,1)} %get-tuple-element.82.refs_8_.refs_9_.refs_10_.refs_11_.refs_12_), channel_id=1, source_target_pairs={{0,32},{8,40},{16,48},{24,56},{32,64},{40,72},{48,80},{56,88},{64,... | collective-permute-start | bytes 2334728 | tf_op jit(solution)/shard_map/ppermute | solution.py:372
  47.9 20.0 %collective-permute-start.8 = (bf16[304,1280]{1,0:T(8,128)(2,1)}, bf16[304,1280]{1,0:T(8,128)(2,1)}, u32[]{:S(2)}, u32[]{:S(2)}) collective-permute-start(bf16[304,1280]{1,0:T(8,128)(2,1)} %get-tuple-element.83.refs_13_.refs_14_.refs_15_.refs_16_.refs_17_), channel_id=1, source_target_pairs={{0,224},{8,232},{16,240},{24,248},{32,0},{40,8},{48,16},{56,24},{6... | collective-permute-start | bytes 2334728 | tf_op jit(solution)/shard_map/ppermute | solution.py:372
  49.8 27.2 %collective-permute-start.12 = (bf16[640,640]{1,0:T(8,128)(2,1)}, bf16[640,640]{1,0:T(8,128)(2,1)S(1)}, u32[]{:S(2)}, u32[]{:S(2)}) collective-permute-start(bf16[640,640]{1,0:T(8,128)(2,1)} %get-tuple-element.89), channel_id=1, source_target_pairs={{0,2},{1,3},{2,4},{3,5},{4,6},{5,7},{6,0},{7,1},{8,10},{9,11},{10,... | collective-permute-start | bytes 2457608 | tf_op jit(solution)/shard_map/ppermute | solution.py:379
  51.3 25.7 %collective-permute-start.13 = (bf16[640,640]{1,0:T(8,128)(2,1)}, bf16[640,640]{1,0:T(8,128)(2,1)S(1)}, u32[]{:S(2)}, u32[]{:S(2)}) collective-permute-start(bf16[640,640]{1,0:T(8,128)(2,1)} %get-tuple-element.90), channel_id=1, source_target_pairs={{0,6},{1,7},{2,0},{3,1},{4,2},{5,3},{6,4},{7,5},{8,14},{9,15},{10,... | collective-permute-start | bytes 2457608 | tf_op jit(solution)/shard_map/ppermute | solution.py:379
  53.0 37.1 %collective-permute-start.14 = (bf16[640,640]{1,0:T(8,128)(2,1)}, bf16[640,640]{1,0:T(8,128)(2,1)S(1)}, u32[]{:S(2)}, u32[]{:S(2)}) collective-permute-start(bf16[640,640]{1,0:T(8,128)(2,1)} %get-tuple-element.91), channel_id=1, source_target_pairs={{0,4},{1,5},{2,6},{3,7},{4,0},{5,1},{6,2},{7,3},{8,12},{9,13},{10,... | collective-permute-start | bytes 2457608 | tf_op jit(solution)/shard_map/ppermute | solution.py:379
  67.8 22.2 %collective-permute-start.10 = (bf16[304,1280]{1,0:T(8,128)(2,1)}, bf16[304,1280]{1,0:T(8,128)(2,1)S(1)}, u32[]{:S(2)}, u32[]{:S(2)}) collective-permute-start(bf16[304,1280]{1,0:T(8,128)(2,1)} %collective-permute-done.7.refs_3_.refs_4_.refs_5_.refs_6_.refs_7_.refs_13_.refs_14_), channel_id=1, source_target_pairs={{0,32},{8,40},{16,48},{24,56},{32,64},{40,72},{48,80},{56,88},{64,... | collective-permute-start | bytes 2334728 | tf_op jit(solution)/shard_map/ppermute | solution.py:372
  69.0 21.1 %collective-permute-start.11 = (bf16[304,1280]{1,0:T(8,128)(2,1)}, bf16[304,1280]{1,0:T(8,128)(2,1)}, u32[]{:S(2)}, u32[]{:S(2)}) collective-permute-start(bf16[304,1280]{1,0:T(8,128)(2,1)} %collective-permute-done.8.refs_8_.refs_9_.refs_10_.refs_11_.refs_12_.refs_17_.refs_18_), channel_id=1, source_target_pairs={{0,224},{8,232},{16,240},{24,248},{32,0},{40,8},{48,16},{56,24},{6... | collective-permute-start | bytes 2334728 | tf_op jit(solution)/shard_map/ppermute | solution.py:372
  90.1 6.0 %copy-start.9 = (bf16[304,1280]{1,0:T(8,128)(2,1)}, bf16[304,1280]{1,0:T(8,128)(2,1)S(1)}, u32[]{:S(2)}) copy-start(bf16[304,1280]{1,0:T(8,128)(2,1)S(1)} %collective-permute-done.10.refs_3_.refs_4_.refs_5_.refs_6_.refs_7_.refs_11_.refs_12_) | copy-start | bytes 2334724
  90.8 11.3 %collective-permute-start.17 = (bf16[32,1280]{1,0:T(8,128)(2,1)}, bf16[32,1280]{1,0:T(8,128)(2,1)}, u32[]{:S(2)}, u32[]{:S(2)}) collective-permute-start(bf16[32,1280]{1,0:T(8,128)(2,1)} %slice.23), channel_id=1, source_target_pairs={{0,64},{8,72},{16,80},{24,88},{32,96},{40,104},{48,112},{56,120},{... | collective-permute-start | bytes 245768 | tf_op jit(solution)/shard_map/ppermute | solution.py:372
  91.8 14.4 %collective-permute-start.15 = (bf16[160,1280]{1,0:T(8,128)(2,1)S(1)}, bf16[160,1280]{1,0:T(8,128)(2,1)}, u32[]{:S(2)}, u32[]{:S(2)}) collective-permute-start(bf16[160,1280]{1,0:T(8,128)(2,1)S(1)} %slice.21), channel_id=1, source_target_pairs={{0,32},{8,40},{16,48},{24,56},{32,64},{40,72},{48,80},{56,88},{64,... | collective-permute-start | bytes 1228808 | tf_op jit(solution)/shard_map/ppermute | solution.py:372
  94.6 11.7 %collective-permute-start.16 = (bf16[176,1280]{1,0:T(8,128)(2,1)S(1)}, bf16[176,1280]{1,0:T(8,128)(2,1)}, u32[]{:S(2)}, u32[]{:S(2)}) collective-permute-start(bf16[176,1280]{1,0:T(8,128)(2,1)S(1)} %slice.22), channel_id=1, source_target_pairs={{0,224},{8,232},{16,240},{24,248},{32,0},{40,8},{48,16},{56,24},{6... | collective-permute-start | bytes 1351688 | tf_op jit(solution)/shard_map/ppermute | solution.py:372
  112.9 1.9 %collective-permute-start.18 = (bf16[656,256]{1,0:T(8,128)(2,1)}, bf16[656,256]{1,0:T(8,128)(2,1)S(1)}, u32[]{:S(2)}, u32[]{:S(2)}) collective-permute-start(bf16[656,256]{1,0:T(8,128)(2,1)} %get-tuple-element.105), channel_id=1, source_target_pairs={{0,8},{8,0},{16,24},{24,16},{32,40},{40,32},{48,56},{56,48},{64,72... | collective-permute-start | bytes 1007624 | tf_op jit(solution)/shard_map/ppermute | solution.py:375
  113.0 13.5 %collective-permute-start.20 = (bf16[640,640]{1,0:T(8,128)(2,1)S(1)}, bf16[640,640]{1,0:T(8,128)(2,1)}, u32[]{:S(2)}, u32[]{:S(2)}) collective-permute-start(bf16[640,640]{1,0:T(8,128)(2,1)S(1)} %collective-permute-done.12), channel_id=1, source_target_pairs={{0,8},{8,0},{16,24},{24,16},{32,40},{40,32},{48,56},{56,48},{64,72... | collective-permute-start | bytes 2457608 | tf_op jit(solution)/shard_map/ppermute | solution.py:375
  113.5 13.0 %collective-permute-start.21 = (bf16[640,640]{1,0:T(8,128)(2,1)S(1)}, bf16[640,640]{1,0:T(8,128)(2,1)}, u32[]{:S(2)}, u32[]{:S(2)}) collective-permute-start(bf16[640,640]{1,0:T(8,128)(2,1)S(1)} %collective-permute-done.14), channel_id=1, source_target_pairs={{0,8},{8,0},{16,24},{24,16},{32,40},{40,32},{48,56},{56,48},{64,72... | collective-permute-start | bytes 2457608 | tf_op jit(solution)/shard_map/ppermute | solution.py:375
  113.6 12.9 %collective-permute-start.22 = (bf16[640,640]{1,0:T(8,128)(2,1)S(1)}, bf16[640,640]{1,0:T(8,128)(2,1)}, u32[]{:S(2)}, u32[]{:S(2)}) collective-permute-start(bf16[640,640]{1,0:T(8,128)(2,1)S(1)} %collective-permute-done.13), channel_id=1, source_target_pairs={{0,8},{8,0},{16,24},{24,16},{32,40},{40,32},{48,56},{56,48},{64,72... | collective-permute-start | bytes 2457608 | tf_op jit(solution)/shard_map/ppermute | solution.py:375
  114.8 0.7 copy-start.5
  117.6 11.7 %collective-permute-start.19 = (bf16[656,256]{1,0:T(8,128)(2,1)}, bf16[656,256]{1,0:T(8,128)(2,1)}, u32[]{:S(2)}, u32[]{:S(2)}) collective-permute-start(bf16[656,256]{1,0:T(8,128)(2,1)} %merge.3), channel_id=1, source_target_pairs={{0,16},{8,24},{16,0},{24,8},{32,48},{40,56},{48,32},{56,40},{64,80... | collective-permute-start | bytes 1007624 | tf_op jit(solution)/shard_map/ppermute | solution.py:375
  126.3 10.8 %copy-start.3 = (bf16[640,640]{1,0:T(8,128)(2,1)S(1)}, bf16[640,640]{1,0:T(8,128)(2,1)}, u32[]{:S(2)}) copy-start(bf16[640,640]{1,0:T(8,128)(2,1)} %get-tuple-element.116) | copy-start | bytes 2457604
  126.3 5.0 %collective-permute-start.23 = (bf16[656,256]{1,0:T(8,128)(2,1)}, bf16[656,256]{1,0:T(8,128)(2,1)}, u32[]{:S(2)}, u32[]{:S(2)}) collective-permute-start(bf16[656,256]{1,0:T(8,128)(2,1)} %get-tuple-element.114), channel_id=1, source_target_pairs={{0,8},{8,0},{16,24},{24,16},{32,40},{40,32},{48,56},{56,48},{64,72... | collective-permute-start | bytes 1007624 | tf_op jit(solution)/shard_map/ppermute | solution.py:375
  131.3 7.3 %copy-start.2 = (bf16[640,640]{1,0:T(8,128)(2,1)S(1)}, bf16[640,640]{1,0:T(8,128)(2,1)}, u32[]{:S(2)}) copy-start(bf16[640,640]{1,0:T(8,128)(2,1)} %get-tuple-element.115) | copy-start | bytes 2457604
  133.4 5.2 %copy-start = (bf16[256,640]{1,0:T(8,128)(2,1)S(1)}, bf16[256,640]{1,0:T(8,128)(2,1)}, u32[]{:S(2)}) copy-start(bf16[256,640]{1,0:T(8,128)(2,1)} %merge.5) | copy-start | bytes 983044
  133.4 17.4 %collective-permute-start.26 = (bf16[256,640]{1,0:T(8,128)(2,1)}, bf16[256,640]{1,0:T(8,128)(2,1)S(1)}, u32[]{:S(2)}, u32[]{:S(2)}) collective-permute-start(bf16[256,640]{1,0:T(8,128)(2,1)} %merge.5), channel_id=1, source_target_pairs={{0,2},{1,3},{2,4},{3,5},{4,6},{5,7},{6,0},{7,1},{8,10},{9,11},{10,... | collective-permute-start | bytes 983048 | tf_op jit(solution)/shard_map/ppermute | solution.py:379
  134.2 18.8 %collective-permute-start.25 = (bf16[256,640]{1,0:T(8,128)(2,1)}, bf16[256,640]{1,0:T(8,128)(2,1)S(1)}, u32[]{:S(2)}, u32[]{:S(2)}) collective-permute-start(bf16[256,640]{1,0:T(8,128)(2,1)} %merge.5), channel_id=1, source_target_pairs={{0,6},{1,7},{2,0},{3,1},{4,2},{5,3},{6,4},{7,5},{8,14},{9,15},{10,... | collective-permute-start | bytes 983048 | tf_op jit(solution)/shard_map/ppermute | solution.py:379
  136.7 18.6 %collective-permute-start.24 = (bf16[256,640]{1,0:T(8,128)(2,1)}, bf16[256,640]{1,0:T(8,128)(2,1)S(1)}, u32[]{:S(2)}, u32[]{:S(2)}) collective-permute-start(bf16[256,640]{1,0:T(8,128)(2,1)} %merge.5), channel_id=1, source_target_pairs={{0,4},{1,5},{2,6},{3,7},{4,0},{5,1},{6,2},{7,3},{8,12},{9,13},{10,... | collective-permute-start | bytes 983048 | tf_op jit(solution)/shard_map/ppermute | solution.py:379
  157.4 7.2 %collective-permute-start.27 = (bf16[256,640]{1,0:T(8,128)(2,1)S(1)}, bf16[256,640]{1,0:T(8,128)(2,1)S(1)}, u32[]{:S(2)}, u32[]{:S(2)}) collective-permute-start(bf16[256,640]{1,0:T(8,128)(2,1)S(1)} %get-tuple-element.133), channel_id=1, source_target_pairs={{0,1},{1,0},{2,3},{3,2},{4,5},{5,4},{6,7},{7,6},{8,9},{9,8},{10,11... | collective-permute-start | bytes 983048 | tf_op jit(solution)/shard_map/ppermute | solution.py:473

commit v3 on v2

--- a/solution.py
+++ b/solution.py
@@ -19,17 +19,14 @@
     return DH ** (-0.5) * math.log2(math.e)
 
 
-def attention_kernel(layout, first, last, with_ctx, head_count, rows, *refs):
+def attention_kernel(array_count, layout, first, last, with_ctx, head_count, rows, *refs):
     refs = list(refs)
     ctx_info = refs.pop(0) if with_ctx else None
     refs.pop(0)
     query_ref = refs.pop(0)
     query_marks = refs.pop(0)
-    chunks = []
-    for segments, marked in layout:
-        keys = [(refs.pop(0), refs.pop(0), begin, count) for begin, count in segments]
-        chunks.append((keys, refs.pop(0) if marked else None))
-    chunk_count = len(chunks)
+    arrays = [refs.pop(0) for _ in range(array_count)]
+    chunk_count = len(layout)
     if not first:
         acc_in = refs.pop(0)
         stat_in = refs.pop(0)
@@ -44,17 +41,17 @@
     bounds = refs.pop(0)
     if last:
         stats = refs.pop(0)
-        levels = refs.pop(0)
-
-    head = pl.program_id(0)
+
+    step = pl.program_id(0)
+    heads = range(head_count) if last else [step]
     span = query_ref.shape[1]
     lane = 128
     factor = scaled_exponent()
 
-    @pl.when(head == 0)
+    @pl.when(step == 0)
     def _():
-        for index, (_, mark_ref) in enumerate(chunks):
-            if mark_ref is None:
+        for index, (_, mark) in enumerate(layout):
+            if mark is None:
                 live = ctx_info[4 + jnp.bitwise_and(ctx_info[8], 3)]
                 limits[index, 0:1, :] = jnp.full(
                     (1, span), live.astype(jnp.float32), jnp.float32
@@ -62,7 +59,8 @@
                 bounds[index] = jnp.int32(1)
                 continue
             frame = lax.broadcasted_iota(jnp.int32, (FRAMES, rows), 0).astype(jnp.float32)
-            key_marks = mark_ref[0:1, 0:rows].astype(jnp.float32)
+            marks_at, mark_row = mark
+            key_marks = arrays[marks_at][mark_row : mark_row + 16, 0:rows][0:1].astype(jnp.float32)
             below = jnp.sum((key_marks <= frame).astype(jnp.float32), axis=1, keepdims=True)
             frame = lax.broadcasted_iota(jnp.int32, (FRAMES, span), 0).astype(jnp.float32)
             marks = query_marks[0:1, :].astype(jnp.float32)
@@ -70,29 +68,36 @@
             limits[index, 0:1, :] = most
             bounds[index] = jnp.max(most).astype(jnp.int32)
 
-    def update():
+    def update(head, at):
+        query_rows, stat_rows = slice(at * DH, (at + 1) * DH), at * 8
         row = lax.broadcasted_iota(jnp.int32, (rows, lane), 0)
         places = [row.astype(jnp.float32)] * chunk_count
         if with_ctx:
             start = (lax.shift_right_logical(ctx_info[8], 2) + 5) * (rows // 8)
             places[-1] = jnp.bitwise_and(row + start, rows - 1).astype(jnp.float32)
-        keys = [
-            jnp.concatenate([ref[begin : begin + count] for ref, _, begin, count in segments])
-            for segments, _ in chunks
-        ]
-        turned = [
-            jnp.concatenate([ref[begin : begin + count] for _, ref, begin, count in segments]).T
-            for segments, _ in chunks
-        ]
+
+        def joined(segments, column):
+            begin_lane = (column + head) * DH
+            if not last:
+                begin_lane = pl.multiple_of(begin_lane, DH)
+            lanes = pl.ds(begin_lane, DH)
+            return jnp.concatenate(
+                [arrays[which][begin : begin + count, lanes] for which, begin, count in segments]
+            )
+
+        keys = [joined(segments, 0) for segments, _ in layout]
+        turned = [joined(segments, head_count).T for segments, _ in layout]
         for tile in range(span // lane):
             spot = slice(tile * lane, (tile + 1) * lane)
-            query = query_ref[:, spot]
+            query = query_ref[query_rows, spot]
             if first:
                 top = jnp.full((1, lane), LOW, jnp.float32)
                 total = jnp.zeros((1, lane), jnp.float32)
                 acc = jnp.zeros((DH, lane), jnp.float32)
             else:
-                top, total, acc = stat_in[0:1, spot], stat_in[1:2, spot], acc_in[:, spot]
+                top = stat_in[stat_rows : stat_rows + 1, spot]
+                total = stat_in[stat_rows + 1 : stat_rows + 2, spot]
+                acc = acc_in[query_rows, spot]
             for index in range(chunk_count):
                 scores = jnp.dot(keys[index], query, preferred_element_type=jnp.float32)
                 scores = jnp.where(places[index] < limits[index, 0:1, spot], scores, MASKED)
@@ -113,25 +118,22 @@
                 continue
             out_ref, begin = (keep_out, 0) if tile * lane < rows else (send_out, rows)
             out_spot = slice(tile * lane - begin, (tile + 1) * lane - begin)
-            out_ref[pl.ds(pl.multiple_of(head * DH, DH), DH), out_spot] = (
-                acc * (1.0 / total)
-            ).astype(jnp.bfloat16)
-            levels[0:1, spot] = top * factor + jnp.log2(total)
-        if last:
-            level = levels[0:1, :]
+            out_ref[query_rows, out_spot] = (acc * (1.0 / total)).astype(jnp.bfloat16)
+            level = top * factor + jnp.log2(total)
             for part in range(3):
                 piece = level.astype(jnp.bfloat16).astype(jnp.float32)
-                stats[pl.ds(part * head_count + head, 1), :] = piece
+                stats[part * head_count + head : part * head_count + head + 1, spot] = piece
                 level = level - piece
 
     if first or last:
-        update()
+        for at, head in enumerate(heads):
+            update(head, at)
     else:
         seen = functools.reduce(jnp.maximum, [bounds[index] for index in range(chunk_count)]) > 0
 
         @pl.when(seen)
         def _():
-            update()
+            update(step, 0)
 
         @pl.when(jnp.logical_not(seen))
         def _():
@@ -141,12 +143,9 @@
     if not last:
         token_out[...] = jnp.zeros_like(token_out)
     else:
-
-        @pl.when(head == head_count - 1)
-        def _():
-            feat = head_count * DH
-            keep_out[feat : feat + 16, :] = stats[:, :rows].astype(jnp.bfloat16)
-            send_out[feat : feat + 16, :] = stats[:, rows:].astype(jnp.bfloat16)
+        feat = head_count * DH
+        keep_out[feat : feat + 16, :] = stats[:, :rows].astype(jnp.bfloat16)
+        send_out[feat : feat + 16, :] = stats[:, rows:].astype(jnp.bfloat16)
 
 
 def attention_call(queries, chunks, state, ctx_info, last, token, side=0):
@@ -155,6 +154,8 @@
     head_count = feat // DH
     first = state is None
     span = (2 if last else 4) * rows
+    steps = 1 if last else head_count
+    high = head_count // steps
     with_ctx = ctx_info is not None
     operands, specs = [], []
     if with_ctx:
@@ -162,31 +163,41 @@
         specs.append(pl.BlockSpec(memory_space=pltpu.SMEM))
     operands += [token, queries, queries]
     specs.append(pl.BlockSpec(memory_space=pl.ANY))
-    specs.append(pl.BlockSpec((DH, span), lambda h: (h, side)))
+    specs.append(pl.BlockSpec((high * DH, span), lambda h: (h, side)))
     specs.append(pl.BlockSpec((16, span), lambda h: (feat // 16, side)))
+    found = []
+    for segments, _ in chunks:
+        for array, begin, count in segments:
+            for known, places in found:
+                if known is array:
+                    places.add((begin, count))
+                    break
+            else:
+                found.append((array, {(begin, count)}))
+    starts = []
+    for array, places in found:
+        begin, count = min(places)
+        exact = len(places) == 1 and begin % count == 0
+        operands.append(array)
+        shape = (count if exact else array.shape[0], array.shape[1])
+        at = begin // count if exact else 0
+        specs.append(pl.BlockSpec(shape, lambda h, at=at: (at, 0)))
+        starts.append(begin if exact else 0)
+
+    def number(array):
+        return next(at for at, (known, _) in enumerate(found) if known is array)
+
     layout = []
     for segments, marks in chunks:
-        places = []
-        for array, begin, count in segments:
-            block, wanted = 0, count
-            if begin % count == 0:
-                block, begin = begin // count, 0
-            else:
-                count = array.shape[0]
-            operands += [array, array]
-            specs.append(pl.BlockSpec((count, DH), lambda h, at=block: (at, h)))
-            specs.append(pl.BlockSpec((count, DH), lambda h, at=block: (at, head_count + h)))
-            places.append((begin, wanted))
-        layout.append((tuple(places), marks is not None))
-        if marks is not None:
-            operands.append(marks)
-            specs.append(
-                pl.BlockSpec((16, rows), lambda h, at=marks.shape[0] // 16 - 1: (at, 0))
-            )
+        parts = tuple(
+            (number(array), begin - starts[number(array)], count)
+            for array, begin, count in segments
+        )
+        layout.append((parts, None if marks is None else (number(marks), marks.shape[0] - 16)))
     aliases = {}
     state_specs = [
-        pl.BlockSpec((DH, span), lambda h: (h, side)),
-        pl.BlockSpec((8, span), lambda h: (h, side)),
+        pl.BlockSpec((high * DH, span), lambda h: (h, side)),
+        pl.BlockSpec((high * 8, span), lambda h: (h, side)),
     ]
     if not first:
         if not last:
@@ -208,15 +219,12 @@
         pltpu.SMEM((len(chunks),), jnp.int32),
     ]
     if last:
-        scratch += [
-            pltpu.VMEM((16, span), jnp.float32),
-            pltpu.VMEM((8, span), jnp.float32),
-        ]
+        scratch.append(pltpu.VMEM((16, span), jnp.float32))
     return pl.pallas_call(
         functools.partial(
-            attention_kernel, layout, first, last, with_ctx, head_count, rows
+            attention_kernel, len(found), layout, first, last, with_ctx, head_count, rows
         ),
-        grid=(head_count,),
+        grid=(steps,),
         in_specs=specs,
         out_specs=out_specs,
         out_shape=out_shape,

time: 167 us -> 165 us (0.988)
  Pallas kernels: 51 us -> 48.4 us
    pallas_call x5, Pallas kernels: 34.9 us -> 32.3 us  [attention_call(): pl.pallas_call(functools.partial(attention_kernel, len(found), layout, fi...]
  transfers between devices with their start and end apart: 29 -> 29, of which waited for: 12 -> 12; matrix products, arithmetic and copies ran while one was open for 7% -> 7% of each run, Pallas kernels for 26% -> 25%
where the time goes in v3:
time: 165 us; the launch traced here: 164 us
  waiting for transfers between devices  53.6 us (32%)
  Pallas kernels  48.4 us (29%)
  starting transfers between devices  41.1 us (25%)
  matrix products  8.11 us (5%)
  other arithmetic  6.41 us (4%)
  local copies, waits for them, and re-layouts  5.96 us (4%)
    pallas_call x5, Pallas kernels, attention_call(): pl.pallas_call(functools.partial(attention_kernel, len(found), layout, fi...  32.3 us
    ppermute x6, waiting for transfers between devices, shift_y(): return lax.ppermute(item, 'heads', steps)  25 us
    ppermute x9, starting transfers between devices, shift(): return lax.ppermute(item, 'blk', steps)  14 us
    ppermute x12, waiting for transfers between devices, swap(): return lax.ppermute(item, 'blk', [(i, i ^ mask) for i in range(blk_count)])  12.7 us
    ppermute x6, starting transfers between devices, shift_y(): return lax.ppermute(item, 'heads', steps)  8.89 us
    ppermute x12, starting transfers between devices, swap(): return lax.ppermute(item, 'blk', [(i, i ^ mask) for i in range(blk_count)])  8.82 us
    all_to_all x1, starting transfers between devices, shards(): pieces = lax.all_to_all(slot, 'blk', 0, 0, axis_index_groups=columns)  8.47 us
    dot_general x8, matrix products, dots(): jnp.dot(block, item[step], preferred_element_type=jnp.float32)  8.11 us
  transfers between devices with their start and end apart: 29, of which 12 were waited for; matrix products, arithmetic and copies ran while one was open for 7% of the time, Pallas kernels for 25%

profile of v3, /device:TPU:2, one launch (start us, length us, event | category | flops | bytes accessed | tf_op | source)
XLA Modules:
  0.0 163.9 jit_solution(12924830228919733269)
XLA Ops:
  0.0 2.1 %pad_maximum_fusion.2 = bf16[8,32,1280]{2,1,0:T(8,128)(2,1)} fusion(bf16[8,32,640]{2,1,0:T(8,128)(2,1)} %bitcast.23, bf16[8,32,640]{2,1,0:T(8,128)(2,1)} %bitcast.24), kind=kLoop, calls=%fused_computation.2 | loop fusion | flops 1310720 | bytes 1310720 | tf_op jit(solution)/shard_map/concatenate | solution.py:395
  2.1 8.5 %all-to-all-start = ((bf16[8,32,1280]{2,1,0:T(8,128)(2,1)}), bf16[8,32,1280]{2,1,0:T(8,128)(2,1)S(1)}, u32[]{:S(2)}, u32[]{:S(2)}) async-start(bf16[8,32,1280]{2,1,0:T(8,128)(2,1)} %pad_maximum_fusion.2), calls=%async_computation | async-start | bytes 1310720 | tf_op jit(solution)/shard_map/all_to_all | solution.py:399
  10.8 0.2 pad_maximum_fusion.1.refs_3_
  11.0 3.3 %collective-permute-start.6 = (bf16[304,1280]{1,0:T(8,128)(2,1)S(1)}, bf16[304,1280]{1,0:T(8,128)(2,1)}, u32[]{:S(2)}, u32[]{:S(2)}) collective-permute-start(bf16[304,1280]{1,0:T(8,128)(2,1)S(1)} %pad_maximum_fusion.1.refs_3_), channel_id=1, source_target_pairs={{0,224},{8,232},{16,240},{24,248},{32,0},{40,8},{48,16},{56,24},{6... | collective-permute-start | bytes 2334728 | tf_op jit(solution)/shard_map/ppermute | solution.py:380
  14.7 2.2 %collective-permute-start.1 = (bf16[656,256]{1,0:T(8,128)(2,1)S(1)}, bf16[656,256]{1,0:T(8,128)(2,1)}, u32[]{:S(2)}, u32[]{:S(2)}) collective-permute-start(bf16[656,256]{1,0:T(8,128)(2,1)S(1)} %pad_maximum_fusion.3), channel_id=1, source_target_pairs={{0,16},{8,24},{16,0},{24,8},{32,48},{40,56},{48,32},{56,40},{64,80... | collective-permute-start | bytes 1007624 | tf_op jit(solution)/shard_map/ppermute | solution.py:383
  16.9 0.6 pad_add_fusion.info.refs_0_
  17.5 6.4 %columns.1 = (bf16[640,640]{1,0:T(8,128)(2,1)}, bf16[640,640]{1,0:T(8,128)(2,1)}, bf16[640,640]{1,0:T(8,128)(2,1)}, bf16[640,640]{1,0:T(8,128)(2,1)}, bf16[640,640]{1,0:T(8,128)(2,1)}) custom-call(s32[10]{0:T(128)} %pad_add_fusion.info.refs_0_, bf16[640,5120]{1,0:T(8,128)(2,1)} %in_ref.1), custom_call_target="tpu_custom_call" | custom-call | bytes 8192000 | tf_op jit(solution)/shard_map/columns/pallas_call | solution.py:305
  24.0 2.6 %collective-permute-done.1 = bf16[656,256]{1,0:T(8,128)(2,1)} collective-permute-done((bf16[656,256]{1,0:T(8,128)(2,1)S(1)}, bf16[656,256]{1,0:T(8,128)(2,1)}, u32[]{:S(2)}, u32[]{:S(2)}) %collective-permute-start.1) | collective-permute-done | bytes 335904 | tf_op jit(solution)/shard_map/ppermute | solution.py:383
  26.6 4.2 %all-to-all-done.in_ref = bf16[8,32,1280]{2,1,0:T(8,128)(2,1)S(1)} async-done(((bf16[8,32,1280]{2,1,0:T(8,128)(2,1)}), bf16[8,32,1280]{2,1,0:T(8,128)(2,1)S(1)}, u32[]{:S(2)}, u32[]{:S(2)}) %all-to-all-start) | async-done | bytes 655392 | tf_op jit(solution)/shard_map/all_to_all | solution.py:399
  30.8 0.9 copy-done.1
  31.7 1.8 %offer.1 = (bf16[32,1280]{1,0:T(8,128)(2,1)}, bf16[32,1280]{1,0:T(8,128)(2,1)}, bf16[32,1280]{1,0:T(8,128)(2,1)}, bf16[32,1280]{1,0:T(8,128)(2,1)}) custom-call(s32[10]{0:T(128)} %pad_add_fusion.info.refs_0_, bf16[8,32,1280]{2,1,0:T(8,128)(2,1)} %copy-done.1), custom_call_target="tpu_custom_call" | custom-call | tf_op jit(solution)/shard_map/offer/pallas_call | solution.py:329
  33.5 2.1 %collective-permute-start.4 = (bf16[32,1280]{1,0:T(8,128)(2,1)}, bf16[32,1280]{1,0:T(8,128)(2,1)S(1)}, u32[]{:S(2)}, u32[]{:S(2)}) collective-permute-start(bf16[32,1280]{1,0:T(8,128)(2,1)} %get-tuple-element.75), channel_id=1, source_target_pairs={{0,16},{8,24},{16,0},{24,8},{32,48},{40,56},{48,32},{56,40},{64,80... | collective-permute-start | bytes 245768 | tf_op jit(solution)/shard_map/ppermute | solution.py:383
  35.7 1.2 collective-permute-start.5
  36.9 3.2 %collective-permute-done.4.refs_2_ = bf16[32,1280]{1,0:T(8,128)(2,1)S(1)} collective-permute-done((bf16[32,1280]{1,0:T(8,128)(2,1)}, bf16[32,1280]{1,0:T(8,128)(2,1)S(1)}, u32[]{:S(2)}, u32[]{:S(2)}) %collective-permute-start.4) | collective-permute-done | bytes 81952 | tf_op jit(solution)/shard_map/ppermute | solution.py:383
  40.1 1.7 %collective-permute-done.5.refs_3_ = bf16[32,1280]{1,0:T(8,128)(2,1)S(1)} collective-permute-done((bf16[32,1280]{1,0:T(8,128)(2,1)}, bf16[32,1280]{1,0:T(8,128)(2,1)S(1)}, u32[]{:S(2)}, u32[]{:S(2)}) %collective-permute-start.5) | collective-permute-done | bytes 81952 | tf_op jit(solution)/shard_map/ppermute | solution.py:383
  41.8 0.6 copy-done.12
  42.4 1.7 %choose.1.refs_8_ = bf16[32,1280]{1,0:T(8,128)(2,1)} custom-call(s32[10]{0:T(128)} %pad_add_fusion.info.refs_0_, bf16[32,1280]{1,0:T(8,128)(2,1)} %get-tuple-element.73.refs_0_, bf16[32,1280]{1,0:T(8,128)(2,1)} %copy-done.10, bf16[32,1280]{1,0:T(8,128)(2,1)} %copy-done.11, bf16[32,1280]{1,0:T(8,128)(2,1)} %copy-done.12), custom_call_target="tpu_custom_call" | custom-call | tf_op jit(solution)/shard_map/choose/pallas_call | solution.py:354
  44.1 0.9 collective-permute-done
  45.0 1.6 constant_dynamic-update-slice_fusion.2
  46.5 1.3 collective-permute-start.7
  47.9 1.9 %collective-permute-start.8 = (bf16[304,1280]{1,0:T(8,128)(2,1)}, bf16[304,1280]{1,0:T(8,128)(2,1)}, u32[]{:S(2)}, u32[]{:S(2)}) collective-permute-start(bf16[304,1280]{1,0:T(8,128)(2,1)} %get-tuple-element.83.refs_5_), channel_id=1, source_target_pairs={{0,224},{8,232},{16,240},{24,248},{32,0},{40,8},{48,16},{56,24},{6... | collective-permute-start | bytes 2334728 | tf_op jit(solution)/shard_map/ppermute | solution.py:380
  49.8 1.6 collective-permute-start.12
  51.3 1.7 %collective-permute-start.13 = (bf16[640,640]{1,0:T(8,128)(2,1)}, bf16[640,640]{1,0:T(8,128)(2,1)S(1)}, u32[]{:S(2)}, u32[]{:S(2)}) collective-permute-start(bf16[640,640]{1,0:T(8,128)(2,1)} %get-tuple-element.90), channel_id=1, source_target_pairs={{0,6},{1,7},{2,0},{3,1},{4,2},{5,3},{6,4},{7,5},{8,14},{9,15},{10,... | collective-permute-start | bytes 2457608 | tf_op jit(solution)/shard_map/ppermute | solution.py:387
  53.0 2.0 %collective-permute-start.14 = (bf16[640,640]{1,0:T(8,128)(2,1)}, bf16[640,640]{1,0:T(8,128)(2,1)S(1)}, u32[]{:S(2)}, u32[]{:S(2)}) collective-permute-start(bf16[640,640]{1,0:T(8,128)(2,1)} %get-tuple-element.91), channel_id=1, source_target_pairs={{0,4},{1,5},{2,6},{3,7},{4,0},{5,1},{6,2},{7,3},{8,12},{9,13},{10,... | collective-permute-start | bytes 2457608 | tf_op jit(solution)/shard_map/ppermute | solution.py:387
  55.0 2.3 %pad_maximum_fusion.refs_1_.refs_2_.refs_3_ = bf16[656,1024]{1,0:T(8,128)(2,1)} fusion(bf16[656,256]{1,0:T(8,128)(2,1)} %collective-permute-done.2, bf16[16,256]{1,0:T(8,128)(2,1)S(1)} %pad_slice_fusion, bf16[640,256]{1,0:T(8,128)(2,1)S(1)} %bitcast.22, bf16[656,256]{1,0:T(8,128)(2,1)S(1)} %collective-permute-done.9, bf16[656,256]{1,0:T(8,128)(2,1)} %collective-permute-done.1), kind=kLoop, calls=%fused_computation | loop fusion | flops 6717440 | bytes 2686976 | tf_op jit(solution)/shard_map/concatenate | solution.py:422
  57.3 10.2 %attend.5 = (f32[640,1024]{1,0:T(8,128)}, f32[40,1024]{1,0:T(8,128)}, f32[8,128]{1,0:T(8,128)}) custom-call(s32[10]{0:T(128)} %pad_add_fusion.info.refs_0_, bf16[656,1024]{1,0:T(8,128)(2,1)} %pad_maximum_fusion.refs_1_.refs_2_.refs_3_, bf16[656,1024]{1,0:T(8,128)(2,1)} %pad_maximum_fusion.refs_1_.refs_2_.refs_3_, bf16[304,1280]{1,0:T(8,128)(2,1)} %copy-done.4, ...), custom_call_target="tpu_custom_call" | custom-call | flops 18432000000 | bytes 8388608 | tf_op jit(solution)/shard_map/attend/pallas_call | solution.py:223
  67.5 0.3 collective-permute-done.7.refs_3_.refs_7_
  67.8 1.2 collective-permute-start.10
  69.0 2.1 %collective-permute-start.11 = (bf16[304,1280]{1,0:T(8,128)(2,1)}, bf16[304,1280]{1,0:T(8,128)(2,1)}, u32[]{:S(2)}, u32[]{:S(2)}) collective-permute-start(bf16[304,1280]{1,0:T(8,128)(2,1)} %collective-permute-done.8.refs_4_.refs_9_), channel_id=1, source_target_pairs={{0,224},{8,232},{16,240},{24,248},{32,0},{40,8},{48,16},{56,24},{6... | collective-permute-start | bytes 2334728 | tf_op jit(solution)/shard_map/ppermute | solution.py:380
  71.1 5.7 %attend.6 = (f32[640,1024]{1,0:T(8,128)}, f32[40,1024]{1,0:T(8,128)}, f32[8,128]{1,0:T(8,128)}) custom-call(f32[8,128]{1,0:T(8,128)} %get-tuple-element.92.refs_0_, bf16[656,1024]{1,0:T(8,128)(2,1)} %pad_maximum_fusion.refs_1_.refs_2_.refs_3_, ...), custom_call_target="tpu_custom_call", output_to_operand_aliasing={{0}: (5, {}), {1}: (6, {})} | custom-call | flops 12288000000 | bytes 8388608 | tf_op jit(solution)/shard_map/attend/pallas_call | solution.py:223
  76.8 13.2 %collective-permute-done.14 = bf16[640,640]{1,0:T(8,128)(2,1)S(1)} collective-permute-done((bf16[640,640]{1,0:T(8,128)(2,1)}, bf16[640,640]{1,0:T(8,128)(2,1)S(1)}, u32[]{:S(2)}, u32[]{:S(2)}) %collective-permute-start.14) | collective-permute-done | bytes 819232 | tf_op jit(solution)/shard_map/ppermute | solution.py:387
  90.1 0.7 slice.23
  90.8 0.9 collective-permute-start.17
  91.8 1.7 %collective-permute-start.15 = (bf16[160,1280]{1,0:T(8,128)(2,1)S(1)}, bf16[160,1280]{1,0:T(8,128)(2,1)}, u32[]{:S(2)}, u32[]{:S(2)}) collective-permute-start(bf16[160,1280]{1,0:T(8,128)(2,1)S(1)} %slice.21), channel_id=1, source_target_pairs={{0,32},{8,40},{16,48},{24,56},{32,64},{40,72},{48,80},{56,88},{64,... | collective-permute-start | bytes 1228808 | tf_op jit(solution)/shard_map/ppermute | solution.py:380
  93.5 1.0 slice.22
  94.6 1.6 collective-permute-start.16
  96.1 5.8 %attend.7 = (f32[640,1024]{1,0:T(8,128)}, f32[40,1024]{1,0:T(8,128)}, f32[8,128]{1,0:T(8,128)}) custom-call(f32[8,128]{1,0:T(8,128)} %get-tuple-element.96.refs_0_, bf16[656,1024]{1,0:T(8,128)(2,1)} %pad_maximum_fusion.refs_1_.refs_2_.refs_3_, ...), custom_call_target="tpu_custom_call", output_to_operand_aliasing={{0}: (5, {}), {1}: (6, {})} | custom-call | flops 12288000000 | bytes 8388608 | tf_op jit(solution)/shard_map/attend/pallas_call | solution.py:223
  101.9 4.3 %collective-permute-done.15.refs_4_ = bf16[160,1280]{1,0:T(8,128)(2,1)} collective-permute-done((bf16[160,1280]{1,0:T(8,128)(2,1)S(1)}, bf16[160,1280]{1,0:T(8,128)(2,1)}, u32[]{:S(2)}, u32[]{:S(2)}) %collective-permute-start.15) | collective-permute-done | bytes 409632 | tf_op jit(solution)/shard_map/ppermute | solution.py:380
  106.2 5.3 %attend.8 = (bf16[656,256]{1,0:T(8,128)(2,1)}, bf16[656,256]{1,0:T(8,128)(2,1)}) custom-call(s32[10]{0:T(128)} %pad_add_fusion.info.refs_0_, f32[8,128]{1,0:T(8,128)} %get-tuple-element.106.refs_1_, bf16[656,1024]{1,0:T(8,128)(2,1)} %pad_maximum_fusion.refs_1_.refs_2_.refs_3_, bf16[656,1024]{1,0:T(8,128)(2,1)} %pad_maximum_fusion.refs_1_.refs_2_.refs_3_, ...), custom_call_target="tpu_custom_call" | custom-call | flops 6144000000 | bytes 8388608 | tf_op jit(solution)/shard_map/attend/pallas_call | solution.py:223
  111.5 0.5 collective-permute-start.20
  112.1 0.4 collective-permute-start.22
  112.5 0.8 collective-permute-done.18.refs_1_
  113.4 0.7 copy-done.5
  114.1 2.0 %merge.3 = bf16[656,256]{1,0:T(8,128)(2,1)} custom-call(bf16[656,256]{1,0:T(8,128)(2,1)} %get-tuple-element.104.refs_0_, bf16[656,256]{1,0:T(8,128)(2,1)} %copy-done.5), custom_call_target="tpu_custom_call" | custom-call | bytes 1024 | tf_op jit(solution)/shard_map/merge/pallas_call | solution.py:282
  116.1 2.1 %collective-permute-start.19 = (bf16[656,256]{1,0:T(8,128)(2,1)}, bf16[656,256]{1,0:T(8,128)(2,1)}, u32[]{:S(2)}, u32[]{:S(2)}) collective-permute-start(bf16[656,256]{1,0:T(8,128)(2,1)} %merge.3), channel_id=1, source_target_pairs={{0,16},{8,24},{16,0},{24,8},{32,48},{40,56},{48,32},{56,40},{64,80... | collective-permute-start | bytes 1007624 | tf_op jit(solution)/shard_map/ppermute | solution.py:383
  118.2 5.3 %attend.9 = (bf16[656,256]{1,0:T(8,128)(2,1)}, bf16[656,256]{1,0:T(8,128)(2,1)}) custom-call(s32[10]{0:T(128)} %pad_add_fusion.info.refs_0_, f32[8,128]{1,0:T(8,128)} %get-tuple-element.106.refs_1_, bf16[656,1024]{1,0:T(8,128)(2,1)} %pad_maximum_fusion.refs_1_.refs_2_.refs_3_, bf16[656,1024]{1,0:T(8,128)(2,1)} %pad_maximum_fusion.refs_1_.refs_2_.refs_3_, ...), custom_call_target="tpu_custom_call" | custom-call | flops 6144000000 | bytes 8388608 | tf_op jit(solution)/shard_map/attend/pallas_call | solution.py:223
  123.6 4.3 %collective-permute-done.19.refs_1_ = bf16[656,256]{1,0:T(8,128)(2,1)} collective-permute-done((bf16[656,256]{1,0:T(8,128)(2,1)}, bf16[656,256]{1,0:T(8,128)(2,1)}, u32[]{:S(2)}, u32[]{:S(2)}) %collective-permute-start.19) | collective-permute-done | bytes 335904 | tf_op jit(solution)/shard_map/ppermute | solution.py:383
  127.8 2.0 %merge.4.refs_0_ = bf16[656,256]{1,0:T(8,128)(2,1)} custom-call(bf16[656,256]{1,0:T(8,128)(2,1)} %get-tuple-element.107.refs_0_, bf16[656,256]{1,0:T(8,128)(2,1)} %collective-permute-done.19.refs_1_), custom_call_target="tpu_custom_call" | custom-call | bytes 1024 | tf_op jit(solution)/shard_map/merge/pallas_call | solution.py:282
  129.9 2.1 %merge.5 = bf16[256,640]{1,0:T(8,128)(2,1)} custom-call(bf16[656,256]{1,0:T(8,128)(2,1)} %merge.4.refs_0_, bf16[656,256]{1,0:T(8,128)(2,1)} %collective-permute-done.23.refs_1_), custom_call_target="tpu_custom_call" | custom-call | bytes 1024 | tf_op jit(solution)/shard_map/merge/pallas_call | solution.py:282
  132.0 0.8 collective-permute-start.26
  132.8 2.4 %collective-permute-start.25 = (bf16[256,640]{1,0:T(8,128)(2,1)}, bf16[256,640]{1,0:T(8,128)(2,1)S(1)}, u32[]{:S(2)}, u32[]{:S(2)}) collective-permute-start(bf16[256,640]{1,0:T(8,128)(2,1)} %merge.5), channel_id=1, source_target_pairs={{0,6},{1,7},{2,0},{3,1},{4,2},{5,3},{6,4},{7,5},{8,14},{9,15},{10,... | collective-permute-start | bytes 983048 | tf_op jit(solution)/shard_map/ppermute | solution.py:387
  135.2 0.4 collective-permute-start.24
  135.7 1.5 fusion.2
  137.1 0.5 fusion.1
  137.6 11.7 %collective-permute-done.26 = bf16[256,640]{1,0:T(8,128)(2,1)S(1)} collective-permute-done((bf16[256,640]{1,0:T(8,128)(2,1)}, bf16[256,640]{1,0:T(8,128)(2,1)S(1)}, u32[]{:S(2)}, u32[]{:S(2)}) %collective-permute-start.26) | collective-permute-done | bytes 327712 | tf_op jit(solution)/shard_map/ppermute | solution.py:387
  149.3 0.5 fusion.3
  149.9 1.6 fusion.4
  151.6 0.5 fusion.5
  152.1 1.6 fusion.6
  153.8 0.5 fusion.7
  154.3 1.6 select_convert_fusion
  155.9 0.9 collective-permute-start.27
  156.8 6.2 %collective-permute-done.27 = bf16[256,640]{1,0:T(8,128)(2,1)S(1)} collective-permute-done((bf16[256,640]{1,0:T(8,128)(2,1)S(1)}, bf16[256,640]{1,0:T(8,128)(2,1)S(1)}, u32[]{:S(2)}, u32[]{:S(2)}) %collective-permute-start.27) | collective-permute-done | bytes 327712 | tf_op jit(solution)/shard_map/ppermute | solution.py:481
  163.1 0.9 add_convert_fusion
  (69 shorter events, 1.0 us)
Async XLA Ops:
  0.0 10.6 %copy-start.15 = (s32[256]{0:T(256)S(1)}, s32[256]{0:T(256)}, u32[]{:S(2)}) copy-start(s32[256]{0:T(256)} %param.12) | copy-start | bytes 3076
  0.0 10.6 %copy-start.6 = (bf16[256,640]{1,0:T(8,128)(2,1)S(1)}, bf16[256,640]{1,0:T(8,128)(2,1)}, u32[]{:S(2)}) copy-start(bf16[256,640]{1,0:T(8,128)(2,1)} %param.10) | copy-start | bytes 983044
  0.0 10.6 %copy-start.7 = (bf16[256,640]{1,0:T(8,128)(2,1)S(1)}, bf16[256,640]{1,0:T(8,128)(2,1)}, u32[]{:S(2)}) copy-start(bf16[256,640]{1,0:T(8,128)(2,1)} %param.11) | copy-start | bytes 983044
  2.1 28.7 %all-to-all-start = ((bf16[8,32,1280]{2,1,0:T(8,128)(2,1)}), bf16[8,32,1280]{2,1,0:T(8,128)(2,1)S(1)}, u32[]{:S(2)}, u32[]{:S(2)}) async-start(bf16[8,32,1280]{2,1,0:T(8,128)(2,1)} %pad_maximum_fusion.2), calls=%async_computation | async-start | bytes 1310720 | tf_op jit(solution)/shard_map/all_to_all | solution.py:399
  10.7 3.6 %copy-start.8 = (bf16[256,640]{1,0:T(8,128)(2,1)S(1)}, bf16[256,640]{1,0:T(8,128)(2,1)}, u32[]{:S(2)}) copy-start(bf16[256,640]{1,0:T(8,128)(2,1)} %param.9) | copy-start | bytes 983044
  10.8 6.1 %copy-start.13 = (s32[4]{0:T(128)S(1)}, s32[4]{0:T(128)}, u32[]{:S(2)}) copy-start(s32[4]{0:T(128)} %param.16) | copy-start | bytes 52
  10.8 6.1 %copy-start.14 = (s32[4]{0:T(128)S(1)}, s32[4]{0:T(128)}, u32[]{:S(2)}) copy-start(s32[4]{0:T(128)} %param.15) | copy-start | bytes 52
  11.0 12.9 %copy-start.4 = (bf16[304,1280]{1,0:T(8,128)(2,1)}, bf16[304,1280]{1,0:T(8,128)(2,1)S(1)}, u32[]{:S(2)}) copy-start(bf16[304,1280]{1,0:T(8,128)(2,1)S(1)} %pad_maximum_fusion.1.refs_3_) | copy-start | bytes 2334724
  11.0 33.1 %collective-permute-start.6 = (bf16[304,1280]{1,0:T(8,128)(2,1)S(1)}, bf16[304,1280]{1,0:T(8,128)(2,1)}, u32[]{:S(2)}, u32[]{:S(2)}) collective-permute-start(bf16[304,1280]{1,0:T(8,128)(2,1)S(1)} %pad_maximum_fusion.1.refs_3_), channel_id=1, source_target_pairs={{0,224},{8,232},{16,240},{24,248},{32,0},{40,8},{48,16},{56,24},{6... | collective-permute-start | bytes 2334728 | tf_op jit(solution)/shard_map/ppermute | solution.py:380
  14.3 30.6 %collective-permute-start = (bf16[304,1280]{1,0:T(8,128)(2,1)S(1)}, bf16[304,1280]{1,0:T(8,128)(2,1)}, u32[]{:S(2)}, u32[]{:S(2)}) collective-permute-start(bf16[304,1280]{1,0:T(8,128)(2,1)S(1)} %pad_maximum_fusion.1.refs_3_), channel_id=1, source_target_pairs={{0,32},{8,40},{16,48},{24,56},{32,64},{40,72},{48,80},{56,88},{64,... | collective-permute-start | bytes 2334728 | tf_op jit(solution)/shard_map/ppermute | solution.py:380
  14.6 9.4 %collective-permute-start.2 = (bf16[656,256]{1,0:T(8,128)(2,1)S(1)}, bf16[656,256]{1,0:T(8,128)(2,1)}, u32[]{:S(2)}, u32[]{:S(2)}) collective-permute-start(bf16[656,256]{1,0:T(8,128)(2,1)S(1)} %pad_maximum_fusion.3), channel_id=1, source_target_pairs={{0,8},{8,0},{16,24},{24,16},{32,40},{40,32},{48,56},{56,48},{64,72... | collective-permute-start | bytes 1007624 | tf_op jit(solution)/shard_map/ppermute | solution.py:383
  14.7 11.9 %collective-permute-start.1 = (bf16[656,256]{1,0:T(8,128)(2,1)S(1)}, bf16[656,256]{1,0:T(8,128)(2,1)}, u32[]{:S(2)}, u32[]{:S(2)}) collective-permute-start(bf16[656,256]{1,0:T(8,128)(2,1)S(1)} %pad_maximum_fusion.3), channel_id=1, source_target_pairs={{0,16},{8,24},{16,0},{24,8},{32,48},{40,56},{48,32},{56,40},{64,80... | collective-permute-start | bytes 1007624 | tf_op jit(solution)/shard_map/ppermute | solution.py:383
  30.8 0.9 copy-start.1
  33.5 3.4 %collective-permute-start.3 = (bf16[32,1280]{1,0:T(8,128)(2,1)}, bf16[32,1280]{1,0:T(8,128)(2,1)S(1)}, u32[]{:S(2)}, u32[]{:S(2)}) collective-permute-start(bf16[32,1280]{1,0:T(8,128)(2,1)} %get-tuple-element.74), channel_id=1, source_target_pairs={{0,8},{8,0},{16,24},{24,16},{32,40},{40,32},{48,56},{56,48},{64,72... | collective-permute-start | bytes 245768 | tf_op jit(solution)/shard_map/ppermute | solution.py:383
  33.5 6.6 %collective-permute-start.4 = (bf16[32,1280]{1,0:T(8,128)(2,1)}, bf16[32,1280]{1,0:T(8,128)(2,1)S(1)}, u32[]{:S(2)}, u32[]{:S(2)}) collective-permute-start(bf16[32,1280]{1,0:T(8,128)(2,1)} %get-tuple-element.75), channel_id=1, source_target_pairs={{0,16},{8,24},{16,0},{24,8},{32,48},{40,56},{48,32},{56,40},{64,80... | collective-permute-start | bytes 245768 | tf_op jit(solution)/shard_map/ppermute | solution.py:383
  35.7 6.1 %collective-permute-start.5 = (bf16[32,1280]{1,0:T(8,128)(2,1)}, bf16[32,1280]{1,0:T(8,128)(2,1)S(1)}, u32[]{:S(2)}, u32[]{:S(2)}) collective-permute-start(bf16[32,1280]{1,0:T(8,128)(2,1)} %get-tuple-element.76), channel_id=1, source_target_pairs={{0,24},{8,16},{16,8},{24,0},{32,56},{40,48},{48,40},{56,32},{64,88... | collective-permute-start | bytes 245768 | tf_op jit(solution)/shard_map/ppermute | solution.py:383
  36.9 4.9 %copy-start.10 = (bf16[32,1280]{1,0:T(8,128)(2,1)}, bf16[32,1280]{1,0:T(8,128)(2,1)S(1)}, u32[]{:S(2)}) copy-start(bf16[32,1280]{1,0:T(8,128)(2,1)S(1)} %collective-permute-done.3.refs_1_) | copy-start | bytes 245764
  40.1 1.7 %copy-start.11 = (bf16[32,1280]{1,0:T(8,128)(2,1)}, bf16[32,1280]{1,0:T(8,128)(2,1)S(1)}, u32[]{:S(2)}) copy-start(bf16[32,1280]{1,0:T(8,128)(2,1)S(1)} %collective-permute-done.4.refs_2_) | copy-start | bytes 245764
  41.8 0.6 copy-start.12
  46.5 6.5 %collective-permute-start.9 = (bf16[656,256]{1,0:T(8,128)(2,1)}, bf16[656,256]{1,0:T(8,128)(2,1)S(1)}, u32[]{:S(2)}, u32[]{:S(2)}) collective-permute-start(bf16[656,256]{1,0:T(8,128)(2,1)} %collective-permute-done.1), channel_id=1, source_target_pairs={{0,8},{8,0},{16,24},{24,16},{32,40},{40,32},{48,56},{56,48},{64,72... | collective-permute-start | bytes 1007624 | tf_op jit(solution)/shard_map/ppermute | solution.py:383
  46.5 21.3 %collective-permute-start.7 = (bf16[304,1280]{1,0:T(8,128)(2,1)}, bf16[304,1280]{1,0:T(8,128)(2,1)}, u32[]{:S(2)}, u32[]{:S(2)}) collective-permute-start(bf16[304,1280]{1,0:T(8,128)(2,1)} %get-tuple-element.82.refs_4_), channel_id=1, source_target_pairs={{0,32},{8,40},{16,48},{24,56},{32,64},{40,72},{48,80},{56,88},{64,... | collective-permute-start | bytes 2334728 | tf_op jit(solution)/shard_map/ppermute | solution.py:380
  47.9 20.0 %collective-permute-start.8 = (bf16[304,1280]{1,0:T(8,128)(2,1)}, bf16[304,1280]{1,0:T(8,128)(2,1)}, u32[]{:S(2)}, u32[]{:S(2)}) collective-permute-start(bf16[304,1280]{1,0:T(8,128)(2,1)} %get-tuple-element.83.refs_5_), channel_id=1, source_target_pairs={{0,224},{8,232},{16,240},{24,248},{32,0},{40,8},{48,16},{56,24},{6... | collective-permute-start | bytes 2334728 | tf_op jit(solution)/shard_map/ppermute | solution.py:380
  49.8 27.1 %collective-permute-start.12 = (bf16[640,640]{1,0:T(8,128)(2,1)}, bf16[640,640]{1,0:T(8,128)(2,1)S(1)}, u32[]{:S(2)}, u32[]{:S(2)}) collective-permute-start(bf16[640,640]{1,0:T(8,128)(2,1)} %get-tuple-element.89), channel_id=1, source_target_pairs={{0,2},{1,3},{2,4},{3,5},{4,6},{5,7},{6,0},{7,1},{8,10},{9,11},{10,... | collective-permute-start | bytes 2457608 | tf_op jit(solution)/shard_map/ppermute | solution.py:387
  51.3 25.5 %collective-permute-start.13 = (bf16[640,640]{1,0:T(8,128)(2,1)}, bf16[640,640]{1,0:T(8,128)(2,1)S(1)}, u32[]{:S(2)}, u32[]{:S(2)}) collective-permute-start(bf16[640,640]{1,0:T(8,128)(2,1)} %get-tuple-element.90), channel_id=1, source_target_pairs={{0,6},{1,7},{2,0},{3,1},{4,2},{5,3},{6,4},{7,5},{8,14},{9,15},{10,... | collective-permute-start | bytes 2457608 | tf_op jit(solution)/shard_map/ppermute | solution.py:387
  53.0 37.1 %collective-permute-start.14 = (bf16[640,640]{1,0:T(8,128)(2,1)}, bf16[640,640]{1,0:T(8,128)(2,1)S(1)}, u32[]{:S(2)}, u32[]{:S(2)}) collective-permute-start(bf16[640,640]{1,0:T(8,128)(2,1)} %get-tuple-element.91), channel_id=1, source_target_pairs={{0,4},{1,5},{2,6},{3,7},{4,0},{5,1},{6,2},{7,3},{8,12},{9,13},{10,... | collective-permute-start | bytes 2457608 | tf_op jit(solution)/shard_map/ppermute | solution.py:387
  67.8 22.2 %collective-permute-start.10 = (bf16[304,1280]{1,0:T(8,128)(2,1)}, bf16[304,1280]{1,0:T(8,128)(2,1)S(1)}, u32[]{:S(2)}, u32[]{:S(2)}) collective-permute-start(bf16[304,1280]{1,0:T(8,128)(2,1)} %collective-permute-done.7.refs_3_.refs_7_), channel_id=1, source_target_pairs={{0,32},{8,40},{16,48},{24,56},{32,64},{40,72},{48,80},{56,88},{64,... | collective-permute-start | bytes 2334728 | tf_op jit(solution)/shard_map/ppermute | solution.py:380
  69.0 21.1 %collective-permute-start.11 = (bf16[304,1280]{1,0:T(8,128)(2,1)}, bf16[304,1280]{1,0:T(8,128)(2,1)}, u32[]{:S(2)}, u32[]{:S(2)}) collective-permute-start(bf16[304,1280]{1,0:T(8,128)(2,1)} %collective-permute-done.8.refs_4_.refs_9_), channel_id=1, source_target_pairs={{0,224},{8,232},{16,240},{24,248},{32,0},{40,8},{48,16},{56,24},{6... | collective-permute-start | bytes 2334728 | tf_op jit(solution)/shard_map/ppermute | solution.py:380
  90.1 6.0 %copy-start.9 = (bf16[304,1280]{1,0:T(8,128)(2,1)}, bf16[304,1280]{1,0:T(8,128)(2,1)S(1)}, u32[]{:S(2)}) copy-start(bf16[304,1280]{1,0:T(8,128)(2,1)S(1)} %collective-permute-done.10.refs_3_.refs_6_) | copy-start | bytes 2334724
  90.8 11.1 %collective-permute-start.17 = (bf16[32,1280]{1,0:T(8,128)(2,1)}, bf16[32,1280]{1,0:T(8,128)(2,1)}, u32[]{:S(2)}, u32[]{:S(2)}) collective-permute-start(bf16[32,1280]{1,0:T(8,128)(2,1)} %slice.23), channel_id=1, source_target_pairs={{0,64},{8,72},{16,80},{24,88},{32,96},{40,104},{48,112},{56,120},{... | collective-permute-start | bytes 245768 | tf_op jit(solution)/shard_map/ppermute | solution.py:380
  91.8 14.4 %collective-permute-start.15 = (bf16[160,1280]{1,0:T(8,128)(2,1)S(1)}, bf16[160,1280]{1,0:T(8,128)(2,1)}, u32[]{:S(2)}, u32[]{:S(2)}) collective-permute-start(bf16[160,1280]{1,0:T(8,128)(2,1)S(1)} %slice.21), channel_id=1, source_target_pairs={{0,32},{8,40},{16,48},{24,56},{32,64},{40,72},{48,80},{56,88},{64,... | collective-permute-start | bytes 1228808 | tf_op jit(solution)/shard_map/ppermute | solution.py:380
  94.6 11.7 %collective-permute-start.16 = (bf16[176,1280]{1,0:T(8,128)(2,1)S(1)}, bf16[176,1280]{1,0:T(8,128)(2,1)}, u32[]{:S(2)}, u32[]{:S(2)}) collective-permute-start(bf16[176,1280]{1,0:T(8,128)(2,1)S(1)} %slice.22), channel_id=1, source_target_pairs={{0,224},{8,232},{16,240},{24,248},{32,0},{40,8},{48,16},{56,24},{6... | collective-permute-start | bytes 1351688 | tf_op jit(solution)/shard_map/ppermute | solution.py:380
  111.5 1.9 %collective-permute-start.18 = (bf16[656,256]{1,0:T(8,128)(2,1)}, bf16[656,256]{1,0:T(8,128)(2,1)S(1)}, u32[]{:S(2)}, u32[]{:S(2)}) collective-permute-start(bf16[656,256]{1,0:T(8,128)(2,1)} %get-tuple-element.105), channel_id=1, source_target_pairs={{0,8},{8,0},{16,24},{24,16},{32,40},{40,32},{48,56},{56,48},{64,72... | collective-permute-start | bytes 1007624 | tf_op jit(solution)/shard_map/ppermute | solution.py:383
  111.5 12.0 %collective-permute-start.20 = (bf16[640,640]{1,0:T(8,128)(2,1)S(1)}, bf16[640,640]{1,0:T(8,128)(2,1)}, u32[]{:S(2)}, u32[]{:S(2)}) collective-permute-start(bf16[640,640]{1,0:T(8,128)(2,1)S(1)} %collective-permute-done.12), channel_id=1, source_target_pairs={{0,8},{8,0},{16,24},{24,16},{32,40},{40,32},{48,56},{56,48},{64,72... | collective-permute-start | bytes 2457608 | tf_op jit(solution)/shard_map/ppermute | solution.py:383
  112.0 11.5 %collective-permute-start.21 = (bf16[640,640]{1,0:T(8,128)(2,1)S(1)}, bf16[640,640]{1,0:T(8,128)(2,1)}, u32[]{:S(2)}, u32[]{:S(2)}) collective-permute-start(bf16[640,640]{1,0:T(8,128)(2,1)S(1)} %collective-permute-done.14), channel_id=1, source_target_pairs={{0,8},{8,0},{16,24},{24,16},{32,40},{40,32},{48,56},{56,48},{64,72... | collective-permute-start | bytes 2457608 | tf_op jit(solution)/shard_map/ppermute | solution.py:383
  112.1 11.4 %collective-permute-start.22 = (bf16[640,640]{1,0:T(8,128)(2,1)S(1)}, bf16[640,640]{1,0:T(8,128)(2,1)}, u32[]{:S(2)}, u32[]{:S(2)}) collective-permute-start(bf16[640,640]{1,0:T(8,128)(2,1)S(1)} %collective-permute-done.13), channel_id=1, source_target_pairs={{0,8},{8,0},{16,24},{24,16},{32,40},{40,32},{48,56},{56,48},{64,72... | collective-permute-start | bytes 2457608 | tf_op jit(solution)/shard_map/ppermute | solution.py:383
  113.4 0.7 copy-start.5
  116.1 11.7 %collective-permute-start.19 = (bf16[656,256]{1,0:T(8,128)(2,1)}, bf16[656,256]{1,0:T(8,128)(2,1)}, u32[]{:S(2)}, u32[]{:S(2)}) collective-permute-start(bf16[656,256]{1,0:T(8,128)(2,1)} %merge.3), channel_id=1, source_target_pairs={{0,16},{8,24},{16,0},{24,8},{32,48},{40,56},{48,32},{56,40},{64,80... | collective-permute-start | bytes 1007624 | tf_op jit(solution)/shard_map/ppermute | solution.py:383
  123.5 12.2 %copy-start.3 = (bf16[640,640]{1,0:T(8,128)(2,1)S(1)}, bf16[640,640]{1,0:T(8,128)(2,1)}, u32[]{:S(2)}) copy-start(bf16[640,640]{1,0:T(8,128)(2,1)} %get-tuple-element.116) | copy-start | bytes 2457604
  123.5 6.4 %collective-permute-start.23 = (bf16[656,256]{1,0:T(8,128)(2,1)}, bf16[656,256]{1,0:T(8,128)(2,1)}, u32[]{:S(2)}, u32[]{:S(2)}) collective-permute-start(bf16[656,256]{1,0:T(8,128)(2,1)} %get-tuple-element.114), channel_id=1, source_target_pairs={{0,8},{8,0},{16,24},{24,16},{32,40},{40,32},{48,56},{56,48},{64,72... | collective-permute-start | bytes 1007624 | tf_op jit(solution)/shard_map/ppermute | solution.py:383
  129.8 7.3 %copy-start.2 = (bf16[640,640]{1,0:T(8,128)(2,1)S(1)}, bf16[640,640]{1,0:T(8,128)(2,1)}, u32[]{:S(2)}) copy-start(bf16[640,640]{1,0:T(8,128)(2,1)} %get-tuple-element.115) | copy-start | bytes 2457604
  132.0 5.2 %copy-start = (bf16[256,640]{1,0:T(8,128)(2,1)S(1)}, bf16[256,640]{1,0:T(8,128)(2,1)}, u32[]{:S(2)}) copy-start(bf16[256,640]{1,0:T(8,128)(2,1)} %merge.5) | copy-start | bytes 983044
  132.0 17.4 %collective-permute-start.26 = (bf16[256,640]{1,0:T(8,128)(2,1)}, bf16[256,640]{1,0:T(8,128)(2,1)S(1)}, u32[]{:S(2)}, u32[]{:S(2)}) collective-permute-start(bf16[256,640]{1,0:T(8,128)(2,1)} %merge.5), channel_id=1, source_target_pairs={{0,2},{1,3},{2,4},{3,5},{4,6},{5,7},{6,0},{7,1},{8,10},{9,11},{10,... | collective-permute-start | bytes 983048 | tf_op jit(solution)/shard_map/ppermute | solution.py:387
  132.8 18.8 %collective-permute-start.25 = (bf16[256,640]{1,0:T(8,128)(2,1)}, bf16[256,640]{1,0:T(8,128)(2,1)S(1)}, u32[]{:S(2)}, u32[]{:S(2)}) collective-permute-start(bf16[256,640]{1,0:T(8,128)(2,1)} %merge.5), channel_id=1, source_target_pairs={{0,6},{1,7},{2,0},{3,1},{4,2},{5,3},{6,4},{7,5},{8,14},{9,15},{10,... | collective-permute-start | bytes 983048 | tf_op jit(solution)/shard_map/ppermute | solution.py:387
  135.2 18.6 %collective-permute-start.24 = (bf16[256,640]{1,0:T(8,128)(2,1)}, bf16[256,640]{1,0:T(8,128)(2,1)S(1)}, u32[]{:S(2)}, u32[]{:S(2)}) collective-permute-start(bf16[256,640]{1,0:T(8,128)(2,1)} %merge.5), channel_id=1, source_target_pairs={{0,4},{1,5},{2,6},{3,7},{4,0},{5,1},{6,2},{7,3},{8,12},{9,13},{10,... | collective-permute-start | bytes 983048 | tf_op jit(solution)/shard_map/ppermute | solution.py:387
  155.9 7.2 %collective-permute-start.27 = (bf16[256,640]{1,0:T(8,128)(2,1)S(1)}, bf16[256,640]{1,0:T(8,128)(2,1)S(1)}, u32[]{:S(2)}, u32[]{:S(2)}) collective-permute-start(bf16[256,640]{1,0:T(8,128)(2,1)S(1)} %get-tuple-element.133), channel_id=1, source_target_pairs={{0,1},{1,0},{2,3},{3,2},{4,5},{5,4},{6,7},{7,6},{8,9},{9,8},{10,11... | collective-permute-start | bytes 983048 | tf_op jit(solution)/shard_map/ppermute | solution.py:481

commit v4 on v3

--- a/solution.py
+++ b/solution.py
@@ -472,12 +472,19 @@
 
     total = dots(attended, 0)
     blocks = [(shift_y(attended, step), step) for step in (1, ring_y - 1, 2)]
+    same = jnp.bitwise_and(jnp.bitwise_xor(me, head_me), 1) == 0
+    *blocks, (block_far, step_far) = blocks
     for block, step in blocks:
         block, *total = lax.optimization_barrier((block, *total))
         total = [old + new for old, new in zip(total, dots(block, step))]
-    same = jnp.bitwise_and(jnp.bitwise_xor(me, head_me), 1) == 0
-    mine = jnp.where(same, total[0], total[1])
-    other = jnp.where(same, total[1], total[0])
+    pairs = [total, (own_slabs[step_far], core_slabs[step_far])]
+    pairs = [(jnp.where(same, b, a), jnp.where(same, a, b)) for a, b in pairs]
+    (other, mine), (slab_other, slab_mine) = pairs
+    block_far, other, mine, slab_other, slab_mine = lax.optimization_barrier(
+        (block_far, other, mine, slab_other, slab_mine)
+    )
+    other += jnp.dot(block_far, slab_other, preferred_element_type=jnp.float32)
+    mine += jnp.dot(block_far, slab_mine, preferred_element_type=jnp.float32)
     received = lax.ppermute(
         other.astype(jnp.bfloat16), "heads", [(i, i ^ 1) for i in range(head_devices)]
     )

time: 165 us -> 161 us (0.976)
  waiting for transfers between devices: 53.6 us -> 47.1 us
  starting transfers between devices: 41.1 us -> 44.7 us
  matrix products: 8.11 us -> 5.81 us
    ppermute x6, waiting for transfers between devices: 25 us -> 19.4 us  [shift_y(): return lax.ppermute(item, 'heads', steps)]
    dot_general x8 -> x6, matrix products: 8.11 us -> 4.9 us  [dots(): jnp.dot(block, item[step], preferred_element_type=jnp.float32)]
    ppermute x1, starting transfers between devices: 0.91 us -> 3.71 us  [shards(): lax.ppermute(other.astype(jnp.bfloat16), 'heads', [(i, i ^ 1) for i in ra...]
    select_n x0 -> x2, other arithmetic: none -> 1.69 us  [shards(): pairs = [(jnp.where(same, b, a), jnp.where(same, a, b)) for a, b in pairs]]
    ppermute x1, waiting for transfers between devices: 6.25 us -> 4.59 us  [shards(): lax.ppermute(other.astype(jnp.bfloat16), 'heads', [(i, i ^ 1) for i in ra...]
    unnamed x34 -> x38, local copies, waits for them, and re-layouts: 2.52 us -> 3.32 us
  transfers between devices with their start and end apart: 29 -> 29, of which waited for: 12 -> 13; matrix products, arithmetic and copies ran while one was open for 7% -> 7% of each run, Pallas kernels for 25% -> 26%
where the time goes in v4:
time: 161 us; the launch traced here: 160 us
  Pallas kernels  48.4 us (30%)
  waiting for transfers between devices  47.1 us (29%)
  starting transfers between devices  44.7 us (28%)
  other arithmetic  7.98 us (5%)
  matrix products  5.81 us (4%)
  local copies, waits for them, and re-layouts  5.74 us (4%)
    pallas_call x5, Pallas kernels, attention_call(): pl.pallas_call(functools.partial(attention_kernel, len(found), layout, fi...  32.3 us
    ppermute x6, waiting for transfers between devices, shift_y(): return lax.ppermute(item, 'heads', steps)  19.4 us
    ppermute x9, starting transfers between devices, shift(): return lax.ppermute(item, 'blk', steps)  14.3 us
    ppermute x12, waiting for transfers between devices, swap(): return lax.ppermute(item, 'blk', [(i, i ^ mask) for i in range(blk_count)])  12.6 us
    ppermute x6, starting transfers between devices, shift_y(): return lax.ppermute(item, 'heads', steps)  9.31 us
    ppermute x12, starting transfers between devices, swap(): return lax.ppermute(item, 'blk', [(i, i ^ mask) for i in range(blk_count)])  8.84 us
    all_to_all x1, starting transfers between devices, shards(): pieces = lax.all_to_all(slot, 'blk', 0, 0, axis_index_groups=columns)  8.47 us
    pallas_call x1, Pallas kernels, column_blocks(): pl.pallas_call(functools.partial(columns_kernel, ring), grid=(rows // DH,...  6.48 us
  transfers between devices with their start and end apart: 29, of which 13 were waited for; matrix products, arithmetic and copies ran while one was open for 7% of the time, Pallas kernels for 26%

profile of v4, /device:TPU:2, one launch (start us, length us, event | category | flops | bytes accessed | tf_op | source)
XLA Modules:
  0.0 160.1 jit_solution(18287557654641947684)
XLA Ops:
  0.0 2.0 %pad_maximum_fusion.2 = bf16[8,32,1280]{2,1,0:T(8,128)(2,1)} fusion(bf16[8,32,640]{2,1,0:T(8,128)(2,1)} %bitcast.23, bf16[8,32,640]{2,1,0:T(8,128)(2,1)} %bitcast.24), kind=kLoop, calls=%fused_computation.4 | loop fusion | flops 1310720 | bytes 1310720 | tf_op jit(solution)/shard_map/concatenate | solution.py:395
  2.0 8.5 %all-to-all-start = ((bf16[8,32,1280]{2,1,0:T(8,128)(2,1)}), bf16[8,32,1280]{2,1,0:T(8,128)(2,1)S(1)}, u32[]{:S(2)}, u32[]{:S(2)}) async-start(bf16[8,32,1280]{2,1,0:T(8,128)(2,1)} %pad_maximum_fusion.2), calls=%async_computation | async-start | bytes 1310720 | tf_op jit(solution)/shard_map/all_to_all | solution.py:399
  11.0 3.3 %collective-permute-start.6 = (bf16[304,1280]{1,0:T(8,128)(2,1)S(1)}, bf16[304,1280]{1,0:T(8,128)(2,1)}, u32[]{:S(2)}, u32[]{:S(2)}) collective-permute-start(bf16[304,1280]{1,0:T(8,128)(2,1)S(1)} %pad_maximum_fusion.1.refs_3_), channel_id=1, source_target_pairs={{0,224},{8,232},{16,240},{24,248},{32,0},{40,8},{48,16},{56,24},{6... | collective-permute-start | bytes 2334728 | tf_op jit(solution)/shard_map/ppermute | solution.py:380
  14.6 2.2 %collective-permute-start.1 = (bf16[656,256]{1,0:T(8,128)(2,1)S(1)}, bf16[656,256]{1,0:T(8,128)(2,1)}, u32[]{:S(2)}, u32[]{:S(2)}) collective-permute-start(bf16[656,256]{1,0:T(8,128)(2,1)S(1)} %pad_maximum_fusion.3), channel_id=1, source_target_pairs={{0,16},{8,24},{16,0},{24,8},{32,48},{40,56},{48,32},{56,40},{64,80... | collective-permute-start | bytes 1007624 | tf_op jit(solution)/shard_map/ppermute | solution.py:383
  16.8 0.6 pad_add_fusion.info.refs_0_
  17.4 6.5 %columns.1 = (bf16[640,640]{1,0:T(8,128)(2,1)}, bf16[640,640]{1,0:T(8,128)(2,1)}, bf16[640,640]{1,0:T(8,128)(2,1)}, bf16[640,640]{1,0:T(8,128)(2,1)}, bf16[640,640]{1,0:T(8,128)(2,1)}) custom-call(s32[10]{0:T(128)} %pad_add_fusion.info.refs_0_, bf16[640,5120]{1,0:T(8,128)(2,1)} %in_ref.1), custom_call_target="tpu_custom_call" | custom-call | bytes 8192000 | tf_op jit(solution)/shard_map/columns/pallas_call | solution.py:305
  23.9 2.6 %collective-permute-done.1 = bf16[656,256]{1,0:T(8,128)(2,1)} collective-permute-done((bf16[656,256]{1,0:T(8,128)(2,1)S(1)}, bf16[656,256]{1,0:T(8,128)(2,1)}, u32[]{:S(2)}, u32[]{:S(2)}) %collective-permute-start.1) | collective-permute-done | bytes 335904 | tf_op jit(solution)/shard_map/ppermute | solution.py:383
  26.5 4.2 %all-to-all-done.in_ref = bf16[8,32,1280]{2,1,0:T(8,128)(2,1)S(1)} async-done(((bf16[8,32,1280]{2,1,0:T(8,128)(2,1)}), bf16[8,32,1280]{2,1,0:T(8,128)(2,1)S(1)}, u32[]{:S(2)}, u32[]{:S(2)}) %all-to-all-start) | async-done | bytes 655392 | tf_op jit(solution)/shard_map/all_to_all | solution.py:399
  30.7 0.8 copy-done.1
  31.6 1.8 %offer.1 = (bf16[32,1280]{1,0:T(8,128)(2,1)}, bf16[32,1280]{1,0:T(8,128)(2,1)}, bf16[32,1280]{1,0:T(8,128)(2,1)}, bf16[32,1280]{1,0:T(8,128)(2,1)}) custom-call(s32[10]{0:T(128)} %pad_add_fusion.info.refs_0_, bf16[8,32,1280]{2,1,0:T(8,128)(2,1)} %copy-done.1), custom_call_target="tpu_custom_call" | custom-call | tf_op jit(solution)/shard_map/offer/pallas_call | solution.py:329
  33.4 2.1 %collective-permute-start.4 = (bf16[32,1280]{1,0:T(8,128)(2,1)}, bf16[32,1280]{1,0:T(8,128)(2,1)S(1)}, u32[]{:S(2)}, u32[]{:S(2)}) collective-permute-start(bf16[32,1280]{1,0:T(8,128)(2,1)} %get-tuple-element.77), channel_id=1, source_target_pairs={{0,16},{8,24},{16,0},{24,8},{32,48},{40,56},{48,32},{56,40},{64,80... | collective-permute-start | bytes 245768 | tf_op jit(solution)/shard_map/ppermute | solution.py:383
  35.5 1.2 collective-permute-start.5
  36.8 3.2 %collective-permute-done.4.refs_2_ = bf16[32,1280]{1,0:T(8,128)(2,1)S(1)} collective-permute-done((bf16[32,1280]{1,0:T(8,128)(2,1)}, bf16[32,1280]{1,0:T(8,128)(2,1)S(1)}, u32[]{:S(2)}, u32[]{:S(2)}) %collective-permute-start.4) | collective-permute-done | bytes 81952 | tf_op jit(solution)/shard_map/ppermute | solution.py:383
  40.0 1.7 %collective-permute-done.5.refs_3_ = bf16[32,1280]{1,0:T(8,128)(2,1)S(1)} collective-permute-done((bf16[32,1280]{1,0:T(8,128)(2,1)}, bf16[32,1280]{1,0:T(8,128)(2,1)S(1)}, u32[]{:S(2)}, u32[]{:S(2)}) %collective-permute-start.5) | collective-permute-done | bytes 81952 | tf_op jit(solution)/shard_map/ppermute | solution.py:383
  41.7 0.6 copy-done.13
  42.3 1.7 %choose.1.refs_8_ = bf16[32,1280]{1,0:T(8,128)(2,1)} custom-call(s32[10]{0:T(128)} %pad_add_fusion.info.refs_0_, bf16[32,1280]{1,0:T(8,128)(2,1)} %get-tuple-element.75.refs_0_, bf16[32,1280]{1,0:T(8,128)(2,1)} %copy-done.11, bf16[32,1280]{1,0:T(8,128)(2,1)} %copy-done.12, bf16[32,1280]{1,0:T(8,128)(2,1)} %copy-done.13), custom_call_target="tpu_custom_call" | custom-call | tf_op jit(solution)/shard_map/choose/pallas_call | solution.py:354
  44.0 0.9 collective-permute-done
  44.9 1.6 constant_dynamic-update-slice_fusion.2
  46.5 1.2 collective-permute-start.7
  47.7 2.0 %collective-permute-start.8 = (bf16[304,1280]{1,0:T(8,128)(2,1)}, bf16[304,1280]{1,0:T(8,128)(2,1)S(1)}, u32[]{:S(2)}, u32[]{:S(2)}) collective-permute-start(bf16[304,1280]{1,0:T(8,128)(2,1)} %get-tuple-element.85.refs_5_), channel_id=1, source_target_pairs={{0,224},{8,232},{16,240},{24,248},{32,0},{40,8},{48,16},{56,24},{6... | collective-permute-start | bytes 2334728 | tf_op jit(solution)/shard_map/ppermute | solution.py:380
  49.7 1.6 collective-permute-start.12
  51.3 1.7 %collective-permute-start.13 = (bf16[640,640]{1,0:T(8,128)(2,1)}, bf16[640,640]{1,0:T(8,128)(2,1)S(1)}, u32[]{:S(2)}, u32[]{:S(2)}) collective-permute-start(bf16[640,640]{1,0:T(8,128)(2,1)} %get-tuple-element.92), channel_id=1, source_target_pairs={{0,6},{1,7},{2,0},{3,1},{4,2},{5,3},{6,4},{7,5},{8,14},{9,15},{10,... | collective-permute-start | bytes 2457608 | tf_op jit(solution)/shard_map/ppermute | solution.py:387
  52.9 2.0 %collective-permute-start.14 = (bf16[640,640]{1,0:T(8,128)(2,1)}, bf16[640,640]{1,0:T(8,128)(2,1)}, u32[]{:S(2)}, u32[]{:S(2)}) collective-permute-start(bf16[640,640]{1,0:T(8,128)(2,1)} %get-tuple-element.93), channel_id=1, source_target_pairs={{0,4},{1,5},{2,6},{3,7},{4,0},{5,1},{6,2},{7,3},{8,12},{9,13},{10,... | collective-permute-start | bytes 2457608 | tf_op jit(solution)/shard_map/ppermute | solution.py:387
  54.9 2.3 %pad_maximum_fusion.refs_1_.refs_2_.refs_3_ = bf16[656,1024]{1,0:T(8,128)(2,1)} fusion(bf16[656,256]{1,0:T(8,128)(2,1)} %collective-permute-done.2, bf16[16,256]{1,0:T(8,128)(2,1)S(1)} %pad_slice_fusion, bf16[640,256]{1,0:T(8,128)(2,1)S(1)} %bitcast.22, bf16[656,256]{1,0:T(8,128)(2,1)S(1)} %collective-permute-done.9, bf16[656,256]{1,0:T(8,128)(2,1)} %collective-permute-done.1), kind=kLoop, calls=%fused_computation | loop fusion | flops 6717440 | bytes 2686976 | tf_op jit(solution)/shard_map/concatenate | solution.py:422
  57.3 10.2 %attend.5 = (f32[640,1024]{1,0:T(8,128)}, f32[40,1024]{1,0:T(8,128)}, f32[8,128]{1,0:T(8,128)}) custom-call(s32[10]{0:T(128)} %pad_add_fusion.info.refs_0_, bf16[656,1024]{1,0:T(8,128)(2,1)} %pad_maximum_fusion.refs_1_.refs_2_.refs_3_, bf16[656,1024]{1,0:T(8,128)(2,1)} %pad_maximum_fusion.refs_1_.refs_2_.refs_3_, bf16[304,1280]{1,0:T(8,128)(2,1)} %copy-done.4, ...), custom_call_target="tpu_custom_call" | custom-call | flops 18432000000 | bytes 8388608 | tf_op jit(solution)/shard_map/attend/pallas_call | solution.py:223
  67.8 0.9 copy-done.16
  68.7 1.0 collective-permute-start.10
  69.7 2.2 %collective-permute-start.11 = (bf16[304,1280]{1,0:T(8,128)(2,1)}, bf16[304,1280]{1,0:T(8,128)(2,1)S(1)}, u32[]{:S(2)}, u32[]{:S(2)}) collective-permute-start(bf16[304,1280]{1,0:T(8,128)(2,1)} %copy-done.16), channel_id=1, source_target_pairs={{0,224},{8,232},{16,240},{24,248},{32,0},{40,8},{48,16},{56,24},{6... | collective-permute-start | bytes 2334728 | tf_op jit(solution)/shard_map/ppermute | solution.py:380
  71.9 5.7 %attend.6 = (f32[640,1024]{1,0:T(8,128)}, f32[40,1024]{1,0:T(8,128)}, f32[8,128]{1,0:T(8,128)}) custom-call(f32[8,128]{1,0:T(8,128)} %get-tuple-element.94.refs_0_, bf16[656,1024]{1,0:T(8,128)(2,1)} %pad_maximum_fusion.refs_1_.refs_2_.refs_3_, ...), custom_call_target="tpu_custom_call", output_to_operand_aliasing={{0}: (5, {}), {1}: (6, {})} | custom-call | flops 12288000000 | bytes 8388608 | tf_op jit(solution)/shard_map/attend/pallas_call | solution.py:223
  77.6 12.5 %collective-permute-done.14 = bf16[640,640]{1,0:T(8,128)(2,1)} collective-permute-done((bf16[640,640]{1,0:T(8,128)(2,1)}, bf16[640,640]{1,0:T(8,128)(2,1)}, u32[]{:S(2)}, u32[]{:S(2)}) %collective-permute-start.14) | collective-permute-done | bytes 819232 | tf_op jit(solution)/shard_map/ppermute | solution.py:387
  90.1 0.7 slice.23
  90.9 1.2 collective-permute-start.17
  92.1 1.9 %collective-permute-start.15 = (bf16[160,1280]{1,0:T(8,128)(2,1)S(1)}, bf16[160,1280]{1,0:T(8,128)(2,1)}, u32[]{:S(2)}, u32[]{:S(2)}) collective-permute-start(bf16[160,1280]{1,0:T(8,128)(2,1)S(1)} %slice.21), channel_id=1, source_target_pairs={{0,32},{8,40},{16,48},{24,56},{32,64},{40,72},{48,80},{56,88},{64,... | collective-permute-start | bytes 1228808 | tf_op jit(solution)/shard_map/ppermute | solution.py:380
  94.0 1.4 collective-permute-start.16
  95.4 5.8 %attend.7 = (f32[640,1024]{1,0:T(8,128)}, f32[40,1024]{1,0:T(8,128)}, f32[8,128]{1,0:T(8,128)}) custom-call(f32[8,128]{1,0:T(8,128)} %get-tuple-element.98.refs_0_, bf16[656,1024]{1,0:T(8,128)(2,1)} %pad_maximum_fusion.refs_1_.refs_2_.refs_3_, ...), custom_call_target="tpu_custom_call", output_to_operand_aliasing={{0}: (5, {}), {1}: (6, {})} | custom-call | flops 12288000000 | bytes 8388608 | tf_op jit(solution)/shard_map/attend/pallas_call | solution.py:223
  101.2 5.0 %collective-permute-done.15.refs_4_ = bf16[160,1280]{1,0:T(8,128)(2,1)} collective-permute-done((bf16[160,1280]{1,0:T(8,128)(2,1)S(1)}, bf16[160,1280]{1,0:T(8,128)(2,1)}, u32[]{:S(2)}, u32[]{:S(2)}) %collective-permute-start.15) | collective-permute-done | bytes 409632 | tf_op jit(solution)/shard_map/ppermute | solution.py:380
  106.3 5.3 %attend.8 = (bf16[656,256]{1,0:T(8,128)(2,1)}, bf16[656,256]{1,0:T(8,128)(2,1)}) custom-call(s32[10]{0:T(128)} %pad_add_fusion.info.refs_0_, f32[8,128]{1,0:T(8,128)} %get-tuple-element.108.refs_1_, bf16[656,1024]{1,0:T(8,128)(2,1)} %pad_maximum_fusion.refs_1_.refs_2_.refs_3_, bf16[656,1024]{1,0:T(8,128)(2,1)} %pad_maximum_fusion.refs_1_.refs_2_.refs_3_, ...), custom_call_target="tpu_custom_call" | custom-call | flops 6144000000 | bytes 8388608 | tf_op jit(solution)/shard_map/attend/pallas_call | solution.py:223
  111.6 0.5 collective-permute-start.20
  112.2 0.4 collective-permute-start.22
  112.6 0.8 collective-permute-done.18.refs_1_
  113.4 0.7 copy-done.5
  114.1 2.0 %merge.3 = bf16[656,256]{1,0:T(8,128)(2,1)} custom-call(bf16[656,256]{1,0:T(8,128)(2,1)} %get-tuple-element.106.refs_0_, bf16[656,256]{1,0:T(8,128)(2,1)} %copy-done.5), custom_call_target="tpu_custom_call" | custom-call | bytes 1024 | tf_op jit(solution)/shard_map/merge/pallas_call | solution.py:282
  116.2 2.1 %collective-permute-start.19 = (bf16[656,256]{1,0:T(8,128)(2,1)}, bf16[656,256]{1,0:T(8,128)(2,1)}, u32[]{:S(2)}, u32[]{:S(2)}) collective-permute-start(bf16[656,256]{1,0:T(8,128)(2,1)} %merge.3), channel_id=1, source_target_pairs={{0,16},{8,24},{16,0},{24,8},{32,48},{40,56},{48,32},{56,40},{64,80... | collective-permute-start | bytes 1007624 | tf_op jit(solution)/shard_map/ppermute | solution.py:383
  118.3 5.3 %attend.9 = (bf16[656,256]{1,0:T(8,128)(2,1)}, bf16[656,256]{1,0:T(8,128)(2,1)}) custom-call(s32[10]{0:T(128)} %pad_add_fusion.info.refs_0_, f32[8,128]{1,0:T(8,128)} %get-tuple-element.108.refs_1_, bf16[656,1024]{1,0:T(8,128)(2,1)} %pad_maximum_fusion.refs_1_.refs_2_.refs_3_, bf16[656,1024]{1,0:T(8,128)(2,1)} %pad_maximum_fusion.refs_1_.refs_2_.refs_3_, ...), custom_call_target="tpu_custom_call" | custom-call | flops 6144000000 | bytes 8388608 | tf_op jit(solution)/shard_map/attend/pallas_call | solution.py:223
  123.6 4.3 %collective-permute-done.19.refs_1_ = bf16[656,256]{1,0:T(8,128)(2,1)} collective-permute-done((bf16[656,256]{1,0:T(8,128)(2,1)}, bf16[656,256]{1,0:T(8,128)(2,1)}, u32[]{:S(2)}, u32[]{:S(2)}) %collective-permute-start.19) | collective-permute-done | bytes 335904 | tf_op jit(solution)/shard_map/ppermute | solution.py:383
  127.9 2.0 %merge.4.refs_0_ = bf16[656,256]{1,0:T(8,128)(2,1)} custom-call(bf16[656,256]{1,0:T(8,128)(2,1)} %get-tuple-element.109.refs_0_, bf16[656,256]{1,0:T(8,128)(2,1)} %collective-permute-done.19.refs_1_), custom_call_target="tpu_custom_call" | custom-call | bytes 1024 | tf_op jit(solution)/shard_map/merge/pallas_call | solution.py:282
  129.9 2.1 %merge.5 = bf16[256,640]{1,0:T(8,128)(2,1)} custom-call(bf16[656,256]{1,0:T(8,128)(2,1)} %merge.4.refs_0_, bf16[656,256]{1,0:T(8,128)(2,1)} %collective-permute-done.23.refs_1_), custom_call_target="tpu_custom_call" | custom-call | bytes 1024 | tf_op jit(solution)/shard_map/merge/pallas_call | solution.py:282
  132.0 0.8 collective-permute-start.26
  132.9 2.4 %collective-permute-start.25 = (bf16[256,640]{1,0:T(8,128)(2,1)}, bf16[256,640]{1,0:T(8,128)(2,1)S(1)}, u32[]{:S(2)}, u32[]{:S(2)}) collective-permute-start(bf16[256,640]{1,0:T(8,128)(2,1)} %merge.5), channel_id=1, source_target_pairs={{0,6},{1,7},{2,0},{3,1},{4,2},{5,3},{6,4},{7,5},{8,14},{9,15},{10,... | collective-permute-start | bytes 983048 | tf_op jit(solution)/shard_map/ppermute | solution.py:387
  135.3 0.9 collective-permute-start.24
  136.1 1.5 fusion.2
  137.6 0.5 fusion.1
  138.1 1.5 broadcast_select_fusion
  139.6 4.2 %collective-permute-done.26 = bf16[256,640]{1,0:T(8,128)(2,1)S(1)} collective-permute-done((bf16[256,640]{1,0:T(8,128)(2,1)}, bf16[256,640]{1,0:T(8,128)(2,1)S(1)}, u32[]{:S(2)}, u32[]{:S(2)}) %collective-permute-start.26) | collective-permute-done | bytes 327712 | tf_op jit(solution)/shard_map/ppermute | solution.py:387
  143.9 0.5 fusion.3
  144.4 1.6 %fusion.4 = f32[256,640]{1,0:T(8,128)S(1)} fusion(bf16[256,640]{1,0:T(8,128)(2,1)S(1)} %collective-permute-done.26, bf16[640,640]{1,0:T(8,128)(2,1)} %collective-permute-done.20), kind=kOutput, calls=%fused_computation.20 | convolution fusion | flops 209715200 | bytes 1802240 | tf_op jit(solution)/shard_map/dot_general | solution.py:469
  146.2 2.7 %collective-permute-done.25 = bf16[256,640]{1,0:T(8,128)(2,1)S(1)} collective-permute-done((bf16[256,640]{1,0:T(8,128)(2,1)}, bf16[256,640]{1,0:T(8,128)(2,1)S(1)}, u32[]{:S(2)}, u32[]{:S(2)}) %collective-permute-start.25) | collective-permute-done | bytes 327712 | tf_op jit(solution)/shard_map/ppermute | solution.py:387
  148.8 0.5 fusion.6
  149.3 0.5 fusion.5
  149.9 0.5 fusion.8
  150.4 3.7 %collective-permute-start.27 = (bf16[256,640]{1,0:T(8,128)(2,1)S(1)}, bf16[256,640]{1,0:T(8,128)(2,1)S(1)}, u32[]{:S(2)}, u32[]{:S(2)}) collective-permute-start(bf16[256,640]{1,0:T(8,128)(2,1)S(1)} %add_convert_fusion.1), channel_id=1, source_target_pairs={{0,1},{1,0},{2,3},{3,2},{4,5},{5,4},{6,7},{7,6},{8,9},{9,8},{10,11... | collective-permute-start | bytes 983048 | tf_op jit(solution)/shard_map/ppermute | solution.py:488
  154.2 0.5 fusion.7
  154.6 4.6 %collective-permute-done.27 = bf16[256,640]{1,0:T(8,128)(2,1)S(1)} collective-permute-done((bf16[256,640]{1,0:T(8,128)(2,1)S(1)}, bf16[256,640]{1,0:T(8,128)(2,1)S(1)}, u32[]{:S(2)}, u32[]{:S(2)}) %collective-permute-start.27) | collective-permute-done | bytes 327712 | tf_op jit(solution)/shard_map/ppermute | solution.py:488
  159.2 0.9 add_convert_fusion
  (74 shorter events, 1.6 us)
Async XLA Ops:
  0.0 10.5 %copy-start.17 = (s32[256]{0:T(256)S(1)}, s32[256]{0:T(256)}, u32[]{:S(2)}) copy-start(s32[256]{0:T(256)} %param.12) | copy-start | bytes 3076
  0.0 10.5 %copy-start.6 = (bf16[256,640]{1,0:T(8,128)(2,1)S(1)}, bf16[256,640]{1,0:T(8,128)(2,1)}, u32[]{:S(2)}) copy-start(bf16[256,640]{1,0:T(8,128)(2,1)} %param.10) | copy-start | bytes 983044
  0.0 10.6 %copy-start.7 = (bf16[256,640]{1,0:T(8,128)(2,1)S(1)}, bf16[256,640]{1,0:T(8,128)(2,1)}, u32[]{:S(2)}) copy-start(bf16[256,640]{1,0:T(8,128)(2,1)} %param.11) | copy-start | bytes 983044
  2.0 28.7 %all-to-all-start = ((bf16[8,32,1280]{2,1,0:T(8,128)(2,1)}), bf16[8,32,1280]{2,1,0:T(8,128)(2,1)S(1)}, u32[]{:S(2)}, u32[]{:S(2)}) async-start(bf16[8,32,1280]{2,1,0:T(8,128)(2,1)} %pad_maximum_fusion.2), calls=%async_computation | async-start | bytes 1310720 | tf_op jit(solution)/shard_map/all_to_all | solution.py:399
  10.6 3.6 %copy-start.8 = (bf16[256,640]{1,0:T(8,128)(2,1)S(1)}, bf16[256,640]{1,0:T(8,128)(2,1)}, u32[]{:S(2)}) copy-start(bf16[256,640]{1,0:T(8,128)(2,1)} %param.9) | copy-start | bytes 983044
  10.7 6.1 %copy-start.14 = (s32[4]{0:T(128)S(1)}, s32[4]{0:T(128)}, u32[]{:S(2)}) copy-start(s32[4]{0:T(128)} %param.16) | copy-start | bytes 52
  10.7 6.1 %copy-start.15 = (s32[4]{0:T(128)S(1)}, s32[4]{0:T(128)}, u32[]{:S(2)}) copy-start(s32[4]{0:T(128)} %param.15) | copy-start | bytes 52
  11.0 12.9 %copy-start.4 = (bf16[304,1280]{1,0:T(8,128)(2,1)}, bf16[304,1280]{1,0:T(8,128)(2,1)S(1)}, u32[]{:S(2)}) copy-start(bf16[304,1280]{1,0:T(8,128)(2,1)S(1)} %pad_maximum_fusion.1.refs_3_) | copy-start | bytes 2334724
  11.0 33.0 %collective-permute-start.6 = (bf16[304,1280]{1,0:T(8,128)(2,1)S(1)}, bf16[304,1280]{1,0:T(8,128)(2,1)}, u32[]{:S(2)}, u32[]{:S(2)}) collective-permute-start(bf16[304,1280]{1,0:T(8,128)(2,1)S(1)} %pad_maximum_fusion.1.refs_3_), channel_id=1, source_target_pairs={{0,224},{8,232},{16,240},{24,248},{32,0},{40,8},{48,16},{56,24},{6... | collective-permute-start | bytes 2334728 | tf_op jit(solution)/shard_map/ppermute | solution.py:380
  14.3 30.6 %collective-permute-start = (bf16[304,1280]{1,0:T(8,128)(2,1)S(1)}, bf16[304,1280]{1,0:T(8,128)(2,1)}, u32[]{:S(2)}, u32[]{:S(2)}) collective-permute-start(bf16[304,1280]{1,0:T(8,128)(2,1)S(1)} %pad_maximum_fusion.1.refs_3_), channel_id=1, source_target_pairs={{0,32},{8,40},{16,48},{24,56},{32,64},{40,72},{48,80},{56,88},{64,... | collective-permute-start | bytes 2334728 | tf_op jit(solution)/shard_map/ppermute | solution.py:380
  14.5 9.4 %collective-permute-start.2 = (bf16[656,256]{1,0:T(8,128)(2,1)S(1)}, bf16[656,256]{1,0:T(8,128)(2,1)}, u32[]{:S(2)}, u32[]{:S(2)}) collective-permute-start(bf16[656,256]{1,0:T(8,128)(2,1)S(1)} %pad_maximum_fusion.3), channel_id=1, source_target_pairs={{0,8},{8,0},{16,24},{24,16},{32,40},{40,32},{48,56},{56,48},{64,72... | collective-permute-start | bytes 1007624 | tf_op jit(solution)/shard_map/ppermute | solution.py:383
  14.6 11.9 %collective-permute-start.1 = (bf16[656,256]{1,0:T(8,128)(2,1)S(1)}, bf16[656,256]{1,0:T(8,128)(2,1)}, u32[]{:S(2)}, u32[]{:S(2)}) collective-permute-start(bf16[656,256]{1,0:T(8,128)(2,1)S(1)} %pad_maximum_fusion.3), channel_id=1, source_target_pairs={{0,16},{8,24},{16,0},{24,8},{32,48},{40,56},{48,32},{56,40},{64,80... | collective-permute-start | bytes 1007624 | tf_op jit(solution)/shard_map/ppermute | solution.py:383
  30.7 0.8 copy-start.1
  33.4 3.4 %collective-permute-start.3 = (bf16[32,1280]{1,0:T(8,128)(2,1)}, bf16[32,1280]{1,0:T(8,128)(2,1)S(1)}, u32[]{:S(2)}, u32[]{:S(2)}) collective-permute-start(bf16[32,1280]{1,0:T(8,128)(2,1)} %get-tuple-element.76), channel_id=1, source_target_pairs={{0,8},{8,0},{16,24},{24,16},{32,40},{40,32},{48,56},{56,48},{64,72... | collective-permute-start | bytes 245768 | tf_op jit(solution)/shard_map/ppermute | solution.py:383
  33.4 6.6 %collective-permute-start.4 = (bf16[32,1280]{1,0:T(8,128)(2,1)}, bf16[32,1280]{1,0:T(8,128)(2,1)S(1)}, u32[]{:S(2)}, u32[]{:S(2)}) collective-permute-start(bf16[32,1280]{1,0:T(8,128)(2,1)} %get-tuple-element.77), channel_id=1, source_target_pairs={{0,16},{8,24},{16,0},{24,8},{32,48},{40,56},{48,32},{56,40},{64,80... | collective-permute-start | bytes 245768 | tf_op jit(solution)/shard_map/ppermute | solution.py:383
  35.5 6.1 %collective-permute-start.5 = (bf16[32,1280]{1,0:T(8,128)(2,1)}, bf16[32,1280]{1,0:T(8,128)(2,1)S(1)}, u32[]{:S(2)}, u32[]{:S(2)}) collective-permute-start(bf16[32,1280]{1,0:T(8,128)(2,1)} %get-tuple-element.78), channel_id=1, source_target_pairs={{0,24},{8,16},{16,8},{24,0},{32,56},{40,48},{48,40},{56,32},{64,88... | collective-permute-start | bytes 245768 | tf_op jit(solution)/shard_map/ppermute | solution.py:383
  36.8 4.9 %copy-start.11 = (bf16[32,1280]{1,0:T(8,128)(2,1)}, bf16[32,1280]{1,0:T(8,128)(2,1)S(1)}, u32[]{:S(2)}) copy-start(bf16[32,1280]{1,0:T(8,128)(2,1)S(1)} %collective-permute-done.3.refs_1_) | copy-start | bytes 245764
  40.0 1.7 %copy-start.12 = (bf16[32,1280]{1,0:T(8,128)(2,1)}, bf16[32,1280]{1,0:T(8,128)(2,1)S(1)}, u32[]{:S(2)}) copy-start(bf16[32,1280]{1,0:T(8,128)(2,1)S(1)} %collective-permute-done.4.refs_2_) | copy-start | bytes 245764
  41.7 0.6 copy-start.13
  46.5 6.5 %collective-permute-start.9 = (bf16[656,256]{1,0:T(8,128)(2,1)}, bf16[656,256]{1,0:T(8,128)(2,1)S(1)}, u32[]{:S(2)}, u32[]{:S(2)}) collective-permute-start(bf16[656,256]{1,0:T(8,128)(2,1)} %collective-permute-done.1), channel_id=1, source_target_pairs={{0,8},{8,0},{16,24},{24,16},{32,40},{40,32},{48,56},{56,48},{64,72... | collective-permute-start | bytes 1007624 | tf_op jit(solution)/shard_map/ppermute | solution.py:383
  46.5 21.3 %collective-permute-start.7 = (bf16[304,1280]{1,0:T(8,128)(2,1)}, bf16[304,1280]{1,0:T(8,128)(2,1)}, u32[]{:S(2)}, u32[]{:S(2)}) collective-permute-start(bf16[304,1280]{1,0:T(8,128)(2,1)} %get-tuple-element.84.refs_4_), channel_id=1, source_target_pairs={{0,32},{8,40},{16,48},{24,56},{32,64},{40,72},{48,80},{56,88},{64,... | collective-permute-start | bytes 2334728 | tf_op jit(solution)/shard_map/ppermute | solution.py:380
  47.7 20.1 %collective-permute-start.8 = (bf16[304,1280]{1,0:T(8,128)(2,1)}, bf16[304,1280]{1,0:T(8,128)(2,1)S(1)}, u32[]{:S(2)}, u32[]{:S(2)}) collective-permute-start(bf16[304,1280]{1,0:T(8,128)(2,1)} %get-tuple-element.85.refs_5_), channel_id=1, source_target_pairs={{0,224},{8,232},{16,240},{24,248},{32,0},{40,8},{48,16},{56,24},{6... | collective-permute-start | bytes 2334728 | tf_op jit(solution)/shard_map/ppermute | solution.py:380
  49.7 27.9 %collective-permute-start.12 = (bf16[640,640]{1,0:T(8,128)(2,1)}, bf16[640,640]{1,0:T(8,128)(2,1)S(1)}, u32[]{:S(2)}, u32[]{:S(2)}) collective-permute-start(bf16[640,640]{1,0:T(8,128)(2,1)} %get-tuple-element.91), channel_id=1, source_target_pairs={{0,2},{1,3},{2,4},{3,5},{4,6},{5,7},{6,0},{7,1},{8,10},{9,11},{10,... | collective-permute-start | bytes 2457608 | tf_op jit(solution)/shard_map/ppermute | solution.py:387
  51.3 26.4 %collective-permute-start.13 = (bf16[640,640]{1,0:T(8,128)(2,1)}, bf16[640,640]{1,0:T(8,128)(2,1)S(1)}, u32[]{:S(2)}, u32[]{:S(2)}) collective-permute-start(bf16[640,640]{1,0:T(8,128)(2,1)} %get-tuple-element.92), channel_id=1, source_target_pairs={{0,6},{1,7},{2,0},{3,1},{4,2},{5,3},{6,4},{7,5},{8,14},{9,15},{10,... | collective-permute-start | bytes 2457608 | tf_op jit(solution)/shard_map/ppermute | solution.py:387
  52.9 37.2 %collective-permute-start.14 = (bf16[640,640]{1,0:T(8,128)(2,1)}, bf16[640,640]{1,0:T(8,128)(2,1)}, u32[]{:S(2)}, u32[]{:S(2)}) collective-permute-start(bf16[640,640]{1,0:T(8,128)(2,1)} %get-tuple-element.93), channel_id=1, source_target_pairs={{0,4},{1,5},{2,6},{3,7},{4,0},{5,1},{6,2},{7,3},{8,12},{9,13},{10,... | collective-permute-start | bytes 2457608 | tf_op jit(solution)/shard_map/ppermute | solution.py:387
  67.8 0.9 copy-start.16
  68.7 21.5 %collective-permute-start.10 = (bf16[304,1280]{1,0:T(8,128)(2,1)}, bf16[304,1280]{1,0:T(8,128)(2,1)S(1)}, u32[]{:S(2)}, u32[]{:S(2)}) collective-permute-start(bf16[304,1280]{1,0:T(8,128)(2,1)} %collective-permute-done.7.refs_3_.refs_7_), channel_id=1, source_target_pairs={{0,32},{8,40},{16,48},{24,56},{32,64},{40,72},{48,80},{56,88},{64,... | collective-permute-start | bytes 2334728 | tf_op jit(solution)/shard_map/ppermute | solution.py:380
  69.7 20.4 %collective-permute-start.11 = (bf16[304,1280]{1,0:T(8,128)(2,1)}, bf16[304,1280]{1,0:T(8,128)(2,1)S(1)}, u32[]{:S(2)}, u32[]{:S(2)}) collective-permute-start(bf16[304,1280]{1,0:T(8,128)(2,1)} %copy-done.16), channel_id=1, source_target_pairs={{0,224},{8,232},{16,240},{24,248},{32,0},{40,8},{48,16},{56,24},{6... | collective-permute-start | bytes 2334728 | tf_op jit(solution)/shard_map/ppermute | solution.py:380
  90.1 5.3 %copy-start.9 = (bf16[304,1280]{1,0:T(8,128)(2,1)}, bf16[304,1280]{1,0:T(8,128)(2,1)S(1)}, u32[]{:S(2)}) copy-start(bf16[304,1280]{1,0:T(8,128)(2,1)S(1)} %collective-permute-done.10.refs_3_.refs_6_) | copy-start | bytes 2334724
  90.1 5.3 %copy-start.10 = (bf16[304,1280]{1,0:T(8,128)(2,1)}, bf16[304,1280]{1,0:T(8,128)(2,1)S(1)}, u32[]{:S(2)}) copy-start(bf16[304,1280]{1,0:T(8,128)(2,1)S(1)} %collective-permute-done.11.refs_4_.refs_10_) | copy-start | bytes 2334724
  90.9 10.3 %collective-permute-start.17 = (bf16[32,1280]{1,0:T(8,128)(2,1)}, bf16[32,1280]{1,0:T(8,128)(2,1)}, u32[]{:S(2)}, u32[]{:S(2)}) collective-permute-start(bf16[32,1280]{1,0:T(8,128)(2,1)} %slice.23), channel_id=1, source_target_pairs={{0,64},{8,72},{16,80},{24,88},{32,96},{40,104},{48,112},{56,120},{... | collective-permute-start | bytes 245768 | tf_op jit(solution)/shard_map/ppermute | solution.py:380
  92.1 14.2 %collective-permute-start.15 = (bf16[160,1280]{1,0:T(8,128)(2,1)S(1)}, bf16[160,1280]{1,0:T(8,128)(2,1)}, u32[]{:S(2)}, u32[]{:S(2)}) collective-permute-start(bf16[160,1280]{1,0:T(8,128)(2,1)S(1)} %slice.21), channel_id=1, source_target_pairs={{0,32},{8,40},{16,48},{24,56},{32,64},{40,72},{48,80},{56,88},{64,... | collective-permute-start | bytes 1228808 | tf_op jit(solution)/shard_map/ppermute | solution.py:380
  94.0 12.3 %collective-permute-start.16 = (bf16[176,1280]{1,0:T(8,128)(2,1)S(1)}, bf16[176,1280]{1,0:T(8,128)(2,1)}, u32[]{:S(2)}, u32[]{:S(2)}) collective-permute-start(bf16[176,1280]{1,0:T(8,128)(2,1)S(1)} %slice.22), channel_id=1, source_target_pairs={{0,224},{8,232},{16,240},{24,248},{32,0},{40,8},{48,16},{56,24},{6... | collective-permute-start | bytes 1351688 | tf_op jit(solution)/shard_map/ppermute | solution.py:380
  111.6 1.9 %collective-permute-start.18 = (bf16[656,256]{1,0:T(8,128)(2,1)}, bf16[656,256]{1,0:T(8,128)(2,1)S(1)}, u32[]{:S(2)}, u32[]{:S(2)}) collective-permute-start(bf16[656,256]{1,0:T(8,128)(2,1)} %get-tuple-element.107), channel_id=1, source_target_pairs={{0,8},{8,0},{16,24},{24,16},{32,40},{40,32},{48,56},{56,48},{64,72... | collective-permute-start | bytes 1007624 | tf_op jit(solution)/shard_map/ppermute | solution.py:383
  111.6 12.0 %collective-permute-start.20 = (bf16[640,640]{1,0:T(8,128)(2,1)S(1)}, bf16[640,640]{1,0:T(8,128)(2,1)}, u32[]{:S(2)}, u32[]{:S(2)}) collective-permute-start(bf16[640,640]{1,0:T(8,128)(2,1)S(1)} %collective-permute-done.12), channel_id=1, source_target_pairs={{0,8},{8,0},{16,24},{24,16},{32,40},{40,32},{48,56},{56,48},{64,72... | collective-permute-start | bytes 2457608 | tf_op jit(solution)/shard_map/ppermute | solution.py:383
  112.1 11.5 %collective-permute-start.21 = (bf16[640,640]{1,0:T(8,128)(2,1)}, bf16[640,640]{1,0:T(8,128)(2,1)}, u32[]{:S(2)}, u32[]{:S(2)}) collective-permute-start(bf16[640,640]{1,0:T(8,128)(2,1)} %collective-permute-done.14), channel_id=1, source_target_pairs={{0,8},{8,0},{16,24},{24,16},{32,40},{40,32},{48,56},{56,48},{64,72... | collective-permute-start | bytes 2457608 | tf_op jit(solution)/shard_map/ppermute | solution.py:383
  112.2 11.4 %collective-permute-start.22 = (bf16[640,640]{1,0:T(8,128)(2,1)S(1)}, bf16[640,640]{1,0:T(8,128)(2,1)S(1)}, u32[]{:S(2)}, u32[]{:S(2)}) collective-permute-start(bf16[640,640]{1,0:T(8,128)(2,1)S(1)} %collective-permute-done.13), channel_id=1, source_target_pairs={{0,8},{8,0},{16,24},{24,16},{32,40},{40,32},{48,56},{56,48},{64,72... | collective-permute-start | bytes 2457608 | tf_op jit(solution)/shard_map/ppermute | solution.py:383
  113.4 0.7 copy-start.5
  116.2 11.7 %collective-permute-start.19 = (bf16[656,256]{1,0:T(8,128)(2,1)}, bf16[656,256]{1,0:T(8,128)(2,1)}, u32[]{:S(2)}, u32[]{:S(2)}) collective-permute-start(bf16[656,256]{1,0:T(8,128)(2,1)} %merge.3), channel_id=1, source_target_pairs={{0,16},{8,24},{16,0},{24,8},{32,48},{40,56},{48,32},{56,40},{64,80... | collective-permute-start | bytes 1007624 | tf_op jit(solution)/shard_map/ppermute | solution.py:383
  123.5 12.6 %copy-start.3 = (bf16[640,640]{1,0:T(8,128)(2,1)S(1)}, bf16[640,640]{1,0:T(8,128)(2,1)}, u32[]{:S(2)}) copy-start(bf16[640,640]{1,0:T(8,128)(2,1)} %get-tuple-element.118) | copy-start | bytes 2457604
  123.6 6.4 %collective-permute-start.23 = (bf16[656,256]{1,0:T(8,128)(2,1)}, bf16[656,256]{1,0:T(8,128)(2,1)}, u32[]{:S(2)}, u32[]{:S(2)}) collective-permute-start(bf16[656,256]{1,0:T(8,128)(2,1)} %get-tuple-element.116), channel_id=1, source_target_pairs={{0,8},{8,0},{16,24},{24,16},{32,40},{40,32},{48,56},{56,48},{64,72... | collective-permute-start | bytes 1007624 | tf_op jit(solution)/shard_map/ppermute | solution.py:383
  129.9 7.7 %copy-start.2 = (bf16[640,640]{1,0:T(8,128)(2,1)S(1)}, bf16[640,640]{1,0:T(8,128)(2,1)}, u32[]{:S(2)}) copy-start(bf16[640,640]{1,0:T(8,128)(2,1)} %get-tuple-element.117) | copy-start | bytes 2457604
  132.0 5.6 %copy-start = (bf16[256,640]{1,0:T(8,128)(2,1)S(1)}, bf16[256,640]{1,0:T(8,128)(2,1)}, u32[]{:S(2)}) copy-start(bf16[256,640]{1,0:T(8,128)(2,1)} %merge.5) | copy-start | bytes 983044
  132.0 11.8 %collective-permute-start.26 = (bf16[256,640]{1,0:T(8,128)(2,1)}, bf16[256,640]{1,0:T(8,128)(2,1)S(1)}, u32[]{:S(2)}, u32[]{:S(2)}) collective-permute-start(bf16[256,640]{1,0:T(8,128)(2,1)} %merge.5), channel_id=1, source_target_pairs={{0,2},{1,3},{2,4},{3,5},{4,6},{5,7},{6,0},{7,1},{8,10},{9,11},{10,... | collective-permute-start | bytes 983048 | tf_op jit(solution)/shard_map/ppermute | solution.py:387
  132.9 15.9 %collective-permute-start.25 = (bf16[256,640]{1,0:T(8,128)(2,1)}, bf16[256,640]{1,0:T(8,128)(2,1)S(1)}, u32[]{:S(2)}, u32[]{:S(2)}) collective-permute-start(bf16[256,640]{1,0:T(8,128)(2,1)} %merge.5), channel_id=1, source_target_pairs={{0,6},{1,7},{2,0},{3,1},{4,2},{5,3},{6,4},{7,5},{8,14},{9,15},{10,... | collective-permute-start | bytes 983048 | tf_op jit(solution)/shard_map/ppermute | solution.py:387
  135.3 14.6 %collective-permute-start.24 = (bf16[256,640]{1,0:T(8,128)(2,1)}, bf16[256,640]{1,0:T(8,128)(2,1)S(1)}, u32[]{:S(2)}, u32[]{:S(2)}) collective-permute-start(bf16[256,640]{1,0:T(8,128)(2,1)} %merge.5), channel_id=1, source_target_pairs={{0,4},{1,5},{2,6},{3,7},{4,0},{5,1},{6,2},{7,3},{8,12},{9,13},{10,... | collective-permute-start | bytes 983048 | tf_op jit(solution)/shard_map/ppermute | solution.py:387
  150.4 8.8 %collective-permute-start.27 = (bf16[256,640]{1,0:T(8,128)(2,1)S(1)}, bf16[256,640]{1,0:T(8,128)(2,1)S(1)}, u32[]{:S(2)}, u32[]{:S(2)}) collective-permute-start(bf16[256,640]{1,0:T(8,128)(2,1)S(1)} %add_convert_fusion.1), channel_id=1, source_target_pairs={{0,1},{1,0},{2,3},{3,2},{4,5},{5,4},{6,7},{7,6},{8,9},{9,8},{10,11... | collective-permute-start | bytes 983048 | tf_op jit(solution)/shard_map/ppermute | solution.py:488

commit v5 on v4

--- a/solution.py
+++ b/solution.py
@@ -387,7 +387,7 @@
         return lax.ppermute(item, "heads", steps)
 
     marks = jnp.pad(frame_ids.astype(jnp.bfloat16)[None], ((0, 15), (0, 2 * feat - rows)))
-    mid = rows // 2
+    mid = 3 * rows // 8
     part = ctx_keys.shape[1] // depth
     both = jnp.concatenate([key_rows, value_rows], axis=1)
     own = jnp.concatenate([both[:mid], jnp.zeros((part, 2 * feat), both.dtype), both[mid:], marks])
@@ -409,7 +409,7 @@
         return lax.dynamic_update_slice(item, piece, (mid, 0))
 
     def halves(item):
-        return [(item, 0, mid), (item, mid + part, mid)], item
+        return [(item, 0, mid), (item, mid + part, rows - mid)], item
 
     def carried(item):
         return item, mid, part
@@ -442,7 +442,7 @@
     *state, token = attention_call(
         query_plane, [halves(ahead), halves(behind)], state, None, False, token
     )
-    far = [(far_ahead, 0, mid), (far_behind, part, mid)], far_behind
+    far = [(far_ahead, 0, mid), (far_behind, part, rows - mid)], far_behind
     ctx = [
         (far_ahead, mid, part),
         carried(ahead),

time: 161 us -> 162 us (level)
  starting transfers between devices: 44.7 us -> 42.1 us
  waiting for transfers between devices: 47.1 us -> 48.9 us
    ppermute x1, starting transfers between devices: 3.71 us -> 0.61 us  [shards(): lax.ppermute(other.astype(jnp.bfloat16), 'heads', [(i, i ^ 1) for i in ra...]
    ppermute x1, waiting for transfers between devices: 4.59 us -> 7.01 us  [shards(): lax.ppermute(other.astype(jnp.bfloat16), 'heads', [(i, i ^ 1) for i in ra...]
  transfers between devices with their start and end apart: 29 -> 29, of which waited for: 13 -> 15; matrix products, arithmetic and copies ran while one was open for 7% -> 7% of each run, Pallas kernels for 26% -> 26%
where the time goes in v5:
time: 162 us; the launch traced here: 160 us
  waiting for transfers between devices  48.9 us (30%)
  Pallas kernels  48.3 us (30%)
  starting transfers between devices  42.1 us (26%)
  other arithmetic  8.08 us (5%)
  local copies, waits for them, and re-layouts  6.36 us (4%)
  matrix products  5.81 us (4%)
    pallas_call x5, Pallas kernels, attention_call(): pl.pallas_call(functools.partial(attention_kernel, len(found), layout, fi...  32.3 us
    ppermute x6, waiting for transfers between devices, shift_y(): return lax.ppermute(item, 'heads', steps)  19.1 us
    ppermute x9, starting transfers between devices, shift(): return lax.ppermute(item, 'blk', steps)  14 us
    ppermute x12, waiting for transfers between devices, swap(): return lax.ppermute(item, 'blk', [(i, i ^ mask) for i in range(blk_count)])  12.6 us
    ppermute x6, starting transfers between devices, shift_y(): return lax.ppermute(item, 'heads', steps)  10.1 us
    ppermute x12, starting transfers between devices, swap(): return lax.ppermute(item, 'blk', [(i, i ^ mask) for i in range(blk_count)])  8.83 us
    all_to_all x1, starting transfers between devices, shards(): pieces = lax.all_to_all(slot, 'blk', 0, 0, axis_index_groups=columns)  8.47 us
    ppermute x1, waiting for transfers between devices, shards(): lax.ppermute(other.astype(jnp.bfloat16), 'heads', [(i, i ^ 1) for i in ra...  7.01 us
  transfers between devices with their start and end apart: 29, of which 15 were waited for; matrix products, arithmetic and copies ran while one was open for 7% of the time, Pallas kernels for 26%

profile of v5, /device:TPU:2, one launch (start us, length us, event | category | flops | bytes accessed | tf_op | source)
XLA Modules:
  0.0 159.9 jit_solution(12193987688077050140)
XLA Ops:
  0.0 2.0 %pad_maximum_fusion.2 = bf16[8,32,1280]{2,1,0:T(8,128)(2,1)} fusion(bf16[8,32,640]{2,1,0:T(8,128)(2,1)} %bitcast.23, bf16[8,32,640]{2,1,0:T(8,128)(2,1)} %bitcast.24), kind=kLoop, calls=%fused_computation.4 | loop fusion | flops 1310720 | bytes 1310720 | tf_op jit(solution)/shard_map/concatenate | solution.py:395
  2.0 8.5 %all-to-all-start = ((bf16[8,32,1280]{2,1,0:T(8,128)(2,1)}), bf16[8,32,1280]{2,1,0:T(8,128)(2,1)S(1)}, u32[]{:S(2)}, u32[]{:S(2)}) async-start(bf16[8,32,1280]{2,1,0:T(8,128)(2,1)} %pad_maximum_fusion.2), calls=%async_computation | async-start | bytes 1310720 | tf_op jit(solution)/shard_map/all_to_all | solution.py:399
  10.7 0.5 copy-done.17
  11.5 3.3 %collective-permute-start.6 = (bf16[304,1280]{1,0:T(8,128)(2,1)S(1)}, bf16[304,1280]{1,0:T(8,128)(2,1)}, u32[]{:S(2)}, u32[]{:S(2)}) collective-permute-start(bf16[304,1280]{1,0:T(8,128)(2,1)S(1)} %pad_maximum_fusion.1.refs_3_), channel_id=1, source_target_pairs={{0,224},{8,232},{16,240},{24,248},{32,0},{40,8},{48,16},{56,24},{6... | collective-permute-start | bytes 2334728 | tf_op jit(solution)/shard_map/ppermute | solution.py:380
  15.1 2.2 %collective-permute-start.1 = (bf16[656,256]{1,0:T(8,128)(2,1)S(1)}, bf16[656,256]{1,0:T(8,128)(2,1)}, u32[]{:S(2)}, u32[]{:S(2)}) collective-permute-start(bf16[656,256]{1,0:T(8,128)(2,1)S(1)} %pad_maximum_fusion.3), channel_id=1, source_target_pairs={{0,16},{8,24},{16,0},{24,8},{32,48},{40,56},{48,32},{56,40},{64,80... | collective-permute-start | bytes 1007624 | tf_op jit(solution)/shard_map/ppermute | solution.py:383
  17.4 0.7 pad_add_fusion.info.refs_0_
  18.0 6.5 %columns.1 = (bf16[640,640]{1,0:T(8,128)(2,1)}, bf16[640,640]{1,0:T(8,128)(2,1)}, bf16[640,640]{1,0:T(8,128)(2,1)}, bf16[640,640]{1,0:T(8,128)(2,1)}, bf16[640,640]{1,0:T(8,128)(2,1)}) custom-call(s32[10]{0:T(128)} %pad_add_fusion.info.refs_0_, bf16[640,5120]{1,0:T(8,128)(2,1)} %in_ref.1), custom_call_target="tpu_custom_call" | custom-call | bytes 8192000 | tf_op jit(solution)/shard_map/columns/pallas_call | solution.py:305
  24.5 2.6 %collective-permute-done.1 = bf16[656,256]{1,0:T(8,128)(2,1)} collective-permute-done((bf16[656,256]{1,0:T(8,128)(2,1)S(1)}, bf16[656,256]{1,0:T(8,128)(2,1)}, u32[]{:S(2)}, u32[]{:S(2)}) %collective-permute-start.1) | collective-permute-done | bytes 335904 | tf_op jit(solution)/shard_map/ppermute | solution.py:383
  27.1 3.7 %all-to-all-done.in_ref = bf16[8,32,1280]{2,1,0:T(8,128)(2,1)S(1)} async-done(((bf16[8,32,1280]{2,1,0:T(8,128)(2,1)}), bf16[8,32,1280]{2,1,0:T(8,128)(2,1)S(1)}, u32[]{:S(2)}, u32[]{:S(2)}) %all-to-all-start) | async-done | bytes 655392 | tf_op jit(solution)/shard_map/all_to_all | solution.py:399
  30.7 0.8 copy-done.1
  31.6 1.8 %offer.1 = (bf16[32,1280]{1,0:T(8,128)(2,1)}, bf16[32,1280]{1,0:T(8,128)(2,1)}, bf16[32,1280]{1,0:T(8,128)(2,1)}, bf16[32,1280]{1,0:T(8,128)(2,1)}) custom-call(s32[10]{0:T(128)} %pad_add_fusion.info.refs_0_, bf16[8,32,1280]{2,1,0:T(8,128)(2,1)} %copy-done.1), custom_call_target="tpu_custom_call" | custom-call | tf_op jit(solution)/shard_map/offer/pallas_call | solution.py:329
  33.4 2.1 %collective-permute-start.4 = (bf16[32,1280]{1,0:T(8,128)(2,1)}, bf16[32,1280]{1,0:T(8,128)(2,1)S(1)}, u32[]{:S(2)}, u32[]{:S(2)}) collective-permute-start(bf16[32,1280]{1,0:T(8,128)(2,1)} %get-tuple-element.77), channel_id=1, source_target_pairs={{0,16},{8,24},{16,0},{24,8},{32,48},{40,56},{48,32},{56,40},{64,80... | collective-permute-start | bytes 245768 | tf_op jit(solution)/shard_map/ppermute | solution.py:383
  35.5 1.2 collective-permute-start.5
  36.8 3.2 %collective-permute-done.4.refs_2_ = bf16[32,1280]{1,0:T(8,128)(2,1)S(1)} collective-permute-done((bf16[32,1280]{1,0:T(8,128)(2,1)}, bf16[32,1280]{1,0:T(8,128)(2,1)S(1)}, u32[]{:S(2)}, u32[]{:S(2)}) %collective-permute-start.4) | collective-permute-done | bytes 81952 | tf_op jit(solution)/shard_map/ppermute | solution.py:383
  40.0 1.7 %collective-permute-done.5.refs_3_ = bf16[32,1280]{1,0:T(8,128)(2,1)S(1)} collective-permute-done((bf16[32,1280]{1,0:T(8,128)(2,1)}, bf16[32,1280]{1,0:T(8,128)(2,1)S(1)}, u32[]{:S(2)}, u32[]{:S(2)}) %collective-permute-start.5) | collective-permute-done | bytes 81952 | tf_op jit(solution)/shard_map/ppermute | solution.py:383
  41.7 0.6 copy-done.13
  42.3 1.7 %choose.1.refs_8_ = bf16[32,1280]{1,0:T(8,128)(2,1)} custom-call(s32[10]{0:T(128)} %pad_add_fusion.info.refs_0_, bf16[32,1280]{1,0:T(8,128)(2,1)} %get-tuple-element.75.refs_0_, bf16[32,1280]{1,0:T(8,128)(2,1)} %copy-done.11, bf16[32,1280]{1,0:T(8,128)(2,1)} %copy-done.12, bf16[32,1280]{1,0:T(8,128)(2,1)} %copy-done.13), custom_call_target="tpu_custom_call" | custom-call | tf_op jit(solution)/shard_map/choose/pallas_call | solution.py:354
  44.0 0.9 collective-permute-done
  44.9 1.6 constant_dynamic-update-slice_fusion.2
  46.5 1.2 collective-permute-start.7
  47.7 2.0 %collective-permute-start.8 = (bf16[304,1280]{1,0:T(8,128)(2,1)}, bf16[304,1280]{1,0:T(8,128)(2,1)}, u32[]{:S(2)}, u32[]{:S(2)}) collective-permute-start(bf16[304,1280]{1,0:T(8,128)(2,1)} %get-tuple-element.85.refs_5_), channel_id=1, source_target_pairs={{0,224},{8,232},{16,240},{24,248},{32,0},{40,8},{48,16},{56,24},{6... | collective-permute-start | bytes 2334728 | tf_op jit(solution)/shard_map/ppermute | solution.py:380
  49.7 1.6 collective-permute-start.12
  51.3 1.7 %collective-permute-start.13 = (bf16[640,640]{1,0:T(8,128)(2,1)}, bf16[640,640]{1,0:T(8,128)(2,1)S(1)}, u32[]{:S(2)}, u32[]{:S(2)}) collective-permute-start(bf16[640,640]{1,0:T(8,128)(2,1)} %get-tuple-element.92), channel_id=1, source_target_pairs={{0,6},{1,7},{2,0},{3,1},{4,2},{5,3},{6,4},{7,5},{8,14},{9,15},{10,... | collective-permute-start | bytes 2457608 | tf_op jit(solution)/shard_map/ppermute | solution.py:387
  52.9 2.0 %collective-permute-start.14 = (bf16[640,640]{1,0:T(8,128)(2,1)}, bf16[640,640]{1,0:T(8,128)(2,1)}, u32[]{:S(2)}, u32[]{:S(2)}) collective-permute-start(bf16[640,640]{1,0:T(8,128)(2,1)} %get-tuple-element.93), channel_id=1, source_target_pairs={{0,4},{1,5},{2,6},{3,7},{4,0},{5,1},{6,2},{7,3},{8,12},{9,13},{10,... | collective-permute-start | bytes 2457608 | tf_op jit(solution)/shard_map/ppermute | solution.py:387
  54.9 2.3 %pad_maximum_fusion.refs_1_.refs_2_.refs_3_ = bf16[656,1024]{1,0:T(8,128)(2,1)} fusion(bf16[656,256]{1,0:T(8,128)(2,1)} %collective-permute-done.2, bf16[16,256]{1,0:T(8,128)(2,1)S(1)} %pad_slice_fusion, bf16[640,256]{1,0:T(8,128)(2,1)S(1)} %bitcast.22, bf16[656,256]{1,0:T(8,128)(2,1)S(1)} %collective-permute-done.9, bf16[656,256]{1,0:T(8,128)(2,1)} %collective-permute-done.1), kind=kLoop, calls=%fused_computation | loop fusion | flops 6717440 | bytes 2686976 | tf_op jit(solution)/shard_map/concatenate | solution.py:422
  57.3 10.2 %attend.5 = (f32[640,1024]{1,0:T(8,128)}, f32[40,1024]{1,0:T(8,128)}, f32[8,128]{1,0:T(8,128)}) custom-call(s32[10]{0:T(128)} %pad_add_fusion.info.refs_0_, bf16[656,1024]{1,0:T(8,128)(2,1)} %pad_maximum_fusion.refs_1_.refs_2_.refs_3_, bf16[656,1024]{1,0:T(8,128)(2,1)} %pad_maximum_fusion.refs_1_.refs_2_.refs_3_, bf16[304,1280]{1,0:T(8,128)(2,1)} %copy-done.4, ...), custom_call_target="tpu_custom_call" | custom-call | flops 18432000000 | bytes 8388608 | tf_op jit(solution)/shard_map/attend/pallas_call | solution.py:223
  67.7 0.9 copy-done.16
  68.9 2.9 %collective-permute-start.11 = (bf16[304,1280]{1,0:T(8,128)(2,1)}, bf16[304,1280]{1,0:T(8,128)(2,1)S(1)}, u32[]{:S(2)}, u32[]{:S(2)}) collective-permute-start(bf16[304,1280]{1,0:T(8,128)(2,1)} %collective-permute-done.8.refs_4_.refs_9_), channel_id=1, source_target_pairs={{0,224},{8,232},{16,240},{24,248},{32,0},{40,8},{48,16},{56,24},{6... | collective-permute-start | bytes 2334728 | tf_op jit(solution)/shard_map/ppermute | solution.py:380
  71.8 5.7 %attend.6 = (f32[640,1024]{1,0:T(8,128)}, f32[40,1024]{1,0:T(8,128)}, f32[8,128]{1,0:T(8,128)}) custom-call(f32[8,128]{1,0:T(8,128)} %get-tuple-element.94.refs_0_, bf16[656,1024]{1,0:T(8,128)(2,1)} %pad_maximum_fusion.refs_1_.refs_2_.refs_3_, ...), custom_call_target="tpu_custom_call", output_to_operand_aliasing={{0}: (5, {}), {1}: (6, {})} | custom-call | flops 12288000000 | bytes 8388608 | tf_op jit(solution)/shard_map/attend/pallas_call | solution.py:223
  77.5 12.6 %collective-permute-done.14 = bf16[640,640]{1,0:T(8,128)(2,1)} collective-permute-done((bf16[640,640]{1,0:T(8,128)(2,1)}, bf16[640,640]{1,0:T(8,128)(2,1)}, u32[]{:S(2)}, u32[]{:S(2)}) %collective-permute-start.14) | collective-permute-done | bytes 819232 | tf_op jit(solution)/shard_map/ppermute | solution.py:387
  90.1 0.7 slice.23
  90.9 0.9 collective-permute-start.17
  91.8 2.0 %collective-permute-start.15 = (bf16[128,1280]{1,0:T(8,128)(2,1)S(1)}, bf16[128,1280]{1,0:T(8,128)(2,1)}, u32[]{:S(2)}, u32[]{:S(2)}) collective-permute-start(bf16[128,1280]{1,0:T(8,128)(2,1)S(1)} %slice.21), channel_id=1, source_target_pairs={{0,32},{8,40},{16,48},{24,56},{32,64},{40,72},{48,80},{56,88},{64,... | collective-permute-start | bytes 983048 | tf_op jit(solution)/shard_map/ppermute | solution.py:380
  93.9 1.3 collective-permute-start.16
  95.2 5.8 %attend.7 = (f32[640,1024]{1,0:T(8,128)}, f32[40,1024]{1,0:T(8,128)}, f32[8,128]{1,0:T(8,128)}) custom-call(f32[8,128]{1,0:T(8,128)} %get-tuple-element.98.refs_0_, bf16[656,1024]{1,0:T(8,128)(2,1)} %pad_maximum_fusion.refs_1_.refs_2_.refs_3_, ...), custom_call_target="tpu_custom_call", output_to_operand_aliasing={{0}: (5, {}), {1}: (6, {})} | custom-call | flops 12288000000 | bytes 8388608 | tf_op jit(solution)/shard_map/attend/pallas_call | solution.py:223
  100.9 3.6 %collective-permute-done.15.refs_4_ = bf16[128,1280]{1,0:T(8,128)(2,1)} collective-permute-done((bf16[128,1280]{1,0:T(8,128)(2,1)S(1)}, bf16[128,1280]{1,0:T(8,128)(2,1)}, u32[]{:S(2)}, u32[]{:S(2)}) %collective-permute-start.15) | collective-permute-done | bytes 327712 | tf_op jit(solution)/shard_map/ppermute | solution.py:380
  104.5 1.8 %collective-permute-done.16.refs_5_ = bf16[208,1280]{1,0:T(8,128)(2,1)} collective-permute-done((bf16[208,1280]{1,0:T(8,128)(2,1)S(1)}, bf16[208,1280]{1,0:T(8,128)(2,1)}, u32[]{:S(2)}, u32[]{:S(2)}) %collective-permute-start.16) | collective-permute-done | bytes 532512 | tf_op jit(solution)/shard_map/ppermute | solution.py:380
  106.3 5.3 %attend.8 = (bf16[656,256]{1,0:T(8,128)(2,1)}, bf16[656,256]{1,0:T(8,128)(2,1)}) custom-call(s32[10]{0:T(128)} %pad_add_fusion.info.refs_0_, f32[8,128]{1,0:T(8,128)} %get-tuple-element.108.refs_1_, bf16[656,1024]{1,0:T(8,128)(2,1)} %pad_maximum_fusion.refs_1_.refs_2_.refs_3_, bf16[656,1024]{1,0:T(8,128)(2,1)} %pad_maximum_fusion.refs_1_.refs_2_.refs_3_, ...), custom_call_target="tpu_custom_call" | custom-call | flops 6144000000 | bytes 8388608 | tf_op jit(solution)/shard_map/attend/pallas_call | solution.py:223
  111.6 0.5 collective-permute-start.20
  112.6 0.8 collective-permute-done.18.refs_1_
  113.5 0.8 copy-done.6
  114.2 2.0 %merge.3 = bf16[656,256]{1,0:T(8,128)(2,1)} custom-call(bf16[656,256]{1,0:T(8,128)(2,1)} %get-tuple-element.106.refs_0_, bf16[656,256]{1,0:T(8,128)(2,1)} %copy-done.6), custom_call_target="tpu_custom_call" | custom-call | bytes 1024 | tf_op jit(solution)/shard_map/merge/pallas_call | solution.py:282
  116.2 2.1 %collective-permute-start.19 = (bf16[656,256]{1,0:T(8,128)(2,1)}, bf16[656,256]{1,0:T(8,128)(2,1)}, u32[]{:S(2)}, u32[]{:S(2)}) collective-permute-start(bf16[656,256]{1,0:T(8,128)(2,1)} %merge.3), channel_id=1, source_target_pairs={{0,16},{8,24},{16,0},{24,8},{32,48},{40,56},{48,32},{56,40},{64,80... | collective-permute-start | bytes 1007624 | tf_op jit(solution)/shard_map/ppermute | solution.py:383
  118.3 5.3 %attend.9 = (bf16[656,256]{1,0:T(8,128)(2,1)}, bf16[656,256]{1,0:T(8,128)(2,1)}) custom-call(s32[10]{0:T(128)} %pad_add_fusion.info.refs_0_, f32[8,128]{1,0:T(8,128)} %get-tuple-element.108.refs_1_, bf16[656,1024]{1,0:T(8,128)(2,1)} %pad_maximum_fusion.refs_1_.refs_2_.refs_3_, bf16[656,1024]{1,0:T(8,128)(2,1)} %pad_maximum_fusion.refs_1_.refs_2_.refs_3_, ...), custom_call_target="tpu_custom_call" | custom-call | flops 6144000000 | bytes 8388608 | tf_op jit(solution)/shard_map/attend/pallas_call | solution.py:223
  123.7 4.3 %collective-permute-done.19.refs_1_ = bf16[656,256]{1,0:T(8,128)(2,1)} collective-permute-done((bf16[656,256]{1,0:T(8,128)(2,1)}, bf16[656,256]{1,0:T(8,128)(2,1)}, u32[]{:S(2)}, u32[]{:S(2)}) %collective-permute-start.19) | collective-permute-done | bytes 335904 | tf_op jit(solution)/shard_map/ppermute | solution.py:383
  128.0 2.0 %merge.4.refs_0_ = bf16[656,256]{1,0:T(8,128)(2,1)} custom-call(bf16[656,256]{1,0:T(8,128)(2,1)} %get-tuple-element.109.refs_0_, bf16[656,256]{1,0:T(8,128)(2,1)} %collective-permute-done.19.refs_1_), custom_call_target="tpu_custom_call" | custom-call | bytes 1024 | tf_op jit(solution)/shard_map/merge/pallas_call | solution.py:282
  130.0 2.1 %merge.5 = bf16[256,640]{1,0:T(8,128)(2,1)} custom-call(bf16[656,256]{1,0:T(8,128)(2,1)} %merge.4.refs_0_, bf16[656,256]{1,0:T(8,128)(2,1)} %collective-permute-done.23.refs_1_), custom_call_target="tpu_custom_call" | custom-call | bytes 1024 | tf_op jit(solution)/shard_map/merge/pallas_call | solution.py:282
  132.1 1.3 collective-permute-start.26
  133.4 2.0 %collective-permute-start.25 = (bf16[256,640]{1,0:T(8,128)(2,1)}, bf16[256,640]{1,0:T(8,128)(2,1)S(1)}, u32[]{:S(2)}, u32[]{:S(2)}) collective-permute-start(bf16[256,640]{1,0:T(8,128)(2,1)} %merge.5), channel_id=1, source_target_pairs={{0,6},{1,7},{2,0},{3,1},{4,2},{5,3},{6,4},{7,5},{8,14},{9,15},{10,... | collective-permute-start | bytes 983048 | tf_op jit(solution)/shard_map/ppermute | solution.py:387
  135.3 1.7 %collective-permute-start.24 = (bf16[256,640]{1,0:T(8,128)(2,1)}, bf16[256,640]{1,0:T(8,128)(2,1)S(1)}, u32[]{:S(2)}, u32[]{:S(2)}) collective-permute-start(bf16[256,640]{1,0:T(8,128)(2,1)} %merge.5), channel_id=1, source_target_pairs={{0,4},{1,5},{2,6},{3,7},{4,0},{5,1},{6,2},{7,3},{8,12},{9,13},{10,... | collective-permute-start | bytes 983048 | tf_op jit(solution)/shard_map/ppermute | solution.py:387
  137.0 1.5 fusion.1
  138.5 0.5 fusion
  139.0 1.5 broadcast_select_fusion
  140.5 2.7 %collective-permute-done.26 = bf16[256,640]{1,0:T(8,128)(2,1)S(1)} collective-permute-done((bf16[256,640]{1,0:T(8,128)(2,1)}, bf16[256,640]{1,0:T(8,128)(2,1)S(1)}, u32[]{:S(2)}, u32[]{:S(2)}) %collective-permute-start.26) | collective-permute-done | bytes 327712 | tf_op jit(solution)/shard_map/ppermute | solution.py:387
  143.2 0.5 fusion.2
  143.8 1.6 %fusion.3 = f32[256,640]{1,0:T(8,128)S(1)} fusion(bf16[256,640]{1,0:T(8,128)(2,1)S(1)} %collective-permute-done.26, bf16[640,640]{1,0:T(8,128)(2,1)} %collective-permute-done.20), kind=kOutput, calls=%fused_computation.19 | convolution fusion | flops 209715200 | bytes 1802240 | tf_op jit(solution)/shard_map/dot_general | solution.py:469
  145.5 3.4 %collective-permute-done.25 = bf16[256,640]{1,0:T(8,128)(2,1)S(1)} collective-permute-done((bf16[256,640]{1,0:T(8,128)(2,1)}, bf16[256,640]{1,0:T(8,128)(2,1)S(1)}, u32[]{:S(2)}, u32[]{:S(2)}) %collective-permute-start.25) | collective-permute-done | bytes 327712 | tf_op jit(solution)/shard_map/ppermute | solution.py:387
  148.9 0.5 fusion.5
  149.3 0.5 fusion.4
  150.4 0.5 fusion.7
  150.9 0.6 collective-permute-start.27
  151.6 0.5 fusion.6
  152.0 7.0 %collective-permute-done.27 = bf16[256,640]{1,0:T(8,128)(2,1)S(1)} collective-permute-done((bf16[256,640]{1,0:T(8,128)(2,1)S(1)}, bf16[256,640]{1,0:T(8,128)(2,1)S(1)}, u32[]{:S(2)}, u32[]{:S(2)}) %collective-permute-start.27) | collective-permute-done | bytes 327712 | tf_op jit(solution)/shard_map/ppermute | solution.py:488
  159.0 0.9 add_convert_fusion
  (75 shorter events, 2.8 us)
Async XLA Ops:
  0.0 10.5 %copy-start.7 = (bf16[256,640]{1,0:T(8,128)(2,1)S(1)}, bf16[256,640]{1,0:T(8,128)(2,1)}, u32[]{:S(2)}) copy-start(bf16[256,640]{1,0:T(8,128)(2,1)} %param.10) | copy-start | bytes 983044
  0.0 10.6 %copy-start.8 = (bf16[256,640]{1,0:T(8,128)(2,1)S(1)}, bf16[256,640]{1,0:T(8,128)(2,1)}, u32[]{:S(2)}) copy-start(bf16[256,640]{1,0:T(8,128)(2,1)} %param.11) | copy-start | bytes 983044
  2.0 28.7 %all-to-all-start = ((bf16[8,32,1280]{2,1,0:T(8,128)(2,1)}), bf16[8,32,1280]{2,1,0:T(8,128)(2,1)S(1)}, u32[]{:S(2)}, u32[]{:S(2)}) async-start(bf16[8,32,1280]{2,1,0:T(8,128)(2,1)} %pad_maximum_fusion.2), calls=%async_computation | async-start | bytes 1310720 | tf_op jit(solution)/shard_map/all_to_all | solution.py:399
  10.5 0.7 copy-start.17
  10.6 4.2 %copy-start.9 = (bf16[256,640]{1,0:T(8,128)(2,1)S(1)}, bf16[256,640]{1,0:T(8,128)(2,1)}, u32[]{:S(2)}) copy-start(bf16[256,640]{1,0:T(8,128)(2,1)} %param.9) | copy-start | bytes 983044
  11.2 6.2 %copy-start.14 = (s32[4]{0:T(128)S(1)}, s32[4]{0:T(128)}, u32[]{:S(2)}) copy-start(s32[4]{0:T(128)} %param.16) | copy-start | bytes 52
  11.2 6.2 %copy-start.15 = (s32[4]{0:T(128)S(1)}, s32[4]{0:T(128)}, u32[]{:S(2)}) copy-start(s32[4]{0:T(128)} %param.15) | copy-start | bytes 52
  11.5 13.0 %copy-start.4 = (bf16[304,1280]{1,0:T(8,128)(2,1)}, bf16[304,1280]{1,0:T(8,128)(2,1)S(1)}, u32[]{:S(2)}) copy-start(bf16[304,1280]{1,0:T(8,128)(2,1)S(1)} %pad_maximum_fusion.1.refs_3_) | copy-start | bytes 2334724
  11.5 32.4 %collective-permute-start.6 = (bf16[304,1280]{1,0:T(8,128)(2,1)S(1)}, bf16[304,1280]{1,0:T(8,128)(2,1)}, u32[]{:S(2)}, u32[]{:S(2)}) collective-permute-start(bf16[304,1280]{1,0:T(8,128)(2,1)S(1)} %pad_maximum_fusion.1.refs_3_), channel_id=1, source_target_pairs={{0,224},{8,232},{16,240},{24,248},{32,0},{40,8},{48,16},{56,24},{6... | collective-permute-start | bytes 2334728 | tf_op jit(solution)/shard_map/ppermute | solution.py:380
  14.8 30.1 %collective-permute-start = (bf16[304,1280]{1,0:T(8,128)(2,1)S(1)}, bf16[304,1280]{1,0:T(8,128)(2,1)}, u32[]{:S(2)}, u32[]{:S(2)}) collective-permute-start(bf16[304,1280]{1,0:T(8,128)(2,1)S(1)} %pad_maximum_fusion.1.refs_3_), channel_id=1, source_target_pairs={{0,32},{8,40},{16,48},{24,56},{32,64},{40,72},{48,80},{56,88},{64,... | collective-permute-start | bytes 2334728 | tf_op jit(solution)/shard_map/ppermute | solution.py:380
  15.0 9.5 %collective-permute-start.2 = (bf16[656,256]{1,0:T(8,128)(2,1)S(1)}, bf16[656,256]{1,0:T(8,128)(2,1)}, u32[]{:S(2)}, u32[]{:S(2)}) collective-permute-start(bf16[656,256]{1,0:T(8,128)(2,1)S(1)} %pad_maximum_fusion.3), channel_id=1, source_target_pairs={{0,8},{8,0},{16,24},{24,16},{32,40},{40,32},{48,56},{56,48},{64,72... | collective-permute-start | bytes 1007624 | tf_op jit(solution)/shard_map/ppermute | solution.py:383
  15.1 11.9 %collective-permute-start.1 = (bf16[656,256]{1,0:T(8,128)(2,1)S(1)}, bf16[656,256]{1,0:T(8,128)(2,1)}, u32[]{:S(2)}, u32[]{:S(2)}) collective-permute-start(bf16[656,256]{1,0:T(8,128)(2,1)S(1)} %pad_maximum_fusion.3), channel_id=1, source_target_pairs={{0,16},{8,24},{16,0},{24,8},{32,48},{40,56},{48,32},{56,40},{64,80... | collective-permute-start | bytes 1007624 | tf_op jit(solution)/shard_map/ppermute | solution.py:383
  30.7 0.8 copy-start.1
  33.4 3.4 %collective-permute-start.3 = (bf16[32,1280]{1,0:T(8,128)(2,1)}, bf16[32,1280]{1,0:T(8,128)(2,1)S(1)}, u32[]{:S(2)}, u32[]{:S(2)}) collective-permute-start(bf16[32,1280]{1,0:T(8,128)(2,1)} %get-tuple-element.76), channel_id=1, source_target_pairs={{0,8},{8,0},{16,24},{24,16},{32,40},{40,32},{48,56},{56,48},{64,72... | collective-permute-start | bytes 245768 | tf_op jit(solution)/shard_map/ppermute | solution.py:383
  33.4 6.6 %collective-permute-start.4 = (bf16[32,1280]{1,0:T(8,128)(2,1)}, bf16[32,1280]{1,0:T(8,128)(2,1)S(1)}, u32[]{:S(2)}, u32[]{:S(2)}) collective-permute-start(bf16[32,1280]{1,0:T(8,128)(2,1)} %get-tuple-element.77), channel_id=1, source_target_pairs={{0,16},{8,24},{16,0},{24,8},{32,48},{40,56},{48,32},{56,40},{64,80... | collective-permute-start | bytes 245768 | tf_op jit(solution)/shard_map/ppermute | solution.py:383
  35.5 6.1 %collective-permute-start.5 = (bf16[32,1280]{1,0:T(8,128)(2,1)}, bf16[32,1280]{1,0:T(8,128)(2,1)S(1)}, u32[]{:S(2)}, u32[]{:S(2)}) collective-permute-start(bf16[32,1280]{1,0:T(8,128)(2,1)} %get-tuple-element.78), channel_id=1, source_target_pairs={{0,24},{8,16},{16,8},{24,0},{32,56},{40,48},{48,40},{56,32},{64,88... | collective-permute-start | bytes 245768 | tf_op jit(solution)/shard_map/ppermute | solution.py:383
  36.8 4.9 %copy-start.11 = (bf16[32,1280]{1,0:T(8,128)(2,1)}, bf16[32,1280]{1,0:T(8,128)(2,1)S(1)}, u32[]{:S(2)}) copy-start(bf16[32,1280]{1,0:T(8,128)(2,1)S(1)} %collective-permute-done.3.refs_1_) | copy-start | bytes 245764
  40.0 1.7 %copy-start.12 = (bf16[32,1280]{1,0:T(8,128)(2,1)}, bf16[32,1280]{1,0:T(8,128)(2,1)S(1)}, u32[]{:S(2)}) copy-start(bf16[32,1280]{1,0:T(8,128)(2,1)S(1)} %collective-permute-done.4.refs_2_) | copy-start | bytes 245764
  41.7 0.6 copy-start.13
  46.5 6.5 %collective-permute-start.9 = (bf16[656,256]{1,0:T(8,128)(2,1)}, bf16[656,256]{1,0:T(8,128)(2,1)S(1)}, u32[]{:S(2)}, u32[]{:S(2)}) collective-permute-start(bf16[656,256]{1,0:T(8,128)(2,1)} %collective-permute-done.1), channel_id=1, source_target_pairs={{0,8},{8,0},{16,24},{24,16},{32,40},{40,32},{48,56},{56,48},{64,72... | collective-permute-start | bytes 1007624 | tf_op jit(solution)/shard_map/ppermute | solution.py:383
  46.5 21.2 %collective-permute-start.7 = (bf16[304,1280]{1,0:T(8,128)(2,1)}, bf16[304,1280]{1,0:T(8,128)(2,1)S(1)}, u32[]{:S(2)}, u32[]{:S(2)}) collective-permute-start(bf16[304,1280]{1,0:T(8,128)(2,1)} %get-tuple-element.84.refs_4_), channel_id=1, source_target_pairs={{0,32},{8,40},{16,48},{24,56},{32,64},{40,72},{48,80},{56,88},{64,... | collective-permute-start | bytes 2334728 | tf_op jit(solution)/shard_map/ppermute | solution.py:380
  47.7 20.0 %collective-permute-start.8 = (bf16[304,1280]{1,0:T(8,128)(2,1)}, bf16[304,1280]{1,0:T(8,128)(2,1)}, u32[]{:S(2)}, u32[]{:S(2)}) collective-permute-start(bf16[304,1280]{1,0:T(8,128)(2,1)} %get-tuple-element.85.refs_5_), channel_id=1, source_target_pairs={{0,224},{8,232},{16,240},{24,248},{32,0},{40,8},{48,16},{56,24},{6... | collective-permute-start | bytes 2334728 | tf_op jit(solution)/shard_map/ppermute | solution.py:380
  49.7 27.8 %collective-permute-start.12 = (bf16[640,640]{1,0:T(8,128)(2,1)}, bf16[640,640]{1,0:T(8,128)(2,1)S(1)}, u32[]{:S(2)}, u32[]{:S(2)}) collective-permute-start(bf16[640,640]{1,0:T(8,128)(2,1)} %get-tuple-element.91), channel_id=1, source_target_pairs={{0,2},{1,3},{2,4},{3,5},{4,6},{5,7},{6,0},{7,1},{8,10},{9,11},{10,... | collective-permute-start | bytes 2457608 | tf_op jit(solution)/shard_map/ppermute | solution.py:387
  51.3 26.2 %collective-permute-start.13 = (bf16[640,640]{1,0:T(8,128)(2,1)}, bf16[640,640]{1,0:T(8,128)(2,1)S(1)}, u32[]{:S(2)}, u32[]{:S(2)}) collective-permute-start(bf16[640,640]{1,0:T(8,128)(2,1)} %get-tuple-element.92), channel_id=1, source_target_pairs={{0,6},{1,7},{2,0},{3,1},{4,2},{5,3},{6,4},{7,5},{8,14},{9,15},{10,... | collective-permute-start | bytes 2457608 | tf_op jit(solution)/shard_map/ppermute | solution.py:387
  52.9 37.2 %collective-permute-start.14 = (bf16[640,640]{1,0:T(8,128)(2,1)}, bf16[640,640]{1,0:T(8,128)(2,1)}, u32[]{:S(2)}, u32[]{:S(2)}) collective-permute-start(bf16[640,640]{1,0:T(8,128)(2,1)} %get-tuple-element.93), channel_id=1, source_target_pairs={{0,4},{1,5},{2,6},{3,7},{4,0},{5,1},{6,2},{7,3},{8,12},{9,13},{10,... | collective-permute-start | bytes 2457608 | tf_op jit(solution)/shard_map/ppermute | solution.py:387
  67.7 0.9 copy-start.16
  68.5 21.6 %collective-permute-start.10 = (bf16[304,1280]{1,0:T(8,128)(2,1)}, bf16[304,1280]{1,0:T(8,128)(2,1)S(1)}, u32[]{:S(2)}, u32[]{:S(2)}) collective-permute-start(bf16[304,1280]{1,0:T(8,128)(2,1)} %copy-done.16), channel_id=1, source_target_pairs={{0,32},{8,40},{16,48},{24,56},{32,64},{40,72},{48,80},{56,88},{64,... | collective-permute-start | bytes 2334728 | tf_op jit(solution)/shard_map/ppermute | solution.py:380
  68.9 21.2 %collective-permute-start.11 = (bf16[304,1280]{1,0:T(8,128)(2,1)}, bf16[304,1280]{1,0:T(8,128)(2,1)S(1)}, u32[]{:S(2)}, u32[]{:S(2)}) collective-permute-start(bf16[304,1280]{1,0:T(8,128)(2,1)} %collective-permute-done.8.refs_4_.refs_9_), channel_id=1, source_target_pairs={{0,224},{8,232},{16,240},{24,248},{32,0},{40,8},{48,16},{56,24},{6... | collective-permute-start | bytes 2334728 | tf_op jit(solution)/shard_map/ppermute | solution.py:380
  90.1 5.0 %copy-start.10 = (bf16[304,1280]{1,0:T(8,128)(2,1)}, bf16[304,1280]{1,0:T(8,128)(2,1)S(1)}, u32[]{:S(2)}) copy-start(bf16[304,1280]{1,0:T(8,128)(2,1)S(1)} %collective-permute-done.10.refs_3_.refs_6_) | copy-start | bytes 2334724
  90.1 5.0 %copy-start.5 = (bf16[304,1280]{1,0:T(8,128)(2,1)}, bf16[304,1280]{1,0:T(8,128)(2,1)S(1)}, u32[]{:S(2)}) copy-start(bf16[304,1280]{1,0:T(8,128)(2,1)S(1)} %collective-permute-done.11.refs_4_.refs_10_) | copy-start | bytes 2334724
  90.9 10.1 %collective-permute-start.17 = (bf16[32,1280]{1,0:T(8,128)(2,1)}, bf16[32,1280]{1,0:T(8,128)(2,1)}, u32[]{:S(2)}, u32[]{:S(2)}) collective-permute-start(bf16[32,1280]{1,0:T(8,128)(2,1)} %slice.23), channel_id=1, source_target_pairs={{0,64},{8,72},{16,80},{24,88},{32,96},{40,104},{48,112},{56,120},{... | collective-permute-start | bytes 245768 | tf_op jit(solution)/shard_map/ppermute | solution.py:380
  91.8 12.7 %collective-permute-start.15 = (bf16[128,1280]{1,0:T(8,128)(2,1)S(1)}, bf16[128,1280]{1,0:T(8,128)(2,1)}, u32[]{:S(2)}, u32[]{:S(2)}) collective-permute-start(bf16[128,1280]{1,0:T(8,128)(2,1)S(1)} %slice.21), channel_id=1, source_target_pairs={{0,32},{8,40},{16,48},{24,56},{32,64},{40,72},{48,80},{56,88},{64,... | collective-permute-start | bytes 983048 | tf_op jit(solution)/shard_map/ppermute | solution.py:380
  93.9 12.5 %collective-permute-start.16 = (bf16[208,1280]{1,0:T(8,128)(2,1)S(1)}, bf16[208,1280]{1,0:T(8,128)(2,1)}, u32[]{:S(2)}, u32[]{:S(2)}) collective-permute-start(bf16[208,1280]{1,0:T(8,128)(2,1)S(1)} %slice.22), channel_id=1, source_target_pairs={{0,224},{8,232},{16,240},{24,248},{32,0},{40,8},{48,16},{56,24},{6... | collective-permute-start | bytes 1597448 | tf_op jit(solution)/shard_map/ppermute | solution.py:380
  111.6 1.9 %collective-permute-start.18 = (bf16[656,256]{1,0:T(8,128)(2,1)}, bf16[656,256]{1,0:T(8,128)(2,1)S(1)}, u32[]{:S(2)}, u32[]{:S(2)}) collective-permute-start(bf16[656,256]{1,0:T(8,128)(2,1)} %get-tuple-element.107), channel_id=1, source_target_pairs={{0,8},{8,0},{16,24},{24,16},{32,40},{40,32},{48,56},{56,48},{64,72... | collective-permute-start | bytes 1007624 | tf_op jit(solution)/shard_map/ppermute | solution.py:383
  111.6 12.0 %collective-permute-start.20 = (bf16[640,640]{1,0:T(8,128)(2,1)S(1)}, bf16[640,640]{1,0:T(8,128)(2,1)}, u32[]{:S(2)}, u32[]{:S(2)}) collective-permute-start(bf16[640,640]{1,0:T(8,128)(2,1)S(1)} %collective-permute-done.12), channel_id=1, source_target_pairs={{0,8},{8,0},{16,24},{24,16},{32,40},{40,32},{48,56},{56,48},{64,72... | collective-permute-start | bytes 2457608 | tf_op jit(solution)/shard_map/ppermute | solution.py:383
  112.1 11.5 %collective-permute-start.21 = (bf16[640,640]{1,0:T(8,128)(2,1)}, bf16[640,640]{1,0:T(8,128)(2,1)}, u32[]{:S(2)}, u32[]{:S(2)}) collective-permute-start(bf16[640,640]{1,0:T(8,128)(2,1)} %collective-permute-done.14), channel_id=1, source_target_pairs={{0,8},{8,0},{16,24},{24,16},{32,40},{40,32},{48,56},{56,48},{64,72... | collective-permute-start | bytes 2457608 | tf_op jit(solution)/shard_map/ppermute | solution.py:383
  112.2 11.5 %collective-permute-start.22 = (bf16[640,640]{1,0:T(8,128)(2,1)S(1)}, bf16[640,640]{1,0:T(8,128)(2,1)S(1)}, u32[]{:S(2)}, u32[]{:S(2)}) collective-permute-start(bf16[640,640]{1,0:T(8,128)(2,1)S(1)} %collective-permute-done.13), channel_id=1, source_target_pairs={{0,8},{8,0},{16,24},{24,16},{32,40},{40,32},{48,56},{56,48},{64,72... | collective-permute-start | bytes 2457608 | tf_op jit(solution)/shard_map/ppermute | solution.py:383
  113.5 0.8 copy-start.6
  116.2 11.7 %collective-permute-start.19 = (bf16[656,256]{1,0:T(8,128)(2,1)}, bf16[656,256]{1,0:T(8,128)(2,1)}, u32[]{:S(2)}, u32[]{:S(2)}) collective-permute-start(bf16[656,256]{1,0:T(8,128)(2,1)} %merge.3), channel_id=1, source_target_pairs={{0,16},{8,24},{16,0},{24,8},{32,48},{40,56},{48,32},{56,40},{64,80... | collective-permute-start | bytes 1007624 | tf_op jit(solution)/shard_map/ppermute | solution.py:383
  123.6 13.4 %copy-start.3 = (bf16[640,640]{1,0:T(8,128)(2,1)S(1)}, bf16[640,640]{1,0:T(8,128)(2,1)}, u32[]{:S(2)}) copy-start(bf16[640,640]{1,0:T(8,128)(2,1)} %get-tuple-element.118) | copy-start | bytes 2457604
  123.6 6.3 %collective-permute-start.23 = (bf16[656,256]{1,0:T(8,128)(2,1)}, bf16[656,256]{1,0:T(8,128)(2,1)}, u32[]{:S(2)}, u32[]{:S(2)}) collective-permute-start(bf16[656,256]{1,0:T(8,128)(2,1)} %get-tuple-element.116), channel_id=1, source_target_pairs={{0,8},{8,0},{16,24},{24,16},{32,40},{40,32},{48,56},{56,48},{64,72... | collective-permute-start | bytes 1007624 | tf_op jit(solution)/shard_map/ppermute | solution.py:383
  130.0 8.5 %copy-start.2 = (bf16[640,640]{1,0:T(8,128)(2,1)S(1)}, bf16[640,640]{1,0:T(8,128)(2,1)}, u32[]{:S(2)}) copy-start(bf16[640,640]{1,0:T(8,128)(2,1)} %get-tuple-element.117) | copy-start | bytes 2457604
  132.1 6.4 %copy-start = (bf16[256,640]{1,0:T(8,128)(2,1)S(1)}, bf16[256,640]{1,0:T(8,128)(2,1)}, u32[]{:S(2)}) copy-start(bf16[256,640]{1,0:T(8,128)(2,1)} %merge.5) | copy-start | bytes 983044
  132.1 11.1 %collective-permute-start.26 = (bf16[256,640]{1,0:T(8,128)(2,1)}, bf16[256,640]{1,0:T(8,128)(2,1)S(1)}, u32[]{:S(2)}, u32[]{:S(2)}) collective-permute-start(bf16[256,640]{1,0:T(8,128)(2,1)} %merge.5), channel_id=1, source_target_pairs={{0,2},{1,3},{2,4},{3,5},{4,6},{5,7},{6,0},{7,1},{8,10},{9,11},{10,... | collective-permute-start | bytes 983048 | tf_op jit(solution)/shard_map/ppermute | solution.py:387
  133.4 15.5 %collective-permute-start.25 = (bf16[256,640]{1,0:T(8,128)(2,1)}, bf16[256,640]{1,0:T(8,128)(2,1)S(1)}, u32[]{:S(2)}, u32[]{:S(2)}) collective-permute-start(bf16[256,640]{1,0:T(8,128)(2,1)} %merge.5), channel_id=1, source_target_pairs={{0,6},{1,7},{2,0},{3,1},{4,2},{5,3},{6,4},{7,5},{8,14},{9,15},{10,... | collective-permute-start | bytes 983048 | tf_op jit(solution)/shard_map/ppermute | solution.py:387
  135.3 15.1 %collective-permute-start.24 = (bf16[256,640]{1,0:T(8,128)(2,1)}, bf16[256,640]{1,0:T(8,128)(2,1)S(1)}, u32[]{:S(2)}, u32[]{:S(2)}) collective-permute-start(bf16[256,640]{1,0:T(8,128)(2,1)} %merge.5), channel_id=1, source_target_pairs={{0,4},{1,5},{2,6},{3,7},{4,0},{5,1},{6,2},{7,3},{8,12},{9,13},{10,... | collective-permute-start | bytes 983048 | tf_op jit(solution)/shard_map/ppermute | solution.py:387
  150.9 8.1 %collective-permute-start.27 = (bf16[256,640]{1,0:T(8,128)(2,1)S(1)}, bf16[256,640]{1,0:T(8,128)(2,1)S(1)}, u32[]{:S(2)}, u32[]{:S(2)}) collective-permute-start(bf16[256,640]{1,0:T(8,128)(2,1)S(1)} %add_convert_fusion.1), channel_id=1, source_target_pairs={{0,1},{1,0},{2,3},{3,2},{4,5},{5,4},{6,7},{7,6},{8,9},{9,8},{10,11... | collective-permute-start | bytes 983048 | tf_op jit(solution)/shard_map/ppermute | solution.py:488
